TPU v7x, 32 devices: a whole 2x2x4 slice. The times are simulated.
32 devices in a mesh: blk: 4 (over x, core), tensor: 8 (over z, y).
Axes of the slice: x: 2, y: 2, z: 4, core: 2. Of those that a mesh axis runs over, the one named last changes fastest.
Arguments:
- hidden_in: bfloat16 [4, 1024, 2048], P(None, 'blk'), may hold values from -6 to 6
- out_grad: bfloat16 [4, 1024, 2048], P(None, 'blk'), may hold values from -6 to 6
- norm_in: bfloat16 [2048], P('blk'), may hold values from 0.5 to 1.5
- w_query: bfloat16 [2048, 2048], P('blk', 'tensor'), may hold values from -0.125 to 0.125
- key_weight: bfloat16 [2048, 1024], P('blk', 'tensor'), may hold values from -0.125 to 0.125
- value_weight: bfloat16 [2048, 1024], P('blk', 'tensor'), may hold values from -0.125 to 0.125
- w_out: bfloat16 [2048, 2048], P('tensor', 'blk'), may hold values from -1 to 1
- query_gain: bfloat16 [128], P('blk'), may hold values from 0.5 to 1.5
- key_gain: bfloat16 [128], P('blk'), may hold values from 0.5 to 1.5
- norm_mid: bfloat16 [2048], P('blk'), may hold values from 0.5 to 1.5
- w_gate: bfloat16 [2048, 6144], P('blk', 'tensor'), may hold values from -0.125 to 0.125
- w_up: bfloat16 [2048, 6144], P('blk', 'tensor'), may hold values from -0.125 to 0.125
- w_down: bfloat16 [6144, 2048], P('tensor', 'blk'), may hold values from -0.078125 to 0.078125
Outputs:
- layer_out: bfloat16 [4, 1024, 2048], P(None, 'blk')
- grad_hidden: bfloat16 [4, 1024, 2048], P(None, 'blk')
- grad_norm_in: float32 [2048], P('blk')
- grad_w_query: float32 [2048, 2048], P('blk', 'tensor')
- grad_w_key: float32 [2048, 1024], P('blk', 'tensor')
- grad_w_value: float32 [2048, 1024], P('blk', 'tensor')
- grad_w_out: float32 [2048, 2048], P('tensor', 'blk')
- grad_query_gain: float32 [128], P('blk')
- grad_key_gain: float32 [128], P('blk')
- grad_norm_mid: float32 [2048], P('blk')
- grad_w_gate: float32 [2048, 6144], P('blk', 'tensor')
- grad_w_up: float32 [2048, 6144], P('blk', 'tensor')
- grad_w_down: float32 [6144, 2048], P('tensor', 'blk')
All inputs are finite; a program needn't handle non-finite values.
Results may differ from a plain program's by a relative error of at most 0.025.
Values may be sent and summed in bfloat16 or wider, within the bound.
No kernel may reach another device: no remote copies, remote signals or barrier semaphores. Data moves between devices by JAX's collectives and lax.ppermute only.
A program may use at most 192 MiB of HBM per device.

v0:
```python
import jax
import jax.numpy as jnp
from jax import lax
from jax.sharding import PartitionSpec as P

EPSILON = 1e-06
ROTARY_BASE = 1000000.0


def as_sent(array):
    return jax.tree.map(lambda a: a.astype(jnp.bfloat16) if a.dtype == jnp.float32 else a, array)


def normed(values, row_gain_vector):
    return (
        values
        * lax.rsqrt(jnp.mean(values * values, axis=-1, keepdims=True) + EPSILON)
        * row_gain_vector
    )


def rotate(values, cosine, sine_table):
    half_dim = values.shape[-1] // 2
    first_half = values[..., :half_dim]
    second_half = values[..., half_dim:]
    return jnp.concatenate(
        [
            first_half * cosine - second_half * sine_table,
            second_half * cosine + first_half * sine_table,
        ],
        axis=-1,
    )


def rotation_tables(positions, head_dim):
    half_dim = head_dim // 2
    inverse = jnp.power(
        jnp.float32(ROTARY_BASE), -(jnp.arange(half_dim, dtype=jnp.float32) * 2.0 / head_dim)
    )
    angles = positions.astype(jnp.float32)[:, None] * inverse[None, :]
    return (jnp.cos(angles)[:, None, :], jnp.sin(angles)[:, None, :])


def project(left_side, right_side):
    return jnp.einsum("btd,dc->btc", left_side, right_side, preferred_element_type=jnp.float32)


def project_back(grad_side, right_side):
    return jnp.einsum("btc,dc->btd", grad_side, right_side, preferred_element_type=jnp.float32)


def outer_sum(left_side, grad_side):
    return jnp.einsum("btd,btc->dc", left_side, grad_side, preferred_element_type=jnp.float32)


def swish_product(gate_part, up_part):
    return jax.nn.silu(gate_part) * up_part


def unchanged(current):
    return current


def total_heads(partial_sum):
    return lax.psum(partial_sum.astype(jnp.bfloat16), "tensor").astype(jnp.float32)


def local(
    hidden_in,
    out_grad,
    norm_in,
    w_query,
    key_weight,
    value_weight,
    w_out,
    query_gain,
    key_gain,
    norm_mid,
    w_gate,
    w_up,
    w_down,
):
    block_count = lax.axis_size("blk")
    tok_rows = hidden_in.shape[1]
    head_dim = query_gain.shape[0] * block_count
    query_heads = w_query.shape[1] // head_dim
    pair_heads = key_weight.shape[1] // head_dim
    group_size = query_heads // pair_heads
    score_scale = head_dim ** (-0.5)
    seq_rows = tok_rows * block_count
    first_row = lax.axis_index("blk") * tok_rows
    positions = first_row + jnp.arange(tok_rows, dtype=jnp.int32)
    last_row = first_row + tok_rows - 1
    cosine, sine_table = rotation_tables(positions, head_dim)

    def prepare(raw_rows, row_gain_vector):
        return rotate(normed(raw_rows, row_gain_vector), cosine, sine_table)

    outputs_list = []
    grads_list = []
    row_total = None
    col_total = None
    for group_index in range(hidden_in.shape[0] // 2):
        row_parts = (
            lax.all_gather(norm_in, "blk", axis=0, tiled=True),
            lax.all_gather(w_query, "blk", axis=0, tiled=True),
            lax.all_gather(key_weight, "blk", axis=0, tiled=True),
            lax.all_gather(value_weight, "blk", axis=0, tiled=True),
            lax.all_gather(query_gain, "blk", axis=0, tiled=True),
            lax.all_gather(key_gain, "blk", axis=0, tiled=True),
            lax.all_gather(norm_mid, "blk", axis=0, tiled=True),
            lax.all_gather(w_gate, "blk", axis=0, tiled=True),
            lax.all_gather(w_up, "blk", axis=0, tiled=True),
        )
        col_parts = (
            lax.all_gather(w_out, "blk", axis=1, tiled=True),
            lax.all_gather(w_down, "blk", axis=1, tiled=True),
        )
        (
            gain_in,
            query_full,
            key_full,
            value_full,
            gain_query,
            gain_key,
            gain_mid,
            gate_full,
            up_full,
            out_full,
            down_full,
        ) = tuple(row_parts) + tuple(col_parts)
        gain_first = gain_in.astype(jnp.float32)
        gain_second = gain_mid.astype(jnp.float32)
        query_scale = gain_query.astype(jnp.float32)
        key_scale = gain_key.astype(jnp.float32)
        x_rows = hidden_in[2 * group_index : 2 * group_index + 2].astype(jnp.float32)
        normal_in = normed(x_rows, gain_first).astype(jnp.bfloat16)
        query_raw = project(normal_in, query_full).reshape(2, tok_rows, query_heads, head_dim)
        key_raw = project(normal_in, key_full).reshape(2, tok_rows, pair_heads, head_dim)
        value_rows = (
            project(normal_in, value_full)
            .astype(jnp.bfloat16)
            .reshape(2, tok_rows, pair_heads, head_dim)
        )
        query_rows = prepare(query_raw, query_scale).astype(jnp.bfloat16)
        key_rows = prepare(key_raw, key_scale).astype(jnp.bfloat16)
        query_group = query_rows.reshape(2, tok_rows, pair_heads, group_size, head_dim).transpose(
            0, 2, 3, 1, 4
        )
        stats_shape = (2, pair_heads, group_size, tok_rows)
        start_state = (
            jnp.full(stats_shape, -1e30, jnp.float32),
            jnp.zeros(stats_shape, jnp.float32),
            jnp.zeros(stats_shape + (head_dim,), jnp.float32),
        )
        key_piece = lax.all_gather(key_rows, "blk", axis=1, tiled=True)
        value_piece = lax.all_gather(value_rows, "blk", axis=1, tiled=True)
        piece_rows = key_piece.shape[1]

        def include(current):
            running_max, running_sum, weighted = current
            scores = (
                jnp.einsum(
                    "bhgqd,bkhd->bhgqk", query_group, key_piece, preferred_element_type=jnp.float32
                )
                * score_scale
            )
            key_pos = jnp.arange(piece_rows, dtype=jnp.int32)
            scores = jnp.where(key_pos[None, :] <= positions[:, None], scores, -jnp.inf)
            new_max = jnp.maximum(running_max, jnp.max(scores, axis=-1))
            weights_now = jnp.exp(scores - new_max[..., None])
            new_sum = jnp.sum(weights_now, axis=-1)
            new_weighted = jnp.einsum(
                "bhgqk,bkhd->bhgqd",
                weights_now.astype(jnp.bfloat16),
                value_piece,
                preferred_element_type=jnp.float32,
            )
            return (new_max, new_sum, new_weighted)

        running_max, running_sum, weighted = lax.cond(
            jnp.int32(0) > last_row, unchanged, include, start_state
        )
        attn_group = weighted / running_sum[..., None]
        log_total = running_max + jnp.log(running_sum)
        attended = (
            attn_group.transpose(0, 3, 1, 2, 4)
            .reshape(2, tok_rows, query_heads * head_dim)
            .astype(jnp.bfloat16)
        )
        attn_part = project(attended, out_full)
        residual = x_rows + total_heads(attn_part)
        normal_mid = normed(residual, gain_second).astype(jnp.bfloat16)
        gate_rows = project(normal_mid, gate_full)
        up_rows = project(normal_mid, up_full)
        active = swish_product(gate_rows, up_rows).astype(jnp.bfloat16)
        mlp_part = project(active, down_full)
        out_part = (residual + total_heads(mlp_part)).astype(jnp.bfloat16)
        grad_out = out_grad[2 * group_index : 2 * group_index + 2].astype(jnp.float32)
        grad_mlp = grad_out.astype(jnp.bfloat16)
        grad_active = project_back(grad_mlp, down_full)
        term_down = outer_sum(active, grad_mlp)
        _, pull_act = jax.vjp(swish_product, gate_rows, up_rows)
        grad_gate, grad_up = pull_act(grad_active)
        grad_gate = grad_gate.astype(jnp.bfloat16)
        grad_up = grad_up.astype(jnp.bfloat16)
        term_gate = outer_sum(normal_mid, grad_gate)
        term_up = outer_sum(normal_mid, grad_up)
        grad_mid_part = project_back(grad_gate, gate_full) + project_back(grad_up, up_full)
        grad_normal_mid = total_heads(grad_mid_part)
        _, pull_mid = jax.vjp(normed, residual, gain_second)
        grad_resid_norm, term_gain_mid = pull_mid(grad_normal_mid)
        grad_residual = grad_out + grad_resid_norm
        grad_branch = grad_residual.astype(jnp.bfloat16)
        term_out = outer_sum(attended, grad_branch)
        grad_attended = project_back(grad_branch, out_full).astype(jnp.bfloat16)
        grad_group = grad_attended.reshape(2, tok_rows, pair_heads, group_size, head_dim).transpose(
            0, 2, 3, 1, 4
        )
        row_dots = jnp.sum(grad_group.astype(jnp.float32) * attn_group, axis=-1)
        back_start = (
            jnp.zeros(stats_shape + (head_dim,), jnp.float32),
            jnp.zeros((2, seq_rows, pair_heads, head_dim), jnp.float32),
            jnp.zeros((2, seq_rows, pair_heads, head_dim), jnp.float32),
        )
        attend_key_piece = lax.all_gather(key_rows, "blk", axis=1, tiled=True)
        attend_value_piece = lax.all_gather(value_rows, "blk", axis=1, tiled=True)
        attend_piece_rows = attend_key_piece.shape[1]

        def attend_include(current):
            scores = (
                jnp.einsum(
                    "bhgqd,bkhd->bhgqk",
                    query_group,
                    attend_key_piece,
                    preferred_element_type=jnp.float32,
                )
                * score_scale
            )
            key_pos = jnp.arange(attend_piece_rows, dtype=jnp.int32)
            scores = jnp.where(key_pos[None, :] <= positions[:, None], scores, -jnp.inf)
            weights_now = jnp.exp(scores - log_total[..., None])
            value_cost_term = jnp.einsum(
                "bhgqk,bhgqd->bkhd",
                weights_now.astype(jnp.bfloat16),
                grad_group,
                preferred_element_type=jnp.float32,
            )
            grad_weights = jnp.einsum(
                "bhgqd,bkhd->bhgqk",
                grad_group,
                attend_value_piece,
                preferred_element_type=jnp.float32,
            )
            grad_scores = (weights_now * (grad_weights - row_dots[..., None]) * score_scale).astype(
                jnp.bfloat16
            )
            grad_query_acc = jnp.einsum(
                "bhgqk,bkhd->bhgqd",
                grad_scores,
                attend_key_piece,
                preferred_element_type=jnp.float32,
            )
            key_term = jnp.einsum(
                "bhgqk,bhgqd->bkhd", grad_scores, query_group, preferred_element_type=jnp.float32
            )
            return (grad_query_acc, key_term, value_cost_term)

        grad_query_acc, key_sum, value_sum = lax.cond(
            jnp.int32(0) > last_row, unchanged, attend_include, back_start
        )
        key_share, value_share = (
            lax.psum_scatter(
                key_sum.astype(jnp.bfloat16), "blk", scatter_dimension=1, tiled=True
            ).astype(jnp.float32),
            lax.psum_scatter(
                value_sum.astype(jnp.bfloat16), "blk", scatter_dimension=1, tiled=True
            ).astype(jnp.float32),
        )
        grad_query = grad_query_acc.transpose(0, 3, 1, 2, 4).reshape(
            2, tok_rows, query_heads, head_dim
        )
        _, pull_query = jax.vjp(prepare, query_raw, query_scale)
        grad_query_raw, term_query_gain = pull_query(grad_query)
        _, pull_key = jax.vjp(prepare, key_raw, key_scale)
        grad_key_raw, term_key_gain = pull_key(key_share)
        grad_query_low = grad_query_raw.reshape(2, tok_rows, query_heads * head_dim).astype(
            jnp.bfloat16
        )
        grad_key_low = grad_key_raw.reshape(2, tok_rows, pair_heads * head_dim).astype(jnp.bfloat16)
        grad_value_low = value_share.reshape(2, tok_rows, pair_heads * head_dim).astype(
            jnp.bfloat16
        )
        term_query = outer_sum(normal_in, grad_query_low)
        term_key = outer_sum(normal_in, grad_key_low)
        term_value = outer_sum(normal_in, grad_value_low)
        grad_in_part = (
            project_back(grad_query_low, query_full)
            + project_back(grad_key_low, key_full)
            + project_back(grad_value_low, value_full)
        )
        grad_normal_in, term_query_gain, term_key_gain = (
            lax.psum(grad_in_part.astype(jnp.bfloat16), "tensor").astype(jnp.float32),
            lax.psum(term_query_gain.astype(jnp.bfloat16), "tensor").astype(jnp.float32),
            lax.psum(term_key_gain.astype(jnp.bfloat16), "tensor").astype(jnp.float32),
        )
        _, pull_first = jax.vjp(normed, x_rows, gain_first)
        grad_x_norm, term_gain_in = pull_first(grad_normal_in)
        hidden_part = (grad_residual + grad_x_norm).astype(jnp.bfloat16)
        outputs_list.append(out_part)
        grads_list.append(hidden_part)
        row_terms = (
            term_gain_in,
            term_query,
            term_key,
            term_value,
            term_query_gain,
            term_key_gain,
            term_gain_mid,
            term_gate,
            term_up,
        )
        col_terms = (term_out, term_down)
        row_part, col_part = (row_terms, col_terms)
        if row_total is None:
            row_total, col_total = (row_part, col_part)
        else:
            row_total = tuple((earlier + further for earlier, further in zip(row_total, row_part)))
            col_total = tuple((earlier + further for earlier, further in zip(col_total, col_part)))
    row_shares = jax.tree.map(
        lambda part: part.astype(jnp.float32),
        lax.psum_scatter(as_sent(row_total), "blk", scatter_dimension=0, tiled=True),
    )
    col_shares = jax.tree.map(
        lambda part: part.astype(jnp.float32),
        lax.psum_scatter(as_sent(col_total), "blk", scatter_dimension=1, tiled=True),
    )
    row_total = tuple(row_shares)
    col_total = tuple(col_shares)
    layer_out = jnp.concatenate(outputs_list, axis=0)
    grad_hidden = jnp.concatenate(grads_list, axis=0)
    return (
        layer_out,
        grad_hidden,
        row_total[0],
        row_total[1],
        row_total[2],
        row_total[3],
        col_total[0],
        row_total[4],
        row_total[5],
        row_total[6],
        row_total[7],
        row_total[8],
        col_total[1],
    )


def solution(mesh):
    return jax.shard_map(
        local,
        mesh=mesh,
        in_specs=(
            P(None, "blk", None),
            P(None, "blk", None),
            P("blk"),
            P("blk", "tensor"),
            P("blk", "tensor"),
            P("blk", "tensor"),
            P("tensor", "blk"),
            P("blk"),
            P("blk"),
            P("blk"),
            P("blk", "tensor"),
            P("blk", "tensor"),
            P("tensor", "blk"),
        ),
        out_specs=(
            P(None, "blk", None),
            P(None, "blk", None),
            P("blk"),
            P("blk", "tensor"),
            P("blk", "tensor"),
            P("blk", "tensor"),
            P("tensor", "blk"),
            P("blk"),
            P("blk"),
            P("blk"),
            P("blk", "tensor"),
            P("blk", "tensor"),
            P("tensor", "blk"),
        ),
        check_vma=False,
    )
```

profile of v0, /device:TPU:0, one launch (start us, length us, event | category | flops | bytes accessed | tf_op | source)
XLA Modules:
  0.0 1187.4 jit_solution(10618413393819610972)
XLA Ops:
  14.9 8.3 all-reduce.19
  32.9 7.4 all_gather.63
  44.6 7.3 all_gather.66
  52.7 7.8 all-gather
  61.3 10.9 all-gather.1
  72.2 10.5 all_gather.73
  82.7 7.7 all_gather.65
  116.5 17.5 %all-gather.3 = bf16[4,1,512]{2,1,0:T(2,128)(2,1)S(1)} all-gather(bf16[1,1,512]{2,1,0:T(2,128)(2,1)S(1)} %reshape.619), channel_id=1, replica_groups=mesh['blk'=4,'tensor'=8] {'blk'}, dimensions={0}, use_global_device_ids=true | all-gather | bytes 5120 | tf_op jit(solution)/shard_map/all_gather | solution.py:111
  142.7 129.7 %all-reduce.28.cloned.1.call-done = (bf16[2,256,2048]{2,1,0:T(8,128)(2,1)}, bf16[2,256,2048]{2,1,0:T(8,128)(2,1)}) async-done(((bf16[2,256,2048]{2,1,0:T(8,128)(2,1)}, bf16[2,256,2048]{2,1,0:T(8,128)(2,1)}), (bf16[2,256,2048]{2,1,0:T(8,128)(2,1)}, bf16[2,256,2048]{2,1,0:T(8,128)(2,1)})) %all-reduce.28.cloned.1.call-update) | async-done | bytes 4194320 | tf_op jit(solution)/shard_map/psum | solution.py:65
  282.1 19.2 %all-gather.16.cloned.1.call-done = bf16[2048,768]{1,0:T(8,128)(2,1)} async-done(((bf16[512,768]{1,0:T(8,128)(2,1)}), bf16[2048,768]{1,0:T(8,128)(2,1)}) %all-gather.16.cloned.1.call-update) | async-done | bytes 3145744 | tf_op jit(solution)/shard_map/all_gather | solution.py:113
  309.9 21.4 %all-gather.14.cloned.1.call-done = bf16[2048,768]{1,0:T(8,128)(2,1)} async-done(((bf16[512,768]{1,0:T(8,128)(2,1)}), bf16[2048,768]{1,0:T(8,128)(2,1)}) %all-gather.14.cloned.1.call-update) | async-done | bytes 3145744 | tf_op jit(solution)/shard_map/all_gather | solution.py:112
  353.7 156.8 %all-reduce.26.cloned.1.call-done = (bf16[2,256,2048]{2,1,0:T(8,128)(2,1)}, bf16[2,256,2048]{2,1,0:T(8,128)(2,1)}) async-done(((bf16[2,256,2048]{2,1,0:T(8,128)(2,1)}, bf16[2,256,2048]{2,1,0:T(8,128)(2,1)}), (bf16[2,256,2048]{2,1,0:T(8,128)(2,1)}, bf16[2,256,2048]{2,1,0:T(8,128)(2,1)})) %all-reduce.26.cloned.1.call-update) | async-done | bytes 4194320 | tf_op jit(solution)/shard_map/psum | solution.py:65
  510.5 7.5 fusion.87
  531.8 14.2 %conditional.6 = (f32[2,1,2,256,128]{4,3,2,0,1:T(8,128)}, bf16[2,1024,1,128]{3,1,0,2:T(8,128)(2,1)}, bf16[2,1024,1,128]{3,1,0,2:T(8,128)(2,1)}) conditional(s32[]{:T(128)} %convert_element_type.376, (s32[256]{0:T(256)}, bf16[2,1,2,256,128]{3,4,2,0,1:T(8,128)(2,1)}, bf16[2,1024,1,128]{1,3,0,2:T(8,128)(2,1)}, f32[2,1,2,256]{3,2,0,1:T(2,128)}, ...), branch_computations={%region_22.24_spmd, %region_24.25_spmd} | conditional | flops 1354235904 | bytes 32273544 | solution.py:269
  555.2 14.2 %conditional.7 = (f32[2,1,2,256,128]{4,3,2,0,1:T(8,128)}, bf16[2,1024,1,128]{3,1,0,2:T(8,128)(2,1)}, bf16[2,1024,1,128]{3,1,0,2:T(8,128)(2,1)}) conditional(s32[]{:T(128)} %convert_element_type.376, (s32[256]{0:T(256)}, bf16[2,1,2,256,128]{3,4,2,0,1:T(8,128)(2,1)S(1)}, bf16[2,1024,1,128]{1,3,0,2:T(8,128)(2,1)}, f32[2,1,2,256]{3,2,0,1:T(2,128)}, ...), branch_computations={%region_33.35_spmd, %region_35.36_spmd} | conditional | flops 1354235904 | bytes 31224940 | solution.py:269
  574.5 19.3 %reduce-scatter.16.cloned.1.call-done = bf16[2,256,1,128]{1,3,0,2:T(8,128)(2,1)} async-done(((bf16[2,1024,1,128]{1,3,0,2:T(8,128)(2,1)}), bf16[2,256,1,128]{1,3,0,2:T(8,128)(2,1)}) %reduce-scatter.16.cloned.1.call-update) | async-done | bytes 131088 | tf_op jit(solution)/shard_map/reduce_scatter | solution.py:273
  605.5 12.9 %reduce-scatter.18.cloned.1.call-done = bf16[2,256,1,128]{3,1,0,2:T(8,128)(2,1)} async-done(((bf16[2,1024,1,128]{3,1,0,2:T(8,128)(2,1)}), bf16[2,256,1,128]{3,1,0,2:T(8,128)(2,1)}) %reduce-scatter.18.cloned.1.call-update) | async-done | bytes 131088 | tf_op jit(solution)/shard_map/reduce_scatter | solution.py:276
  621.9 20.8 %reduce-scatter.14.cloned.1.call-done = bf16[2,256,1,128]{3,1,0,2:T(8,128)(2,1)} async-done(((bf16[2,1024,1,128]{3,1,0,2:T(8,128)(2,1)}), bf16[2,256,1,128]{3,1,0,2:T(8,128)(2,1)}) %reduce-scatter.14.cloned.1.call-update) | async-done | bytes 131088 | tf_op jit(solution)/shard_map/reduce_scatter | solution.py:276
  701.9 21.6 %all-reduce.14 = (bf16[128]{0:T(256)(128)(2,1)S(1)}, bf16[128]{0:T(256)(128)(2,1)S(1)}, bf16[128]{0:T(256)(128)(2,1)S(1)}, bf16[128]{0:T(256)(128)(2,1)S(1)}) all-reduce(bf16[128]{0:T(256)(128)(2,1)S(1)} %get-tuple-element.310, bf16[128]{0:T(256)(128)(2,1)S(1)} %get-tuple-element.227, ...), channel_id=1, replica_groups=mesh['blk'=4,'tensor'=8] {'tensor'}, use_global_device_ids=true, to_apply=%region_52.53 | all-reduce | flops 512 | bytes 2048 | tf_op jit(solution)/shard_map/psum | solution.py:304
  728.6 18.4 %reduce-scatter.20.cloned.1.call-done = bf16[512,256]{1,0:T(8,128)(2,1)} async-done(((bf16[2048,256]{1,0:T(8,128)(2,1)}), bf16[512,256]{1,0:T(8,128)(2,1)}) %reduce-scatter.20.cloned.1.call-update) | async-done | bytes 262160 | tf_op jit(solution)/shard_map/reduce_scatter | solution.py:332
  748.8 39.2 %reduce-scatter.28.cloned.1.call-done = bf16[512,768]{1,0:T(8,128)(2,1)} async-done(((bf16[2048,768]{1,0:T(8,128)(2,1)}), bf16[512,768]{1,0:T(8,128)(2,1)}) %reduce-scatter.28.cloned.1.call-update) | async-done | bytes 786448 | tf_op jit(solution)/shard_map/reduce_scatter | solution.py:332
  790.3 38.7 %reduce-scatter.30.cloned.1.call-done = bf16[512,768]{1,0:T(8,128)(2,1)} async-done(((bf16[2048,768]{1,0:T(8,128)(2,1)}), bf16[512,768]{1,0:T(8,128)(2,1)}) %reduce-scatter.30.cloned.1.call-update) | async-done | bytes 786448 | tf_op jit(solution)/shard_map/reduce_scatter | solution.py:332
  831.4 38.0 %reduce-scatter.32.cloned.1.call-done = bf16[768,512]{1,0:T(8,128)(2,1)} async-done(((bf16[768,2048]{1,0:T(8,128)(2,1)}), bf16[768,512]{1,0:T(8,128)(2,1)}) %reduce-scatter.32.cloned.1.call-update) | async-done | bytes 786448 | tf_op jit(solution)/shard_map/reduce_scatter | solution.py:336
  871.9 275.3 %all-reduce.24.cloned.1.call-done = (bf16[2,256,2048]{2,1,0:T(8,128)(2,1)}, bf16[2,256,2048]{2,1,0:T(8,128)(2,1)}, bf16[2,256,2048]{2,1,0:T(8,128)(2,1)}, bf16[2,256,2048]{2,1,0:T(8,128)(2,1)}) async-done(((bf16[2,256,2048]{2,1,0:T(8,128)(2,1)}, bf16[2,256,2048]{2,1,0:T(8,128)(2,1)}, bf16[2,256,2048]{2,1,0:T(8,128)(2,1)}, bf16[2,256,2048]{2,1,0:T(8,128)(2,1)}), (bf16[2,256,2048]{2,1,0:T(8,128)(2,1)}, ...) | async-done | bytes 8388624 | tf_op jit(solution)/shard_map/psum | solution.py:65
  (451 shorter events, 281.5 us)
Async XLA Ops:
  7.2 83.1 %all-gather.10.cloned.1.call-start = ((), (), s32[]{:S(2)}) async-start(), calls=%async_computation.11 | async-start | bytes 1310720 | tf_op jit(solution)/shard_map/all_gather | solution.py:106
  9.1 99.5 %all-gather.12.cloned.1.call-start = ((), (), s32[]{:S(2)}) async-start(), calls=%async_computation.12 | async-start | bytes 1310720 | tf_op jit(solution)/shard_map/all_gather | solution.py:116
  9.8 124.2 %all-gather.18.cloned.1.call-start = ((), (), s32[]{:S(2)}) async-start(), calls=%async_computation.15 | async-start | bytes 3932160 | tf_op jit(solution)/shard_map/all_gather | solution.py:117
  10.6 261.8 %all-reduce.28.cloned.1.call-start = ((), (), s32[]{:S(2)}) async-start(), calls=%async_computation.29 | async-start | bytes 8388608 | tf_op jit(solution)/shard_map/psum | solution.py:65
  23.2 71.8 %copy-start.114 = (f32[128]{0:T(128)}, f32[128]{0:T(128)S(1)}, u32[]{:S(2)}) copy-start(f32[128]{0:T(128)S(1)} %convert_element_type.379) | copy-start | bytes 1540
  27.1 66.2 %copy-start.97 = (f32[2,256]{1,0:T(2,128)}, f32[2,256]{1,0:T(2,128)S(1)}, u32[]{:S(2)}) copy-start(f32[2,256]{1,0:T(2,128)S(1)} %fusion.200) | copy-start | bytes 6148
  27.6 62.7 %copy-start.93 = (f32[2,256]{1,0:T(2,128)}, f32[2,256]{1,0:T(2,128)S(1)}, u32[]{:S(2)}) copy-start(f32[2,256]{1,0:T(2,128)S(1)} %fusion.203) | copy-start | bytes 6148
  115.3 186.0 %all-gather.16.cloned.1.call-start = ((), (), s32[]{:S(2)}) async-start(), calls=%async_computation.14 | async-start | bytes 3932160 | tf_op jit(solution)/shard_map/all_gather | solution.py:113
  115.9 215.4 %all-gather.14.cloned.1.call-start = ((), (), s32[]{:S(2)}) async-start(), calls=%async_computation.13 | async-start | bytes 3932160 | tf_op jit(solution)/shard_map/all_gather | solution.py:112
  116.5 394.0 %all-reduce.26.cloned.1.call-start = ((), (), s32[]{:S(2)}) async-start(), calls=%async_computation.28 | async-start | bytes 8388608 | tf_op jit(solution)/shard_map/psum | solution.py:65
  353.7 219.2 %reduce-scatter.12.cloned.1.call-start = ((), (), s32[]{:S(2)}) async-start(), calls=%async_computation.16 | async-start | bytes 655360 | tf_op jit(solution)/shard_map/reduce_scatter | solution.py:273
  548.1 45.7 %reduce-scatter.16.cloned.1.call-start = ((), (), s32[]{:S(2)}) async-start(), calls=%async_computation.18 | async-start | bytes 655360 | tf_op jit(solution)/shard_map/reduce_scatter | solution.py:273
  569.4 26.5 %copy-start.37 = (f32[2,256,128]{1,2,0:T(8,128)S(1)}, f32[2,256,128]{1,2,0:T(8,128)}, u32[]{:S(2)}) copy-start(f32[2,256,128]{1,2,0:T(8,128)} %copy-done.36) | copy-start | bytes 786436
  571.5 46.9 %reduce-scatter.18.cloned.1.call-start = ((), (), s32[]{:S(2)}) async-start(), calls=%async_computation.19 | async-start | bytes 655360 | tf_op jit(solution)/shard_map/reduce_scatter | solution.py:276
  572.1 70.6 %reduce-scatter.14.cloned.1.call-start = ((), (), s32[]{:S(2)}) async-start(), calls=%async_computation.17 | async-start | bytes 655360 | tf_op jit(solution)/shard_map/reduce_scatter | solution.py:276
  572.8 150.7 %reduce-scatter.22.cloned.1.call-start = ((), (), s32[]{:S(2)}) async-start(), calls=%async_computation.21 | async-start | bytes 655360 | tf_op jit(solution)/shard_map/reduce_scatter | solution.py:332
  605.4 119.7 %reduce-scatter.24.cloned.1.call-start = ((), (), s32[]{:S(2)}) async-start(), calls=%async_computation.22 | async-start | bytes 655360 | tf_op jit(solution)/shard_map/reduce_scatter | solution.py:332
  646.5 80.3 %reduce-scatter.26.cloned.1.call-start = ((), (), s32[]{:S(2)}) async-start(), calls=%async_computation.23 | async-start | bytes 1310720 | tf_op jit(solution)/shard_map/reduce_scatter | solution.py:336
  650.8 96.2 %reduce-scatter.20.cloned.1.call-start = ((), (), s32[]{:S(2)}) async-start(), calls=%async_computation.20 | async-start | bytes 1310720 | tf_op jit(solution)/shard_map/reduce_scatter | solution.py:332
  661.5 126.4 %reduce-scatter.28.cloned.1.call-start = ((), (), s32[]{:S(2)}) async-start(), calls=%async_computation.24 | async-start | bytes 3932160 | tf_op jit(solution)/shard_map/reduce_scatter | solution.py:332
  669.2 159.9 %reduce-scatter.30.cloned.1.call-start = ((), (), s32[]{:S(2)}) async-start(), calls=%async_computation.25 | async-start | bytes 3932160 | tf_op jit(solution)/shard_map/reduce_scatter | solution.py:332
  676.8 192.6 %reduce-scatter.32.cloned.1.call-start = ((), (), s32[]{:S(2)}) async-start(), calls=%async_computation.26 | async-start | bytes 3932160 | tf_op jit(solution)/shard_map/reduce_scatter | solution.py:336
  684.9 462.4 %all-reduce.24.cloned.1.call-start = ((), (), s32[]{:S(2)}) async-start(), calls=%async_computation.27 | async-start | bytes 16777216 | tf_op jit(solution)/shard_map/psum | solution.py:65
  726.8 420.4 %copy-start.96 = (f32[2,256]{1,0:T(2,128)S(1)}, f32[2,256]{1,0:T(2,128)}, u32[]{:S(2)}) copy-start(f32[2,256]{1,0:T(2,128)} %copy-done.93) | copy-start | bytes 6148
  (121 other events, 662.8 us)
Sparse Core Ops, SparseCore 0:
  10.2 19.4 all-gather.9
  31.2 16.7 all-gather.11
  49.5 34.1 all-gather.17
  115.4 156.9 all-reduce.27
  273.8 27.5 all-gather.15
  302.7 28.5 all-gather.13
  353.8 156.6 all-reduce.25
  548.2 20.6 reduce-scatter.11
  572.1 21.6 reduce-scatter.15
  596.7 21.6 reduce-scatter.17
  621.1 21.6 reduce-scatter.13
  645.1 21.6 reduce-scatter.21
  669.4 21.6 reduce-scatter.23
  694.0 24.8 reduce-scatter.25
  722.0 24.8 reduce-scatter.19
  749.9 37.9 reduce-scatter.27
  791.0 37.9 reduce-scatter.29
  831.4 37.9 reduce-scatter.31
  874.6 272.5 all-reduce.23
where the time goes:
time: 1190 us
  waiting for transfers between devices  793 us (67%)
  matrix products  138 us (12%)
  blocking collectives  111 us (9%)
  other arithmetic  92.8 us (8%)
  local copies, waits for them, and re-layouts  32.7 us (3%)
  between operations  17.7 us (1%)
    psum x3, waiting for transfers between devices, total_heads(): lax.psum(partial_sum.astype(jnp.bfloat16), 'tensor').astype(jnp.float32)  562 us
    reduce_scatter x5, waiting for transfers between devices, local(): lax.psum_scatter(as_sent(row_total), 'blk', scatter_dimension=0, tiled=True)  96.2 us
    dot_general x14, matrix products, project(): jnp.einsum('btd,dc->btc', left_side, right_side, preferred_element_type=j...  42.8 us
    dot_general x14, matrix products, outer_sum(): jnp.einsum('btd,btc->dc', left_side, grad_side, preferred_element_type=jn...  41.8 us
    reduce_scatter x2, waiting for transfers between devices, local(): lax.psum_scatter(as_sent(col_total), 'blk', scatter_dimension=1, tiled=True)  38 us
    reduce_scatter x2, waiting for transfers between devices, local(): lax.psum_scatter(value_sum.astype(jnp.bfloat16), 'blk', scatter_dimension...  33.7 us
    dot_general x14, matrix products, project_back(): jnp.einsum('btc,dc->btd', grad_side, right_side, preferred_element_type=j...  30.5 us
  transfers between devices with their start and end apart: 19, of which 12 were waited for; matrix products, arithmetic and copies ran while one was open for 14% of the time, Pallas kernels for 0%

commit v1 on v0

v1 whole, which is shorter than its diff:
```python
import jax
import jax.numpy as jnp
from jax import lax
from jax.sharding import Mesh
from jax.sharding import PartitionSpec as P

EPSILON = 1e-06
ROTARY_BASE = 1000000.0
BF16 = jnp.bfloat16
F32 = jnp.float32
BLOCKS = ("bo", "bi")
TENSORS = ("to", "ti")


def normed(values, gain):
    return values * lax.rsqrt(jnp.mean(values * values, axis=-1, keepdims=True) + EPSILON) * gain


def rotate(values, cosine, sine):
    half = values.shape[-1] // 2
    first = values[..., :half]
    second = values[..., half:]
    return jnp.concatenate(
        [first * cosine - second * sine, second * cosine + first * sine], axis=-1
    )


def rotation_tables(positions, head_dim):
    half = head_dim // 2
    inverse = jnp.power(F32(ROTARY_BASE), -(jnp.arange(half, dtype=F32) * 2.0 / head_dim))
    angles = positions.astype(F32)[:, None] * inverse[None, :]
    return (jnp.cos(angles)[:, None, :], jnp.sin(angles)[:, None, :])


def dot(left, right):
    return jnp.dot(left, right, preferred_element_type=F32)


def dot_back(left, right):
    return jnp.einsum("tc,dc->td", left, right, preferred_element_type=F32)


def after(array, *earlier):
    return lax.optimization_barrier((array,) + earlier)[0]


def shifted(array, axis, step):
    count = lax.axis_size(axis)
    return lax.ppermute(array, axis, [(i, (i + step) % count) for i in range(count)])


def swapped(array, axis, distance=1):
    count = lax.axis_size(axis)
    return lax.ppermute(array, axis, [(i, i ^ distance) for i in range(count)])


def pick(array, index, dimension=0):
    return lax.dynamic_index_in_dim(array, index, dimension, keepdims=False)


def paired(own, other, first, dimension):
    return jnp.where(
        first, jnp.stack([own, other], dimension), jnp.stack([other, own], dimension)
    )


def gather_axis(array, axis, dimension=0):
    count = lax.axis_size(axis)
    index = lax.axis_index(axis)
    if count == 2:
        return paired(array, swapped(array, axis), index == 0, dimension)
    shape = array.shape[:dimension] + (count,) + array.shape[dimension:]
    whole = jnp.zeros(shape, array.dtype)
    for step in range(count):
        piece = array if step == 0 else shifted(array, axis, step)
        whole = lax.dynamic_update_index_in_dim(
            whole, piece, (index + count - step) % count, dimension
        )
    return whole


def sum_rows(partial):
    count = lax.axis_size("to")
    index = lax.axis_index("to")
    width = partial.shape[-1]
    current = partial
    distance = 1
    while distance < count:
        low = (index // distance) % 2
        left = count // (2 * distance)
        shard = partial.shape[0] // count
        view = current.reshape(left, 2, shard, width)
        sent = pick(view, 1 - low, 1).astype(BF16)
        current = pick(view, low, 1) + swapped(sent, "to", distance).astype(F32)
        distance *= 2
    return current.reshape(-1, width)


def gather_rows(shard):
    count = lax.axis_size("to")
    index = lax.axis_index("to")
    rows, width = shard.shape
    current = shard.reshape(1, rows, width)
    distance = count // 2
    while distance >= 1:
        low = (index // distance) % 2
        current = paired(current, swapped(current, "to", distance), low == 0, 1)
        current = current.reshape(-1, rows, width)
        distance //= 2
    return current.reshape(-1, width)


def sum_all(vector):
    for axis in BLOCKS + TENSORS:
        distance = 1
        while distance < lax.axis_size(axis):
            vector = vector + swapped(vector, axis, distance)
            distance *= 2
    return vector


def over_pair(array):
    return jnp.concatenate([array, swapped(array, "ti")], axis=-1)


def over_blocks(array):
    return gather_axis(array, "bo")


def over_cores(array):
    whole = gather_axis(array, "bi", 1)
    return whole.reshape(-1, whole.shape[-1])


def gather_blocks(array):
    count = lax.axis_size("bo")
    mine = jnp.stack([array] + [shifted(array, "bo", step) for step in range(1, count)])
    return jnp.concatenate([mine, swapped(mine, "bi")])


def scatter_blocks(array):
    count = lax.axis_size("bo")
    mine = array[:count] + swapped(array[count:].astype(BF16), "bi").astype(F32)
    low = mine.astype(BF16)
    total = mine[0]
    for step in range(1, count):
        total += shifted(low[step], "bo", count - step).astype(F32)
    return total


def local(
    hidden_in,
    out_grad,
    norm_in,
    w_query,
    key_weight,
    value_weight,
    w_out,
    query_gain,
    key_gain,
    norm_mid,
    w_gate,
    w_up,
    w_down,
):
    block_outers = lax.axis_size("bo")
    blocks = block_outers * lax.axis_size("bi")
    block_outer = lax.axis_index("bo")
    block_inner = lax.axis_index("bi")
    block = block_outer * lax.axis_size("bi") + block_inner
    outer = lax.axis_index("to")
    inner = lax.axis_index("ti")
    pair = lax.axis_size("ti")
    batch, rows, width = hidden_in.shape
    head_dim = query_gain.shape[0] * blocks
    query_width = w_query.shape[1]
    key_width = key_weight.shape[1]
    hidden_units = w_gate.shape[1]
    query_heads = query_width * pair // head_dim
    pair_heads = key_width * pair // head_dim
    group_size = query_heads // pair_heads
    shard_rows = rows // lax.axis_size("to")
    scale = head_dim ** (-0.5)

    own_gains = jnp.concatenate([norm_in, norm_mid, query_gain, key_gain])[None]
    all_gains = gather_axis(gather_axis(own_gains, "bo"), "bi", 1)
    all_gains = all_gains.reshape(blocks, -1).astype(F32)
    part = norm_in.shape[0]
    gain_in = all_gains[:, :part].reshape(-1)
    gain_mid = all_gains[:, part : 2 * part].reshape(-1)
    head_part = query_gain.shape[0]
    gain_query = all_gains[:, 2 * part : 2 * part + head_part].reshape(-1)
    gain_key = all_gains[:, 2 * part + head_part :].reshape(-1)

    query_half = over_pair(w_query)
    kv_half = over_blocks(jnp.concatenate([key_weight, value_weight], axis=1))
    query_most = over_blocks(query_half)
    kv_most = over_pair(kv_half)
    query_full = over_cores(query_most)
    kv_full = over_cores(kv_most)
    out_half = over_pair(after(w_out.T, query_most, kv_most))
    up_half = over_blocks(after(w_up, query_most, kv_most))
    gate_half = over_pair(after(w_gate, out_half))
    out_full = over_cores(over_blocks(out_half))
    down_half = over_blocks(after(w_down.T, up_half))
    gate_full = over_cores(over_blocks(gate_half))
    up_full = over_cores(over_pair(up_half))
    down_full = over_cores(over_pair(down_half))

    positions = block * rows + jnp.arange(rows, dtype=jnp.int32)
    cosine, sine = rotation_tables(positions, head_dim)
    key_blocks = []
    for side in range(2):
        side_inner = block_inner if side == 0 else 1 - block_inner
        for step in range(block_outers):
            owner = (block_outer + block_outers - step) % block_outers
            key_blocks.append(owner * 2 + side_inner)
    key_positions = (
        jnp.stack(key_blocks).astype(jnp.int32)[:, None] * rows
        + jnp.arange(rows, dtype=jnp.int32)[None, :]
    ).reshape(-1)
    visible = key_positions[None, :] <= positions[:, None]

    def prepare(raw, gain):
        return rotate(normed(raw, gain), cosine, sine)

    groups = batch // pair
    own_hidden = pick(hidden_in.reshape(pair, groups, rows, width), inner)
    own_grad = pick(out_grad.reshape(pair, groups, rows, width), inner)
    layer_parts = []
    hidden_parts = []
    kept = []
    vector_terms = 0.0
    for group in range(groups):
        normal_in = normed(own_hidden[group].astype(F32), gain_in).astype(BF16)
        query_raw = dot(normal_in, query_full).reshape(rows, query_heads, head_dim)
        kv_raw = dot(normal_in, kv_full).reshape(rows, pair, 2, -1, head_dim)
        key_raw = kv_raw[:, :, 0].reshape(rows, pair_heads, head_dim)
        value_rows = kv_raw[:, :, 1].reshape(rows, pair_heads, head_dim).astype(BF16)
        query_rows = prepare(query_raw, gain_query).astype(BF16)
        key_rows = prepare(key_raw, gain_key).astype(BF16)
        key_value = gather_blocks(
            jnp.stack([key_rows.transpose(1, 0, 2), value_rows.transpose(1, 0, 2)])
        )
        key_value = key_value.transpose(1, 2, 0, 3, 4).reshape(
            2, pair_heads, blocks * rows, head_dim
        )
        keys, values = key_value[0], key_value[1]
        query_group = query_rows.reshape(rows, pair_heads, group_size, head_dim).transpose(
            1, 2, 0, 3
        )
        scores = jnp.einsum("hgqd,hkd->hgqk", query_group, keys, preferred_element_type=F32) * scale
        scores = jnp.where(visible, scores, -jnp.inf)
        row_max = jnp.max(scores, axis=-1)
        weights = jnp.exp(scores - row_max[..., None])
        row_sum = jnp.sum(weights, axis=-1)
        weighted = jnp.einsum(
            "hgqk,hkd->hgqd", weights.astype(BF16), values, preferred_element_type=F32
        )
        attn_group = weighted / row_sum[..., None]
        log_total = row_max + jnp.log(row_sum)
        attended = attn_group.transpose(2, 0, 1, 3).reshape(rows, -1).astype(BF16)

        start = outer * shard_rows
        x_shard = lax.dynamic_slice_in_dim(own_hidden[group], start, shard_rows, 0).astype(F32)
        grad_out_shard = lax.dynamic_slice_in_dim(own_grad[group], start, shard_rows, 0).astype(F32)
        residual = x_shard + sum_rows(dot_back(attended, out_full))
        mid = gather_rows(normed(residual, gain_mid).astype(BF16))

        grad_active = dot(own_grad[group], down_full)
        gate = dot(mid, gate_full)
        up = dot(mid, up_full)
        slope = jax.nn.sigmoid(gate)
        silu = gate * slope
        active = (silu * up).astype(BF16)
        grad_gate = (grad_active * up * slope * (1.0 + gate * (1.0 - slope))).astype(BF16)
        grad_up = (grad_active * silu).astype(BF16)
        grad_normal_mid = sum_rows(dot_back(grad_gate, gate_full) + dot_back(grad_up, up_full))

        mlp_part = dot_back(active, down_full)

        _, pull_mid = jax.vjp(normed, residual, gain_mid)
        grad_resid_norm, term_gain_mid = pull_mid(grad_normal_mid)
        grad_residual = grad_out_shard + grad_resid_norm
        branch = gather_rows(grad_residual.astype(BF16))
        layer_shard = (residual + sum_rows(after(mlp_part, branch))).astype(BF16)
        grad_attended = dot(branch, out_full).astype(BF16)

        grad_group = grad_attended.reshape(rows, pair_heads, group_size, head_dim).transpose(
            1, 2, 0, 3
        )
        row_dots = jnp.sum(grad_group.astype(F32) * attn_group, axis=-1)
        scores = jnp.einsum("hgqd,hkd->hgqk", query_group, keys, preferred_element_type=F32) * scale
        scores = jnp.where(visible, scores, -jnp.inf)
        probs = jnp.exp(scores - log_total[..., None])
        value_sum = jnp.einsum(
            "hgqk,hgqd->hkd", probs.astype(BF16), grad_group, preferred_element_type=F32
        )
        grad_probs = jnp.einsum("hgqd,hkd->hgqk", grad_group, values, preferred_element_type=F32)
        grad_scores = (probs * (grad_probs - row_dots[..., None]) * scale).astype(BF16)
        grad_query = jnp.einsum("hgqk,hkd->hgqd", grad_scores, keys, preferred_element_type=F32)
        key_sum = jnp.einsum(
            "hgqk,hgqd->hkd", grad_scores, query_group, preferred_element_type=F32
        )
        sums = jnp.stack([key_sum, value_sum]).reshape(2, pair_heads, blocks, rows, head_dim)
        shares = scatter_blocks(sums.transpose(2, 0, 1, 3, 4))
        grad_query = grad_query.transpose(2, 0, 1, 3).reshape(rows, query_heads, head_dim)
        _, pull_query = jax.vjp(prepare, query_raw, gain_query)
        grad_query_raw, term_query_gain = pull_query(grad_query)
        _, pull_key = jax.vjp(prepare, key_raw, gain_key)
        grad_key_raw, term_key_gain = pull_key(shares[0].transpose(1, 0, 2))
        grad_query_low = grad_query_raw.reshape(rows, -1).astype(BF16)
        grad_kv_low = (
            jnp.stack(
                [
                    grad_key_raw.reshape(rows, pair, -1),
                    shares[1].transpose(1, 0, 2).reshape(rows, pair, -1),
                ],
                axis=2,
            )
            .reshape(rows, -1)
            .astype(BF16)
        )
        grad_normal_in = sum_rows(
            after(
                dot_back(grad_query_low, query_full) + dot_back(grad_kv_low, kv_full), layer_shard
            )
        )
        _, pull_first = jax.vjp(normed, x_shard, gain_in)
        grad_x_norm, term_gain_in = pull_first(grad_normal_in)
        hidden_shard = (grad_residual + grad_x_norm).astype(BF16)
        layer_rows = gather_rows(layer_shard)
        layer_parts.append(gather_axis(layer_rows, "ti"))
        hidden_parts.append(gather_axis(gather_rows(after(hidden_shard, layer_rows)), "ti"))

        vector_terms += jnp.concatenate(
            [term_gain_in, term_gain_mid, term_query_gain, term_key_gain]
        )
        kept.append(
            (normal_in, grad_query_low, grad_kv_low, attended, branch, mid, grad_gate, grad_up, active)
        )

    normal_in, grad_query_low, grad_kv_low, attended, branch, mid, grad_gate, grad_up, active = (
        jnp.concatenate(parts) for parts in zip(*kept)
    )

    def in_order(array):
        own, other = jnp.split(array, 2, axis=1)
        return paired(own, other, inner == 0, 0)

    def weight_sum(left, right):
        term = jnp.concatenate(
            [
                jnp.einsum("td,tc->dc", left, right[i], preferred_element_type=F32).astype(BF16)
                for i in range(pair)
            ]
        )
        return lax.psum_scatter(
            term, ("ti", "bo", "bi"), scatter_dimension=0, tiled=True
        ).astype(F32)

    share_gu = weight_sum(mid, jnp.concatenate([in_order(grad_gate), in_order(grad_up)], axis=-1))
    grad_down = weight_sum(own_grad.reshape(-1, width), in_order(active)).T
    grad_out_w = weight_sum(branch, in_order(attended)).T
    share_qkv = weight_sum(
        normal_in, jnp.concatenate([in_order(grad_query_low), in_order(grad_kv_low)], axis=-1)
    )

    vectors = sum_all(vector_terms[None])[0]

    def vector_share(first, size):
        return lax.dynamic_slice_in_dim(vectors, first + block * (size // blocks), size // blocks)

    def whole_batch(parts):
        return jnp.stack(parts, axis=1).reshape(batch, rows, width)

    return (
        whole_batch(layer_parts),
        whole_batch(hidden_parts),
        vector_share(0, width),
        share_qkv[:, :query_width],
        share_qkv[:, query_width : query_width + key_width],
        share_qkv[:, query_width + key_width :],
        grad_out_w,
        vector_share(2 * width, head_dim),
        vector_share(2 * width + head_dim, head_dim),
        vector_share(width, width),
        share_gu[:, :hidden_units],
        share_gu[:, hidden_units:],
        grad_down,
    )


def solution(mesh):
    block_count, tensor_count = mesh.devices.shape
    split = Mesh(
        mesh.devices.reshape(block_count // 2, 2, tensor_count // 2, 2), BLOCKS + TENSORS
    )
    row_weight = P(BLOCKS, TENSORS)
    column_weight = P(TENSORS, BLOCKS)
    tokens = P(None, BLOCKS, None)
    vector = P(BLOCKS)
    weights = (
        vector,
        row_weight,
        row_weight,
        row_weight,
        column_weight,
        vector,
        vector,
        vector,
        row_weight,
        row_weight,
        column_weight,
    )
    return jax.shard_map(
        local,
        mesh=split,
        in_specs=(tokens, tokens) + weights,
        out_specs=(tokens, tokens) + weights,
        check_vma=False,
    )
```

time: 1190 us -> 758 us (0.64)
  waiting for transfers between devices: 793 us -> 368 us
  blocking collectives: 111 us -> 0 us
  starting transfers between devices: 1.56 us -> 59.1 us
  local copies, waits for them, and re-layouts: 32.7 us -> 77.6 us
  matrix products: 138 us -> 105 us
  other arithmetic: 92.8 us -> 125 us
    psum x3 -> x0, waiting for transfers between devices: 562 us -> none  [total_heads(): lax.psum(partial_sum.astype(jnp.bfloat16), 'tensor').astype(jnp.float32)]
    ppermute x0 -> x69, waiting for transfers between devices: none -> 368 us  [the longest x65 352 us: swapped(): return lax.ppermute(array, axis, [(i, i ^ distance) for i in range(count)])]
    reduce_scatter x11 -> x4, waiting for transfers between devices: 187 us -> 0.01 us  [weight_sum(): lax.psum_scatter(term, ('ti', 'bo', 'bi'), scatter_dimension=0, tiled=True)]
    all_gather x8 -> x0, blocking collectives: 74.1 us -> none  [the longest x2 18.7 us: local(): value_piece = lax.all_gather(value_rows, 'blk', axis=1, tiled=True)]
    ppermute x0 -> x69, starting transfers between devices: none -> 58.8 us  [the longest x65 54.6 us: swapped(): return lax.ppermute(array, axis, [(i, i ^ distance) for i in range(count)])]
    select_n x0 -> x51, other arithmetic: none -> 51.1 us  [paired(): jnp.where(first, jnp.stack([own, other], dimension), jnp.stack([other, ow...]
    all_gather x5 -> x0, waiting for transfers between devices: 40.6 us -> none  [the longest x1 21.4 us: local(): lax.all_gather(w_gate, 'blk', axis=0, tiled=True)]
    convert_element_type x30 -> x13, other arithmetic: 49.6 us -> 11.1 us  [the longest x2 3.32 us: local(): branch = gather_rows(grad_residual.astype(BF16))]
  transfers between devices with their start and end apart: 19 -> 73, of which waited for: 12 -> 39; matrix products, arithmetic and copies ran while one was open for 14% -> 32% of each run, Pallas kernels for 0% -> 0%
where the time goes in v1:
time: 758 us; the launch traced here: 751 us
  waiting for transfers between devices  368 us (49%)
  other arithmetic  125 us (16%)
  matrix products  105 us (14%)
  local copies, waits for them, and re-layouts  77.6 us (10%)
  starting transfers between devices  59.1 us (8%)
  between operations  17 us (2%)
    ppermute x65, waiting for transfers between devices, swapped(): return lax.ppermute(array, axis, [(i, i ^ distance) for i in range(count)])  352 us
    ppermute x65, starting transfers between devices, swapped(): return lax.ppermute(array, axis, [(i, i ^ distance) for i in range(count)])  54.6 us
    select_n x51, other arithmetic, paired(): jnp.where(first, jnp.stack([own, other], dimension), jnp.stack([other, ow...  51.1 us
    dot_general x12, matrix products, dot(): return jnp.dot(left, right, preferred_element_type=F32)  32.8 us
    unnamed x300, local copies, waits for them, and re-layouts  22.3 us
    dot_general x12, matrix products, dot_back(): return jnp.einsum('tc,dc->td', left, right, preferred_element_type=F32)  21.8 us
    dot_general x8, matrix products, weight_sum(): jnp.einsum('td,tc->dc', left, right[i], preferred_element_type=F32)  17.3 us
    ppermute x4, waiting for transfers between devices, shifted(): lax.ppermute(array, axis, [(i, (i + step) % count) for i in range(count)])  16.3 us
  transfers between devices with their start and end apart: 73, of which 39 were waited for; matrix products, arithmetic and copies ran while one was open for 32% of the time, Pallas kernels for 0%

profile of v1, /device:TPU:0, one launch (start us, length us, event | category | flops | bytes accessed | tf_op | source)
XLA Modules:
  0.0 751.3 jit_solution(2604042792771061906)
XLA Ops:
  28.4 9.1 %collective-permute-done.3 = bf16[512,512]{1,0:T(8,128)(2,1)S(1)} collective-permute-done((bf16[512,512]{1,0:T(8,128)(2,1)S(1)}, bf16[512,512]{1,0:T(8,128)(2,1)S(1)}, u32[]{:S(2)}, u32[]{:S(2)}) %collective-permute-start.3) | collective-permute-done | bytes 524320 | tf_op jit(solution)/shard_map/ppermute | solution.py:54
  102.4 5.9 collective-permute-done.8
  167.0 12.2 %collective-permute-done.13 = bf16[2,64,2048]{2,1,0:T(8,128)(2,1)S(1)} collective-permute-done((bf16[2,64,2048]{2,1,0:T(8,128)(2,1)S(1)}, bf16[2,64,2048]{2,1,0:T(8,128)(2,1)S(1)}, u32[]{:S(2)}, u32[]{:S(2)}) %collective-permute-start.13) | collective-permute-done | bytes 524320 | tf_op jit(solution)/shard_map/ppermute | solution.py:54
  183.6 10.0 %collective-permute-done.14 = bf16[1,64,2048]{2,1,0:T(8,128)(2,1)S(1)} collective-permute-done((bf16[1,64,2048]{2,1,0:T(8,128)(2,1)S(1)}, bf16[1,64,2048]{2,1,0:T(8,128)(2,1)S(1)}, u32[]{:S(2)}, u32[]{:S(2)}) %collective-permute-start.14) | collective-permute-done | bytes 262176 | tf_op jit(solution)/shard_map/ppermute | solution.py:54
  205.4 9.3 %collective-permute-done.15 = bf16[1,64,2048]{2,1,0:T(8,128)(2,1)S(1)} collective-permute-done((bf16[1,64,2048]{2,1,0:T(8,128)(2,1)S(1)}, bf16[1,64,2048]{2,1,0:T(8,128)(2,1)S(1)}, u32[]{:S(2)}, u32[]{:S(2)}) %collective-permute-start.15) | collective-permute-done | bytes 262176 | tf_op jit(solution)/shard_map/ppermute | solution.py:54
  224.6 5.9 collective-permute-done.16
  230.7 10.9 %collective-permute-done.40 = bf16[2,64,2048]{2,1,0:T(8,128)(2,1)S(1)} collective-permute-done((bf16[2,64,2048]{2,1,0:T(8,128)(2,1)S(1)}, bf16[2,64,2048]{2,1,0:T(8,128)(2,1)S(1)}, u32[]{:S(2)}, u32[]{:S(2)}) %collective-permute-start.40) | collective-permute-done | bytes 524320 | tf_op jit(solution)/shard_map/ppermute | solution.py:54
  295.5 15.6 %collective-permute-done.41 = bf16[2,64,2048]{2,1,0:T(8,128)(2,1)S(1)} collective-permute-done((bf16[2,64,2048]{2,1,0:T(8,128)(2,1)S(1)}, bf16[2,64,2048]{2,1,0:T(8,128)(2,1)S(1)}, u32[]{:S(2)}, u32[]{:S(2)}) %collective-permute-start.41) | collective-permute-done | bytes 524320 | tf_op jit(solution)/shard_map/ppermute | solution.py:54
  312.9 11.4 %collective-permute-done.42 = bf16[1,64,2048]{2,1,0:T(8,128)(2,1)S(1)} collective-permute-done((bf16[1,64,2048]{2,1,0:T(8,128)(2,1)S(1)}, bf16[1,64,2048]{2,1,0:T(8,128)(2,1)S(1)}, u32[]{:S(2)}, u32[]{:S(2)}) %collective-permute-start.42) | collective-permute-done | bytes 262176 | tf_op jit(solution)/shard_map/ppermute | solution.py:54
  332.0 15.5 %collective-permute-done.28 = bf16[1,64,2048]{2,1,0:T(8,128)(2,1)S(1)} collective-permute-done((bf16[1,64,2048]{2,1,0:T(8,128)(2,1)S(1)}, bf16[1,64,2048]{2,1,0:T(8,128)(2,1)S(1)}, u32[]{:S(2)}, u32[]{:S(2)}) %collective-permute-start.28) | collective-permute-done | bytes 262176 | tf_op jit(solution)/shard_map/ppermute | solution.py:54
  355.0 9.4 %collective-permute-done.29 = bf16[2,64,2048]{2,1,0:T(8,128)(2,1)S(1)} collective-permute-done((bf16[2,64,2048]{2,1,0:T(8,128)(2,1)S(1)}, bf16[2,64,2048]{2,1,0:T(8,128)(2,1)S(1)}, u32[]{:S(2)}, u32[]{:S(2)}) %collective-permute-start.29) | collective-permute-done | bytes 524320 | tf_op jit(solution)/shard_map/ppermute | solution.py:54
  428.5 5.9 collective-permute-done.58
  467.1 5.9 pad_maximum_fusion
  486.2 11.9 %collective-permute-done.30 = bf16[2,64,2048]{2,1,0:T(8,128)(2,1)S(1)} collective-permute-done((bf16[2,64,2048]{2,1,0:T(8,128)(2,1)S(1)}, bf16[2,64,2048]{2,1,0:T(8,128)(2,1)S(1)}, u32[]{:S(2)}, u32[]{:S(2)}) %collective-permute-start.30) | collective-permute-done | bytes 524320 | tf_op jit(solution)/shard_map/ppermute | solution.py:54
  498.9 14.5 %collective-permute-done.45 = bf16[2,64,2048]{2,1,0:T(8,128)(2,1)S(1)} collective-permute-done((bf16[2,64,2048]{2,1,0:T(8,128)(2,1)S(1)}, bf16[2,64,2048]{2,1,0:T(8,128)(2,1)S(1)}, u32[]{:S(2)}, u32[]{:S(2)}) %collective-permute-start.45) | collective-permute-done | bytes 524320 | tf_op jit(solution)/shard_map/ppermute | solution.py:54
  514.4 11.4 %collective-permute-done.46 = bf16[1,64,2048]{2,1,0:T(8,128)(2,1)S(1)} collective-permute-done((bf16[1,64,2048]{2,1,0:T(8,128)(2,1)S(1)}, bf16[1,64,2048]{2,1,0:T(8,128)(2,1)S(1)}, u32[]{:S(2)}, u32[]{:S(2)}) %collective-permute-start.46) | collective-permute-done | bytes 262176 | tf_op jit(solution)/shard_map/ppermute | solution.py:54
  533.2 11.5 %collective-permute-done.47 = bf16[1,64,2048]{2,1,0:T(8,128)(2,1)S(1)} collective-permute-done((bf16[1,64,2048]{2,1,0:T(8,128)(2,1)S(1)}, bf16[1,64,2048]{2,1,0:T(8,128)(2,1)S(1)}, u32[]{:S(2)}, u32[]{:S(2)}) %collective-permute-start.47) | collective-permute-done | bytes 262176 | tf_op jit(solution)/shard_map/ppermute | solution.py:54
  557.9 14.9 %collective-permute-done.59 = bf16[2,64,2048]{2,1,0:T(8,128)(2,1)S(1)} collective-permute-done((bf16[2,64,2048]{2,1,0:T(8,128)(2,1)S(1)}, bf16[2,64,2048]{2,1,0:T(8,128)(2,1)S(1)}, u32[]{:S(2)}, u32[]{:S(2)}) %collective-permute-start.59) | collective-permute-done | bytes 524320 | tf_op jit(solution)/shard_map/ppermute | solution.py:54
  575.0 14.7 %collective-permute-done.48 = bf16[2,64,2048]{2,1,0:T(8,128)(2,1)S(1)} collective-permute-done((bf16[2,64,2048]{2,1,0:T(8,128)(2,1)S(1)}, bf16[2,64,2048]{2,1,0:T(8,128)(2,1)S(1)}, u32[]{:S(2)}, u32[]{:S(2)}) %collective-permute-start.48) | collective-permute-done | bytes 524320 | tf_op jit(solution)/shard_map/ppermute | solution.py:54
  607.0 12.0 %collective-permute-done.67 = f32[1,4352]{1,0:T(1,128)S(1)} collective-permute-done((f32[1,4352]{1,0:T(1,128)S(1)}, f32[1,4352]{1,0:T(1,128)S(1)}, u32[]{:S(2)}, u32[]{:S(2)}) %collective-permute-start.67) | collective-permute-done | bytes 17440 | tf_op jit(solution)/shard_map/ppermute | solution.py:54
  621.9 35.7 %collective-permute-done.68 = f32[1,4352]{1,0:T(1,128)S(1)} collective-permute-done((f32[1,4352]{1,0:T(1,128)S(1)}, f32[1,4352]{1,0:T(1,128)S(1)}, u32[]{:S(2)}, u32[]{:S(2)}) %collective-permute-start.68) | collective-permute-done | bytes 17440 | tf_op jit(solution)/shard_map/ppermute | solution.py:54
  661.2 6.8 collective-permute-done.62
  679.6 28.0 %collective-permute-done.63 = bf16[256,2048]{1,0:T(8,128)(2,1)} collective-permute-done((bf16[256,2048]{1,0:T(8,128)(2,1)S(1)}, bf16[256,2048]{1,0:T(8,128)(2,1)}, u32[]{:S(2)}, u32[]{:S(2)}) %collective-permute-start.63) | collective-permute-done | bytes 1048608 | tf_op jit(solution)/shard_map/ppermute | solution.py:54
  709.4 21.0 %collective-permute-done.56 = bf16[256,2048]{1,0:T(8,128)(2,1)} collective-permute-done((bf16[256,2048]{1,0:T(8,128)(2,1)S(1)}, bf16[256,2048]{1,0:T(8,128)(2,1)}, u32[]{:S(2)}, u32[]{:S(2)}) %collective-permute-start.56) | collective-permute-done | bytes 1048608 | tf_op jit(solution)/shard_map/ppermute | solution.py:54
  (703 shorter events, 425.2 us)
Async XLA Ops:
  7.2 670.4 %reduce-scatter.7.cloned.1.call-start = ((), (), s32[]{:S(2)}) async-start(), calls=%async_computation.5 | async-start | bytes 2359296 | tf_op jit(solution)/shard_map/reduce_scatter | solution.py:358
  55.0 33.4 %collective-permute-start.4 = (bf16[2,512,512]{2,1,0:T(8,128)(2,1)}, bf16[2,512,512]{2,1,0:T(8,128)(2,1)}, u32[]{:S(2)}, u32[]{:S(2)}) collective-permute-start(bf16[2,512,512]{2,1,0:T(8,128)(2,1)} %maximum_select_fusion.17), channel_id=1, source_target_pairs={{0,8},{8,0},{1,9},{9,1},{2,10},{10,2},{3,11},{11,3},{4,12},{12,4},... | collective-permute-start | bytes 3145736 | tf_op jit(solution)/shard_map/ppermute | solution.py:54
  56.1 58.9 %collective-permute-start.17 = (bf16[512,768]{1,0:T(8,128)(2,1)}, bf16[512,768]{1,0:T(8,128)(2,1)}, u32[]{:S(2)}, u32[]{:S(2)}) collective-permute-start(bf16[512,768]{1,0:T(8,128)(2,1)} %param.23), channel_id=1, source_target_pairs={{0,1},{1,0},{2,3},{3,2},{4,5},{5,4},{6,7},{7,6},{8,9},{9,8},{10,11... | collective-permute-start | bytes 2359304 | tf_op jit(solution)/shard_map/ppermute | solution.py:54
  67.5 113.6 %collective-permute-start.21 = (bf16[2,512,768]{2,1,0:T(8,128)(2,1)}, bf16[2,512,768]{2,1,0:T(8,128)(2,1)}, u32[]{:S(2)}, u32[]{:S(2)}) collective-permute-start(bf16[2,512,768]{2,1,0:T(8,128)(2,1)} %maximum_select_fusion.12), channel_id=1, source_target_pairs={{0,1},{1,0},{2,3},{3,2},{4,5},{5,4},{6,7},{7,6},{8,9},{9,8},{10,11... | collective-permute-start | bytes 4718600 | tf_op jit(solution)/shard_map/ppermute | solution.py:54
  72.9 46.6 %collective-permute-start.23 = (bf16[512,768]{1,0:T(8,128)(2,1)}, bf16[512,768]{1,0:T(8,128)(2,1)}, u32[]{:S(2)}, u32[]{:S(2)}) collective-permute-start(bf16[512,768]{1,0:T(8,128)(2,1)} %bitcast.80), channel_id=1, source_target_pairs={{0,16},{16,0},{1,17},{17,1},{2,18},{18,2},{3,19},{19,3},{4,20},{20... | collective-permute-start | bytes 2359304 | tf_op jit(solution)/shard_map/ppermute | solution.py:54
  117.6 76.8 %collective-permute-start.18 = (bf16[512,1536]{1,0:T(8,128)(2,1)}, bf16[512,1536]{1,0:T(8,128)(2,1)}, u32[]{:S(2)}, u32[]{:S(2)}) collective-permute-start(bf16[512,1536]{1,0:T(8,128)(2,1)} %constant_dynamic-update-slice_fusion.6), channel_id=1, source_target_pairs={{0,16},{16,0},{1,17},{17,1},{2,18},{18,2},{3,19},{19,3},{4,20},{20... | collective-permute-start | bytes 4718600 | tf_op jit(solution)/shard_map/ppermute | solution.py:54
  122.9 96.7 %collective-permute-start.24 = (bf16[2,512,768]{2,1,0:T(8,128)(2,1)}, bf16[2,512,768]{2,1,0:T(8,128)(2,1)}, u32[]{:S(2)}, u32[]{:S(2)}) collective-permute-start(bf16[2,512,768]{2,1,0:T(8,128)(2,1)} %maximum_select_fusion.13), channel_id=1, source_target_pairs={{0,1},{1,0},{2,3},{3,2},{4,5},{5,4},{6,7},{7,6},{8,9},{9,8},{10,11... | collective-permute-start | bytes 4718600 | tf_op jit(solution)/shard_map/ppermute | solution.py:54
  183.5 58.4 %collective-permute-start.22 = (bf16[2,512,1536]{2,1,0:T(8,128)(2,1)S(1)}, bf16[2,512,1536]{2,1,0:T(8,128)(2,1)S(1)}, u32[]{:S(2)}, u32[]{:S(2)}) collective-permute-start(bf16[2,512,1536]{2,1,0:T(8,128)(2,1)S(1)} %get-tuple-element.123), channel_id=1, source_target_pairs={{0,8},{8,0},{1,9},{9,1},{2,10},{10,2},{3,11},{11,3},{4,12},{12,4},... | collective-permute-start | bytes 9437192 | tf_op jit(solution)/shard_map/ppermute | solution.py:54
  199.1 57.6 %collective-permute-start.19 = (bf16[2,512,1536]{2,1,0:T(8,128)(2,1)}, bf16[2,512,1536]{2,1,0:T(8,128)(2,1)}, u32[]{:S(2)}, u32[]{:S(2)}) collective-permute-start(bf16[2,512,1536]{2,1,0:T(8,128)(2,1)} %maximum_select_fusion.4), channel_id=1, source_target_pairs={{0,8},{8,0},{1,9},{9,1},{2,10},{10,2},{3,11},{11,3},{4,12},{12,4},... | collective-permute-start | bytes 9437192 | tf_op jit(solution)/shard_map/ppermute | solution.py:54
  224.6 38.0 %collective-permute-start.25 = (bf16[2,512,1536]{2,1,0:T(8,128)(2,1)}, bf16[2,512,1536]{2,1,0:T(8,128)(2,1)}, u32[]{:S(2)}, u32[]{:S(2)}) collective-permute-start(bf16[2,512,1536]{2,1,0:T(8,128)(2,1)} %get-tuple-element.121), channel_id=1, source_target_pairs={{0,8},{8,0},{1,9},{9,1},{2,10},{10,2},{3,11},{11,3},{4,12},{12,4},... | collective-permute-start | bytes 9437192 | tf_op jit(solution)/shard_map/ppermute | solution.py:54
  421.7 313.1 %reduce-scatter.5.cloned.1.call-start = ((), (), s32[]{:S(2)}) async-start(), calls=%async_computation.4 | async-start | bytes 4718592 | tf_op jit(solution)/shard_map/reduce_scatter | solution.py:358
  446.3 292.0 %reduce-scatter.11.cloned.1.call-start = ((), (), s32[]{:S(2)}) async-start(), calls=%async_computation.7 | async-start | bytes 7077888 | tf_op jit(solution)/shard_map/reduce_scatter | solution.py:358
  455.8 285.4 %reduce-scatter.9.cloned.1.call-start = ((), (), s32[]{:S(2)}) async-start(), calls=%async_computation.6 | async-start | bytes 14155776 | tf_op jit(solution)/shard_map/reduce_scatter | solution.py:358
  530.8 42.0 %collective-permute-start.59 = (bf16[2,64,2048]{2,1,0:T(8,128)(2,1)S(1)}, bf16[2,64,2048]{2,1,0:T(8,128)(2,1)S(1)}, u32[]{:S(2)}, u32[]{:S(2)}) collective-permute-start(bf16[2,64,2048]{2,1,0:T(8,128)(2,1)S(1)} %fusion.120), channel_id=1, source_target_pairs={{0,2},{2,0},{4,6},{6,4},{1,3},{3,1},{5,7},{7,5},{8,10},{10,8},{12,... | collective-permute-start | bytes 1572872 | tf_op jit(solution)/shard_map/ppermute | solution.py:54
  544.7 44.9 %collective-permute-start.48 = (bf16[2,64,2048]{2,1,0:T(8,128)(2,1)S(1)}, bf16[2,64,2048]{2,1,0:T(8,128)(2,1)S(1)}, u32[]{:S(2)}, u32[]{:S(2)}) collective-permute-start(bf16[2,64,2048]{2,1,0:T(8,128)(2,1)S(1)} %maximum_select_fusion.40), channel_id=1, source_target_pairs={{0,2},{2,0},{4,6},{6,4},{1,3},{3,1},{5,7},{7,5},{8,10},{10,8},{12,... | collective-permute-start | bytes 1572872 | tf_op jit(solution)/shard_map/ppermute | solution.py:54
  550.3 49.0 %collective-permute-start.33 = (bf16[2,64,2048]{2,1,0:T(8,128)(2,1)S(1)}, bf16[2,64,2048]{2,1,0:T(8,128)(2,1)S(1)}, u32[]{:S(2)}, u32[]{:S(2)}) collective-permute-start(bf16[2,64,2048]{2,1,0:T(8,128)(2,1)S(1)} %maximum_select_fusion.34), channel_id=1, source_target_pairs={{0,2},{2,0},{4,6},{6,4},{1,3},{3,1},{5,7},{7,5},{8,10},{10,8},{12,... | collective-permute-start | bytes 1572872 | tf_op jit(solution)/shard_map/ppermute | solution.py:54
  556.1 34.1 %collective-permute-start.53 = (bf16[1,64,2048]{2,1,0:T(8,128)(2,1)S(1)}, bf16[1,64,2048]{2,1,0:T(8,128)(2,1)S(1)}, u32[]{:S(2)}, u32[]{:S(2)}) collective-permute-start(bf16[1,64,2048]{2,1,0:T(8,128)(2,1)S(1)} %dynamic-slice_convert_fusion.2), channel_id=1, source_target_pairs={{0,4},{2,6},{4,0},{6,2},{1,5},{3,7},{5,1},{7,3},{8,12},{10,14},{12... | collective-permute-start | bytes 786440 | tf_op jit(solution)/shard_map/ppermute | solution.py:54
  589.9 84.6 %collective-permute-start.49 = (bf16[256,2048]{1,0:T(8,128)(2,1)S(1)}, bf16[256,2048]{1,0:T(8,128)(2,1)S(1)}, u32[]{:S(2)}, u32[]{:S(2)}) collective-permute-start(bf16[256,2048]{1,0:T(8,128)(2,1)S(1)} %bitcast.864), channel_id=1, source_target_pairs={{0,1},{1,0},{2,3},{3,2},{4,5},{5,4},{6,7},{7,6},{8,9},{9,8},{10,11... | collective-permute-start | bytes 3145736 | tf_op jit(solution)/shard_map/ppermute | solution.py:54
  599.6 75.2 %collective-permute-start.34 = (bf16[256,2048]{1,0:T(8,128)(2,1)S(1)}, bf16[256,2048]{1,0:T(8,128)(2,1)S(1)}, u32[]{:S(2)}, u32[]{:S(2)}) collective-permute-start(bf16[256,2048]{1,0:T(8,128)(2,1)S(1)} %bitcast.866), channel_id=1, source_target_pairs={{0,1},{1,0},{2,3},{3,2},{4,5},{5,4},{6,7},{7,6},{8,9},{9,8},{10,11... | collective-permute-start | bytes 3145736 | tf_op jit(solution)/shard_map/ppermute | solution.py:54
  603.6 55.1 %collective-permute-start.61 = (bf16[1,64,2048]{2,1,0:T(8,128)(2,1)S(1)}, bf16[1,64,2048]{2,1,0:T(8,128)(2,1)S(1)}, u32[]{:S(2)}, u32[]{:S(2)}) collective-permute-start(bf16[1,64,2048]{2,1,0:T(8,128)(2,1)S(1)} %bitcast.896), channel_id=1, source_target_pairs={{0,4},{2,6},{4,0},{6,2},{1,5},{3,7},{5,1},{7,3},{8,12},{10,14},{12... | collective-permute-start | bytes 786440 | tf_op jit(solution)/shard_map/ppermute | solution.py:54
  619.0 38.5 %collective-permute-start.68 = (f32[1,4352]{1,0:T(1,128)S(1)}, f32[1,4352]{1,0:T(1,128)S(1)}, u32[]{:S(2)}, u32[]{:S(2)}) collective-permute-start(f32[1,4352]{1,0:T(1,128)S(1)} %add.590), channel_id=1, source_target_pairs={{0,1},{1,0},{2,3},{3,2},{4,5},{5,4},{6,7},{7,6},{8,9},{9,8},{10,11... | collective-permute-start | bytes 52232 | tf_op jit(solution)/shard_map/ppermute | solution.py:54
  621.8 37.1 %collective-permute-start.54 = (bf16[1,64,2048]{2,1,0:T(8,128)(2,1)S(1)}, bf16[1,64,2048]{2,1,0:T(8,128)(2,1)S(1)}, u32[]{:S(2)}, u32[]{:S(2)}) collective-permute-start(bf16[1,64,2048]{2,1,0:T(8,128)(2,1)S(1)} %bitcast.899), channel_id=1, source_target_pairs={{0,4},{2,6},{4,0},{6,2},{1,5},{3,7},{5,1},{7,3},{8,12},{10,14},{12... | collective-permute-start | bytes 786440 | tf_op jit(solution)/shard_map/ppermute | solution.py:54
  668.4 39.2 %collective-permute-start.63 = (bf16[256,2048]{1,0:T(8,128)(2,1)S(1)}, bf16[256,2048]{1,0:T(8,128)(2,1)}, u32[]{:S(2)}, u32[]{:S(2)}) collective-permute-start(bf16[256,2048]{1,0:T(8,128)(2,1)S(1)} %bitcast.869), channel_id=1, source_target_pairs={{0,1},{1,0},{2,3},{3,2},{4,5},{5,4},{6,7},{7,6},{8,9},{9,8},{10,11... | collective-permute-start | bytes 3145736 | tf_op jit(solution)/shard_map/ppermute | solution.py:54
  674.0 56.5 %collective-permute-start.56 = (bf16[256,2048]{1,0:T(8,128)(2,1)S(1)}, bf16[256,2048]{1,0:T(8,128)(2,1)}, u32[]{:S(2)}, u32[]{:S(2)}) collective-permute-start(bf16[256,2048]{1,0:T(8,128)(2,1)S(1)} %bitcast.872), channel_id=1, source_target_pairs={{0,1},{1,0},{2,3},{3,2},{4,5},{5,4},{6,7},{7,6},{8,9},{9,8},{10,11... | collective-permute-start | bytes 3145736 | tf_op jit(solution)/shard_map/ppermute | solution.py:54
  (193 other events, 1858.6 us)
Sparse Core Ops, SparseCore 0:
  421.8 39.4 reduce-scatter.6
  465.1 51.3 reduce-scatter.4
  519.8 61.7 reduce-scatter.10
  585.4 133.8 reduce-scatter.8

commit v2 on v1

v2 whole, which is shorter than its diff:
```python
import functools

import jax
import jax.numpy as jnp
from jax import lax
from jax.experimental import pallas as pl
from jax.experimental.pallas import tpu as pltpu
from jax.sharding import Mesh
from jax.sharding import PartitionSpec as P

EPSILON = 1e-06
ROTARY_BASE = 1000000.0
BF16 = jnp.bfloat16
F32 = jnp.float32
BLOCKS = ("bo", "bi")
TENSORS = ("to", "ti")
HIDDEN_CHUNK = 512
VMEM_LIMIT = 48 * 1024 * 1024


def normed(values, gain):
    return values * lax.rsqrt(jnp.mean(values * values, axis=-1, keepdims=True) + EPSILON) * gain


def rotation_tables(positions, head_dim):
    half = head_dim // 2
    inverse = jnp.power(F32(ROTARY_BASE), -(jnp.arange(half, dtype=F32) * 2.0 / head_dim))
    angles = positions.astype(F32)[:, None] * inverse[None, :]
    cosine, sine = jnp.cos(angles), jnp.sin(angles)
    return jnp.concatenate([cosine, cosine], -1), jnp.concatenate([-sine, sine], -1)


def after(array, *earlier):
    return lax.optimization_barrier((array,) + earlier)[0]


def shifted(array, axis, step):
    count = lax.axis_size(axis)
    return lax.ppermute(array, axis, [(i, (i + step) % count) for i in range(count)])


def swapped(array, axis, distance=1):
    count = lax.axis_size(axis)
    return lax.ppermute(array, axis, [(i, i ^ distance) for i in range(count)])


def pick(array, index, dimension=0):
    return lax.dynamic_index_in_dim(array, index, dimension, keepdims=False)


def paired(own, other, first, dimension):
    return jnp.where(
        first, jnp.stack([own, other], dimension), jnp.stack([other, own], dimension)
    )


def gather_axis(array, axis, dimension=0):
    count = lax.axis_size(axis)
    index = lax.axis_index(axis)
    if count == 2:
        return paired(array, swapped(array, axis), index == 0, dimension)
    shape = array.shape[:dimension] + (count,) + array.shape[dimension:]
    whole = jnp.zeros(shape, array.dtype)
    for step in range(count):
        piece = array if step == 0 else shifted(array, axis, step)
        whole = lax.dynamic_update_index_in_dim(
            whole, piece, (index + count - step) % count, dimension
        )
    return whole


def sum_rows(kept, sent):
    count = lax.axis_size("to")
    index = lax.axis_index("to")
    rows, width = kept.shape
    shard = 2 * rows // count
    current = kept + swapped(sent, "to", 1).astype(F32)
    distance = 2
    while distance < count:
        low = (index // distance) % 2
        view = current.reshape(-1, 2, shard, width)
        sent = pick(view, 1 - low, 1).astype(BF16)
        current = pick(view, low, 1) + swapped(sent, "to", distance).astype(F32)
        distance *= 2
    return current.reshape(-1, width)


def gather_rows(shard):
    count = lax.axis_size("to")
    index = lax.axis_index("to")
    rows, width = shard.shape
    current = shard.reshape(1, rows, width)
    distance = count // 2
    while distance >= 1:
        low = (index // distance) % 2
        current = paired(current, swapped(current, "to", distance), low == 0, 1)
        current = current.reshape(-1, rows, width)
        distance //= 2
    return current.reshape(-1, width)


def sum_all(vector):
    for axis in BLOCKS + TENSORS:
        distance = 1
        while distance < lax.axis_size(axis):
            vector = vector + swapped(vector, axis, distance)
            distance *= 2
    return vector


def over_pair(array):
    return jnp.concatenate([array, swapped(array, "ti")], axis=-1)


def over_blocks(array):
    count = lax.axis_size("bo")
    return jnp.stack([array] + [shifted(array, "bo", step) for step in range(1, count)])


def over_cores(array):
    return array, swapped(array, "bi")


def mxu(left, right):
    return jnp.dot(left, right, preferred_element_type=F32)


def mxu_back(left, right):
    return lax.dot_general(left, right, (((1,), (1,)), ((), ())), preferred_element_type=F32)


def mxu_outer(left, right):
    return lax.dot_general(left, right, (((0,), (0,)), ((), ())), preferred_element_type=F32)


def columns(info, position, size):
    return pl.ds(pl.multiple_of(info[1 + position] * size, 128), size)


def project(info, rows_ref, mine, theirs):
    count, size = mine.shape[0], mine.shape[1]
    total = None
    for position in range(2 * count):
        block = mine[position] if position < count else theirs[position - count]
        term = mxu(rows_ref[:, columns(info, position, size)], block)
        total = term if total is None else total + term
    return total


def project_back(info, grads, mine, theirs, position):
    count = mine.shape[0]
    block = mine[position] if position < count else theirs[position - count]
    return mxu_back(grads, block)


def row_block(info, rows, count, position, own):
    shard = rows // count
    low = info[0] if own else 1 - info[0]
    return pl.ds(pl.multiple_of((2 * position + low) * shard, shard), shard)


def unit(values):
    return lax.rsqrt(jnp.mean(values * values, axis=-1, keepdims=True) + EPSILON)


def swap_halves(values):
    return pltpu.roll(values, values.shape[-1] // 2, 1)


def prepare_kernel(
    sizes,
    info,
    x_ref,
    gain_ref,
    query_gain_ref,
    key_gain_ref,
    cosine_ref,
    sine_ref,
    query_mine,
    query_theirs,
    kv_mine,
    kv_theirs,
    normal_ref,
    query_raw_ref,
    key_raw_ref,
    query_ref,
    kv_ref,
):
    head_dim, pair_heads, key_heads = sizes
    x = x_ref[...].astype(F32)
    normal_ref[...] = (x * unit(x) * gain_ref[...]).astype(BF16)
    cosine, sine = cosine_ref[...], sine_ref[...]

    def rotated(raw, gain):
        values = raw * unit(raw) * gain
        return (values * cosine + swap_halves(values) * sine).astype(BF16)

    query_raw = project(info, normal_ref, query_mine, query_theirs)
    query_raw_ref[...] = query_raw
    for head in range(query_raw.shape[1] // head_dim):
        part = slice(head * head_dim, (head + 1) * head_dim)
        query_ref[:, part] = rotated(query_raw[:, part], query_gain_ref[...])
    kv_raw = project(info, normal_ref, kv_mine, kv_theirs)
    for head in range(pair_heads):
        start = (2 * key_heads * (head // key_heads) + head % key_heads) * head_dim
        raw = kv_raw[:, start : start + head_dim]
        key_raw_ref[:, head * head_dim : (head + 1) * head_dim] = raw
        kv_ref[0, head] = rotated(raw, key_gain_ref[...])
        start += key_heads * head_dim
        kv_ref[1, head] = kv_raw[:, start : start + head_dim].astype(BF16)


def visible_scores(info, queries, keys, position, blocks, rows, scale):
    scores = mxu_back(queries, keys) * scale
    if position == 0:
        query_rows = lax.broadcasted_iota(jnp.int32, scores.shape, 0) % rows
        key_rows = lax.broadcasted_iota(jnp.int32, scores.shape, 1)
        return jnp.where(key_rows <= query_rows, scores, -jnp.inf)
    return jnp.where(info[1 + blocks + position] > 0, scores, -jnp.inf)


def attend_kernel(
    sizes,
    info,
    query_ref,
    kv_mine,
    kv_theirs,
    out_mine,
    out_theirs,
    attn_ref,
    log_ref,
    attended_ref,
    kept_ref,
    sent_ref,
    scores_ref,
):
    head_dim, pair_heads, group, counts = sizes
    rows = query_ref.shape[0]
    half = kv_mine.shape[0]
    scale = head_dim ** (-0.5)
    lanes = lax.broadcasted_iota(jnp.int32, (rows, head_dim), 1)
    logs = jnp.zeros((rows, head_dim), F32)

    def key_value(which, position, head):
        ref = kv_mine if position < half else kv_theirs
        return ref[position % half, which, head]

    for head in range(pair_heads):
        queries = jnp.concatenate(
            [
                query_ref[:, (head * group + i) * head_dim : (head * group + i + 1) * head_dim]
                for i in range(group)
            ]
        )
        top = None
        for position in range(2 * half):
            scores = visible_scores(
                info, queries, key_value(0, position, head), position, 2 * half, rows, scale
            )
            scores_ref[position] = scores
            block_top = jnp.max(scores, axis=-1, keepdims=True)
            top = block_top if top is None else jnp.maximum(top, block_top)
        total = jnp.zeros_like(top)
        weighted = jnp.zeros((group * rows, head_dim), F32)
        for position in range(2 * half):
            weights = jnp.exp(scores_ref[position] - top)
            total += jnp.sum(weights, axis=-1, keepdims=True)
            weighted += mxu(weights.astype(BF16), key_value(1, position, head))
        attn = weighted / total
        log_total = top + jnp.log(total)
        for i in range(group):
            index = head * group + i
            part = slice(index * head_dim, (index + 1) * head_dim)
            piece = attn[i * rows : (i + 1) * rows]
            attn_ref[:, part] = piece
            attended_ref[:, part] = piece.astype(BF16)
            logs = jnp.where(lanes == index, log_total[i * rows : (i + 1) * rows], logs)
    log_ref[...] = logs
    for own, target in ((True, kept_ref), (False, sent_ref)):
        chosen = jnp.concatenate(
            [
                attended_ref[row_block(info, rows, counts, j, own), :]
                for j in range(counts // 2)
            ]
        )
        for position in range(2 * half):
            target[:, columns(info, position, out_mine.shape[1])] = project_back(
                info, chosen, out_mine, out_theirs, position
            ).astype(target.dtype)


def feed_forward_kernel(
    counts,
    info,
    mid_ref,
    grad_ref,
    gate_mine,
    gate_theirs,
    up_mine,
    up_theirs,
    down_mine,
    down_theirs,
    active_ref,
    grad_gate_ref,
    grad_up_ref,
    grad_kept,
    grad_sent,
    mlp_kept,
    mlp_sent,
    grad_total,
    mlp_total,
):
    step = pl.program_id(0)
    rows = mid_ref.shape[0]
    half, size = gate_mine.shape[0], gate_mine.shape[1]
    gate = project(info, mid_ref, gate_mine, gate_theirs)
    up = project(info, mid_ref, up_mine, up_theirs)
    grad = project(info, grad_ref, down_mine, down_theirs)
    slope = jax.nn.sigmoid(gate)
    silu = gate * slope
    active = (silu * up).astype(BF16)
    grad_gate = (grad * up * slope * (1.0 + gate * (1.0 - slope))).astype(BF16)
    grad_up = (grad * silu).astype(BF16)
    active_ref[...] = active
    grad_gate_ref[...] = grad_gate
    grad_up_ref[...] = grad_up

    def term(position):
        part = columns(info, position, size)
        grad_term = project_back(
            info, grad_gate, gate_mine, gate_theirs, position
        ) + project_back(info, grad_up, up_mine, up_theirs, position)
        return part, grad_term, project_back(info, active, down_mine, down_theirs, position)

    @pl.when(step == 0)
    def _():
        for position in range(2 * half):
            part, grad_term, mlp_term = term(position)
            grad_total[:, part] = grad_term
            mlp_total[:, part] = mlp_term

    @pl.when(step > 0)
    def _():
        for position in range(2 * half):
            part, grad_term, mlp_term = term(position)
            grad_total[:, part] += grad_term
            mlp_total[:, part] += mlp_term

    @pl.when(step == pl.num_programs(0) - 1)
    def _():
        shard = rows // counts
        for j in range(counts // 2):
            place = slice(j * shard, (j + 1) * shard)
            for own, grad_out, mlp_out in (
                (True, grad_kept, mlp_kept),
                (False, grad_sent, mlp_sent),
            ):
                source = row_block(info, rows, counts, j, own)
                grad_out[place, :] = grad_total[source, :].astype(grad_out.dtype)
                mlp_out[place, :] = mlp_total[source, :].astype(mlp_out.dtype)


def attend_back_kernel(
    sizes,
    info,
    branch_ref,
    out_mine,
    out_theirs,
    query_ref,
    kv_mine,
    kv_theirs,
    attn_ref,
    log_ref,
    grad_query_ref,
    kept_ref,
    sent_ref,
):
    head_dim, pair_heads, group = sizes
    rows = query_ref.shape[0]
    half = kv_mine.shape[0]
    scale = head_dim ** (-0.5)
    grad_attended = project(info, branch_ref, out_mine, out_theirs).astype(BF16)

    def key_value(which, position, head):
        ref = kv_mine if position < half else kv_theirs
        return ref[position % half, which, head]

    for head in range(pair_heads):
        parts = [
            slice((head * group + i) * head_dim, (head * group + i + 1) * head_dim)
            for i in range(group)
        ]
        queries = jnp.concatenate([query_ref[:, part] for part in parts])
        grads = jnp.concatenate([grad_attended[:, part] for part in parts])
        attn = jnp.concatenate([attn_ref[:, part] for part in parts])
        logs = jnp.concatenate(
            [log_ref[:, head * group + i : head * group + i + 1] for i in range(group)]
        )
        row_dots = jnp.sum(grads.astype(F32) * attn, axis=-1, keepdims=True)
        grad_query = jnp.zeros((group * rows, head_dim), F32)
        for position in range(2 * half):
            keys = key_value(0, position, head)
            scores = visible_scores(info, queries, keys, position, 2 * half, rows, scale)
            probs = jnp.exp(scores - logs)
            grad_probs = mxu_back(grads, key_value(1, position, head))
            grad_scores = (probs * (grad_probs - row_dots) * scale).astype(BF16)
            grad_query += mxu(grad_scores, keys)
            target = kept_ref if position < half else sent_ref
            target[position % half, 0, head] = mxu_outer(grad_scores, queries).astype(target.dtype)
            target[position % half, 1, head] = mxu_outer(probs.astype(BF16), grads).astype(
                target.dtype
            )
        for i, part in enumerate(parts):
            grad_query_ref[:, part] = grad_query[i * rows : (i + 1) * rows]


def finish_kernel(
    sizes,
    info,
    grad_query_ref,
    query_raw_ref,
    key_raw_ref,
    shares_ref,
    query_gain_ref,
    key_gain_ref,
    cosine_ref,
    sine_ref,
    query_mine,
    query_theirs,
    kv_mine,
    kv_theirs,
    query_low_ref,
    kv_low_ref,
    gains_ref,
    kept_ref,
    sent_ref,
):
    head_dim, pair_heads, key_heads, counts = sizes
    rows = grad_query_ref.shape[0]
    cosine, sine = cosine_ref[...], sine_ref[...]

    def back(grad, raw, gain):
        grad = grad * cosine - swap_halves(grad) * sine
        scale = unit(raw)
        gain_term = jnp.sum(grad * raw * scale, axis=0, keepdims=True)
        inner = grad * gain
        mean = jnp.mean(inner * raw, axis=-1, keepdims=True)
        return (scale * inner - raw * (scale * scale * scale * mean)).astype(BF16), gain_term

    total = jnp.zeros((1, head_dim), F32)
    for head in range(query_raw_ref.shape[1] // head_dim):
        part = slice(head * head_dim, (head + 1) * head_dim)
        query_low_ref[:, part], term = back(
            grad_query_ref[:, part], query_raw_ref[:, part], query_gain_ref[...]
        )
        total += term
    gains_ref[0:1, :] = total
    total = jnp.zeros((1, head_dim), F32)
    for head in range(pair_heads):
        start = (2 * key_heads * (head // key_heads) + head % key_heads) * head_dim
        kv_low_ref[:, start : start + head_dim], term = back(
            shares_ref[0, head],
            key_raw_ref[:, head * head_dim : (head + 1) * head_dim],
            key_gain_ref[...],
        )
        total += term
        start += key_heads * head_dim
        kv_low_ref[:, start : start + head_dim] = shares_ref[1, head].astype(BF16)
    gains_ref[1:2, :] = total
    for own, target in ((True, kept_ref), (False, sent_ref)):
        places = [row_block(info, rows, counts, j, own) for j in range(counts // 2)]
        query_low = jnp.concatenate([query_low_ref[place, :] for place in places])
        kv_low = jnp.concatenate([kv_low_ref[place, :] for place in places])
        for position in range(2 * query_mine.shape[0]):
            target[:, columns(info, position, query_mine.shape[1])] = (
                project_back(info, query_low, query_mine, query_theirs, position)
                + project_back(info, kv_low, kv_mine, kv_theirs, position)
            ).astype(target.dtype)


def weight_kernel(groups, products, info, *refs):
    inputs, out_ref = refs[:-1], refs[-1]
    place = 0
    for index, (left, rights) in enumerate(products):
        lefts = [inputs[left * groups + g][...] for g in range(groups)]
        for right in rights:
            total = None
            for g in range(groups):
                term = mxu_outer(lefts[g], inputs[right * groups + g][...])
                total = term if total is None else total + term
            size = total.shape[1]
            if out_ref.ndim == 5:
                out_ref[0, 0, place] = total.astype(BF16)
                place += 1
            else:
                out_ref[0, 0, :, place : place + size] = total.astype(BF16)
                place += size


def call(kernel, operands, outputs, scratch=(), flops=0, memory=()):
    smem = pl.BlockSpec(memory_space=pltpu.SMEM)
    vmem = pl.BlockSpec(memory_space=pltpu.VMEM)
    moved = sum(a.size * a.dtype.itemsize for a in tuple(operands[1:]) + tuple(outputs))
    return pl.pallas_call(
        kernel,
        out_shape=tuple(outputs),
        in_specs=[smem] + [vmem] * (len(operands) - 1),
        out_specs=tuple(vmem for _ in outputs),
        scratch_shapes=list(scratch),
        compiler_params=pltpu.CompilerParams(vmem_limit_bytes=VMEM_LIMIT),
        cost_estimate=pl.CostEstimate(flops=flops, bytes_accessed=moved, transcendentals=0),
    )(*operands)


def shape(dims, dtype):
    return jax.ShapeDtypeStruct(dims, dtype)


def weight_blocks(info, lefts, rights, products, blocks, pair, stacked):
    groups = len(lefts[0])
    rows, width = lefts[0][0].shape
    size = width // blocks
    operands, specs = [], []
    for members in lefts:
        for array in members:
            operands.append(array)
            specs.append(pl.BlockSpec((rows, size), lambda t, b, info: (0, b)))
    for members in rights:
        for array in members:
            operands.append(array)
            specs.append(
                pl.BlockSpec(
                    (rows, array.shape[1] // pair),
                    lambda t, b, info: (0, lax.rem(t + info[0], 2)),
                )
            )
    widths = [array.shape[1] // pair for array, *_ in rights]
    if stacked:
        dims = (pair, blocks, len(rights), size, widths[0])
        out_spec = pl.BlockSpec((1, 1) + dims[2:], lambda t, b, info: (t, b, 0, 0, 0))
    else:
        dims = (pair, blocks, size, sum(widths))
        out_spec = pl.BlockSpec((1, 1) + dims[2:], lambda t, b, info: (t, b, 0, 0))
    shifted_products = [
        (left, [len(lefts) + right for right in columns_of]) for left, columns_of in products
    ]
    flops = 2 * groups * rows * width * pair * sum(widths)
    moved = 2 * pair * width * sum(widths)
    return pl.pallas_call(
        functools.partial(weight_kernel, groups, shifted_products),
        out_shape=shape(dims, BF16),
        grid_spec=pltpu.PrefetchScalarGridSpec(
            num_scalar_prefetch=1,
            grid=(pair, blocks),
            in_specs=specs,
            out_specs=out_spec,
        ),
        compiler_params=pltpu.CompilerParams(vmem_limit_bytes=VMEM_LIMIT),
        cost_estimate=pl.CostEstimate(flops=flops, bytes_accessed=moved, transcendentals=0),
    )(info, *operands)


def local(
    hidden_in,
    out_grad,
    norm_in,
    w_query,
    key_weight,
    value_weight,
    w_out,
    query_gain,
    key_gain,
    norm_mid,
    w_gate,
    w_up,
    w_down,
):
    block_outers = lax.axis_size("bo")
    blocks = block_outers * lax.axis_size("bi")
    block_outer = lax.axis_index("bo")
    block_inner = lax.axis_index("bi")
    block = block_outer * lax.axis_size("bi") + block_inner
    outer = lax.axis_index("to")
    inner = lax.axis_index("ti")
    pair = lax.axis_size("ti")
    counts = lax.axis_size("to")
    batch, rows, width = hidden_in.shape
    head_dim = query_gain.shape[0] * blocks
    query_width = w_query.shape[1]
    key_width = key_weight.shape[1]
    hidden_units = w_gate.shape[1]
    key_heads = key_width // head_dim
    query_heads = query_width * pair // head_dim
    pair_heads = key_heads * pair
    group_size = query_heads // pair_heads
    shard_rows = rows // counts

    own_gains = jnp.concatenate([norm_in, norm_mid, query_gain, key_gain])[None]
    all_gains = gather_axis(gather_axis(own_gains, "bo"), "bi", 1)
    all_gains = all_gains.reshape(blocks, -1).astype(F32)
    part = norm_in.shape[0]
    gain_in = all_gains[:, :part].reshape(-1)
    gain_mid = all_gains[:, part : 2 * part].reshape(-1)
    head_part = query_gain.shape[0]
    gain_query = all_gains[:, 2 * part : 2 * part + head_part].reshape(1, -1)
    gain_key = all_gains[:, 2 * part + head_part :].reshape(1, -1)

    query_half = over_pair(w_query)
    kv_half = over_blocks(jnp.concatenate([key_weight, value_weight], axis=1))
    query_most = over_blocks(query_half)
    kv_most = over_pair(kv_half)
    query_full = over_cores(query_most)
    kv_full = over_cores(kv_most)
    out_half = over_pair(after(w_out.T, query_most, kv_most))
    up_half = over_blocks(after(w_up, query_most, kv_most))
    gate_half = over_pair(after(w_gate, out_half))
    out_full = over_cores(over_blocks(out_half))
    down_half = over_blocks(after(w_down.T, up_half))
    gate_full = over_cores(over_blocks(gate_half))
    up_full = over_cores(over_pair(up_half))
    down_full = over_cores(over_pair(down_half))

    positions = block * rows + jnp.arange(rows, dtype=jnp.int32)
    cosine, sine = rotation_tables(positions, head_dim)
    block_ids = []
    for side in range(2):
        side_inner = block_inner if side == 0 else 1 - block_inner
        for step in range(block_outers):
            owner = lax.rem(block_outer + block_outers - step, block_outers)
            block_ids.append(owner * 2 + side_inner)
    info = jnp.stack(
        [lax.rem(outer, 2)] + block_ids + [(b < block).astype(jnp.int32) for b in block_ids]
    ).astype(jnp.int32)
    inner_info = inner.astype(jnp.int32)[None]

    groups = batch // pair
    own_hidden = pick(hidden_in.reshape(pair, groups, rows, width), inner)
    own_grad = pick(out_grad.reshape(pair, groups, rows, width), inner)
    half_rows = rows // 2
    halves = (shape((half_rows, width), F32), shape((half_rows, width), BF16))
    all_heads = query_heads * head_dim
    all_keys = pair_heads * head_dim
    kv_dims = (2, pair_heads, rows, head_dim)
    layer_parts = []
    hidden_parts = []
    kept = []
    vector_terms = 0.0
    for group in range(groups):
        normal_in, query_raw, key_raw, query_rows, kv_rows = call(
            functools.partial(prepare_kernel, (head_dim, pair_heads, key_heads)),
            (info, own_hidden[group], gain_in[None], gain_query, gain_key, cosine, sine)
            + query_full
            + kv_full,
            (
                shape((rows, width), BF16),
                shape((rows, all_heads), F32),
                shape((rows, all_keys), F32),
                shape((rows, all_heads), BF16),
                shape(kv_dims, BF16),
            ),
            flops=2 * rows * width * (all_heads + 2 * all_keys),
        )
        key_value = over_cores(over_blocks(kv_rows))
        attn, log_total, attended, out_kept, out_sent = call(
            functools.partial(attend_kernel, (head_dim, pair_heads, group_size, counts)),
            (info, query_rows) + key_value + out_full,
            (
                shape((rows, all_heads), F32),
                shape((rows, head_dim), F32),
                shape((rows, all_heads), BF16),
            )
            + halves,
            scratch=[pltpu.VMEM((blocks, group_size * rows, rows), F32)],
            flops=2 * rows * all_heads * (width + 4 * blocks * rows),
        )

        start = outer * shard_rows
        x_shard = lax.dynamic_slice_in_dim(own_hidden[group], start, shard_rows, 0).astype(F32)
        grad_out_shard = lax.dynamic_slice_in_dim(own_grad[group], start, shard_rows, 0).astype(F32)
        residual = x_shard + sum_rows(out_kept, out_sent)
        mid = gather_rows(normed(residual, gain_mid).astype(BF16))

        whole = pl.BlockSpec((rows, width), lambda i: (0, 0))
        weight = pl.BlockSpec(
            (block_outers, width // blocks, HIDDEN_CHUNK), lambda i: (0, 0, i)
        )
        piece = pl.BlockSpec((rows, HIDDEN_CHUNK), lambda i: (0, i))
        half_spec = pl.BlockSpec((half_rows, width), lambda i: (0, 0))
        hidden_shape = shape((rows, pair * hidden_units), BF16)
        active, grad_gate, grad_up, grad_kept, grad_sent, mlp_kept, mlp_sent = pl.pallas_call(
            functools.partial(feed_forward_kernel, counts),
            out_shape=(hidden_shape,) * 3 + halves + halves,
            grid=(pair * hidden_units // HIDDEN_CHUNK,),
            in_specs=[pl.BlockSpec(memory_space=pltpu.SMEM), whole, whole] + [weight] * 6,
            out_specs=(piece,) * 3 + (half_spec,) * 4,
            scratch_shapes=[pltpu.VMEM((rows, width), F32)] * 2,
            compiler_params=pltpu.CompilerParams(vmem_limit_bytes=VMEM_LIMIT),
            cost_estimate=pl.CostEstimate(
                flops=12 * rows * width * pair * hidden_units,
                bytes_accessed=6 * width * pair * hidden_units,
                transcendentals=rows * pair * hidden_units,
            ),
        )(info, mid, own_grad[group], *gate_full, *up_full, *down_full)
        grad_normal_mid = sum_rows(grad_kept, grad_sent)

        _, pull_mid = jax.vjp(normed, residual, gain_mid)
        grad_resid_norm, term_gain_mid = pull_mid(grad_normal_mid)
        grad_residual = grad_out_shard + grad_resid_norm
        branch = gather_rows(grad_residual.astype(BF16))
        layer_shard = (residual + sum_rows(mlp_kept, after(mlp_sent, branch))).astype(BF16)

        side_dims = (block_outers,) + kv_dims
        grad_query, kv_kept, kv_sent = call(
            functools.partial(attend_back_kernel, (head_dim, pair_heads, group_size)),
            (info, branch) + out_full + (query_rows,) + key_value + (attn, log_total),
            (shape((rows, all_heads), F32), shape(side_dims, F32), shape(side_dims, BF16)),
            flops=2 * rows * all_heads * (width + 10 * blocks * rows),
        )
        mine = kv_kept + swapped(kv_sent, "bi").astype(F32)
        low = mine.astype(BF16)
        shares = mine[0]
        for step in range(1, block_outers):
            shares += shifted(low[step], "bo", block_outers - step).astype(F32)
        grad_query_low, grad_kv_low, gain_terms, in_kept, in_sent = call(
            functools.partial(finish_kernel, (head_dim, pair_heads, key_heads, counts)),
            (info, grad_query, query_raw, key_raw, shares, gain_query, gain_key, cosine, sine)
            + query_full
            + kv_full,
            (
                shape((rows, all_heads), BF16),
                shape((rows, 2 * all_keys), BF16),
                shape((2, head_dim), F32),
            )
            + halves,
            flops=2 * rows * width * (all_heads + 2 * all_keys),
        )
        grad_normal_in = sum_rows(in_kept, after(in_sent, layer_shard))
        _, pull_first = jax.vjp(normed, x_shard, gain_in)
        grad_x_norm, term_gain_in = pull_first(grad_normal_in)
        hidden_shard = (grad_residual + grad_x_norm).astype(BF16)
        layer_rows = gather_rows(layer_shard)
        layer_parts.append(gather_axis(layer_rows, "ti"))
        hidden_parts.append(gather_axis(gather_rows(after(hidden_shard, layer_rows)), "ti"))

        vector_terms += jnp.concatenate([term_gain_in, term_gain_mid, gain_terms.reshape(-1)])
        kept.append(
            (normal_in, grad_query_low, grad_kv_low, attended, branch, mid)
            + (own_grad[group], grad_gate, grad_up, active)
        )

    (
        normal_in,
        grad_query_low,
        grad_kv_low,
        attended,
        branch,
        mid,
        grad_rows,
        grad_gate,
        grad_up,
        active,
    ) = zip(*kept)

    def weight_sum(terms):
        flat = terms.reshape((-1,) + terms.shape[-1:])
        share = lax.psum_scatter(flat, ("ti", "bo", "bi"), scatter_dimension=0, tiled=True)
        return share.astype(F32).reshape(terms.shape[2:])

    share_mlp = weight_sum(
        weight_blocks(
            inner_info,
            (mid, grad_rows),
            (grad_gate, grad_up, active),
            [(0, [0, 1]), (1, [2])],
            blocks,
            pair,
            True,
        )
    )
    share_attn = weight_sum(
        weight_blocks(
            inner_info,
            (normal_in, branch),
            (grad_query_low, grad_kv_low, attended),
            [(0, [0, 1]), (1, [2])],
            blocks,
            pair,
            False,
        )
    )
    vectors = sum_all(vector_terms[None])[0]

    def vector_share(first, size):
        return lax.dynamic_slice_in_dim(vectors, first + block * (size // blocks), size // blocks)

    def whole_batch(parts):
        return jnp.stack(parts, axis=1).reshape(batch, rows, width)

    kv_start = query_width + 2 * key_width
    return (
        whole_batch(layer_parts),
        whole_batch(hidden_parts),
        vector_share(0, width),
        share_attn[:, :query_width],
        share_attn[:, query_width : query_width + key_width],
        share_attn[:, query_width + key_width : kv_start],
        share_attn[:, kv_start:].T,
        vector_share(2 * width, head_dim),
        vector_share(2 * width + head_dim, head_dim),
        vector_share(width, width),
        share_mlp[0],
        share_mlp[1],
        share_mlp[2].T,
    )


def solution(mesh):
    block_count, tensor_count = mesh.devices.shape
    split = Mesh(
        mesh.devices.reshape(block_count // 2, 2, tensor_count // 2, 2), BLOCKS + TENSORS
    )
    row_weight = P(BLOCKS, TENSORS)
    column_weight = P(TENSORS, BLOCKS)
    tokens = P(None, BLOCKS, None)
    vector = P(BLOCKS)
    weights = (
        vector,
        row_weight,
        row_weight,
        row_weight,
        column_weight,
        vector,
        vector,
        vector,
        row_weight,
        row_weight,
        column_weight,
    )
    return jax.shard_map(
        local,
        mesh=split,
        in_specs=(tokens, tokens) + weights,
        out_specs=(tokens, tokens) + weights,
        check_vma=False,
    )
```

time: 758 us -> 691 us (0.912)
  matrix products: 105 us -> 0 us
  Pallas kernels: 0 us -> 97.4 us
  other arithmetic: 125 us -> 38.2 us
  local copies, waits for them, and re-layouts: 77.6 us -> 94.3 us
  starting transfers between devices: 59.1 us -> 68.4 us
    dot_general x44 -> x0, matrix products: 105 us -> none  [the longest x12 32.8 us: dot(): return jnp.dot(left, right, preferred_element_type=F32)]
    pallas_call x0 -> x12, Pallas kernels: none -> 97.4 us  [the longest x8 42.3 us: call(): pl.pallas_call(kernel, out_shape=tuple(outputs), in_specs=[smem] + [vmem]...]
    select_n x51 -> x30, other arithmetic: 51.1 us -> 4.07 us  [paired(): jnp.where(first, jnp.stack([own, other], dimension), jnp.stack([other, ow...]
    reshape x0 -> x4, local copies, waits for them, and re-layouts: none -> 31.8 us  [the longest x2 31.6 us: weight_sum(): flat = terms.reshape((-1,) + terms.shape[-1:])]
    ppermute x65 -> x59, waiting for transfers between devices: 352 us -> 326 us  [swapped(): return lax.ppermute(array, axis, [(i, i ^ distance) for i in range(count)])]
    ppermute x4 -> x10, waiting for transfers between devices: 16.3 us -> 39.2 us  [shifted(): lax.ppermute(array, axis, [(i, (i + step) % count) for i in range(count)])]
    unnamed x300 -> x165, local copies, waits for them, and re-layouts: 22.3 us -> 37.7 us
    another operation x9 -> x1, local copies, waits for them, and re-layouts: 12.1 us -> 0.08 us  [local(): jnp.stack([lax.rem(outer, 2)] + block_ids + [(b < block).astype(jnp.int32...]
  transfers between devices with their start and end apart: 73 -> 71, of which waited for: 39 -> 40; matrix products, arithmetic and copies ran while one was open for 32% -> 13% of each run, Pallas kernels for 0% -> 9%
where the time goes in v2:
time: 691 us; the launch traced here: 680 us
  waiting for transfers between devices  366 us (53%)
  Pallas kernels  97.4 us (14%)
  local copies, waits for them, and re-layouts  94.3 us (14%)
  starting transfers between devices  68.4 us (10%)
  other arithmetic  38.2 us (6%)
  between operations  16 us (2%)
    ppermute x59, waiting for transfers between devices, swapped(): return lax.ppermute(array, axis, [(i, i ^ distance) for i in range(count)])  326 us
    ppermute x59, starting transfers between devices, swapped(): return lax.ppermute(array, axis, [(i, i ^ distance) for i in range(count)])  58.6 us
    pallas_call x8, Pallas kernels, call(): pl.pallas_call(kernel, out_shape=tuple(outputs), in_specs=[smem] + [vmem]...  42.3 us
    ppermute x10, waiting for transfers between devices, shifted(): lax.ppermute(array, axis, [(i, (i + step) % count) for i in range(count)])  39.2 us
    unnamed x165, local copies, waits for them, and re-layouts  37.7 us
    pallas_call x2, Pallas kernels, local(): pl.pallas_call(functools.partial(feed_forward_kernel, counts), out_shape=...  31.9 us
    reshape x2, local copies, waits for them, and re-layouts, weight_sum(): flat = terms.reshape((-1,) + terms.shape[-1:])  31.6 us
    pallas_call x2, Pallas kernels, weight_blocks(): pl.pallas_call(functools.partial(weight_kernel, groups, shifted_products)...  23.2 us
  transfers between devices with their start and end apart: 71, of which 40 were waited for; matrix products, arithmetic and copies ran while one was open for 13% of the time, Pallas kernels for 9%

profile of v2, /device:TPU:0, one launch (start us, length us, event | category | flops | bytes accessed | tf_op | source)
XLA Modules:
  0.0 679.9 jit_solution(186684470009331403)
XLA Ops:
  25.6 10.5 %collective-permute-done.3 = bf16[512,512]{1,0:T(8,128)(2,1)S(1)} collective-permute-done((bf16[512,512]{1,0:T(8,128)(2,1)S(1)}, bf16[512,512]{1,0:T(8,128)(2,1)S(1)}, u32[]{:S(2)}, u32[]{:S(2)}) %collective-permute-start.3) | collective-permute-done | bytes 524320 | tf_op jit(solution)/shard_map/ppermute | solution.py:39
  51.4 9.4 %collective-permute-done.20 = bf16[512,768]{1,0:T(8,128)(2,1)} collective-permute-done((bf16[512,768]{1,0:T(8,128)(2,1)}, bf16[512,768]{1,0:T(8,128)(2,1)}, u32[]{:S(2)}, u32[]{:S(2)}) %collective-permute-start.20) | collective-permute-done | bytes 786464 | tf_op jit(solution)/shard_map/ppermute | solution.py:39
  123.1 12.5 %collective-permute-done.37 = bf16[128,2048]{1,0:T(8,128)(2,1)S(1)} collective-permute-done((bf16[128,2048]{1,0:T(8,128)(2,1)S(1)}, bf16[128,2048]{1,0:T(8,128)(2,1)S(1)}, u32[]{:S(2)}, u32[]{:S(2)}) %collective-permute-start.37) | collective-permute-done | bytes 524320 | tf_op jit(solution)/shard_map/ppermute | solution.py:44
  153.0 17.6 %collective-permute-done.39 = bf16[1,64,2048]{2,1,0:T(8,128)(2,1)S(1)} collective-permute-done((bf16[1,64,2048]{2,1,0:T(8,128)(2,1)S(1)}, bf16[1,64,2048]{2,1,0:T(8,128)(2,1)S(1)}, u32[]{:S(2)}, u32[]{:S(2)}) %collective-permute-start.39) | collective-permute-done | bytes 262176 | tf_op jit(solution)/shard_map/ppermute | solution.py:44
  175.5 10.3 %collective-permute-done.40 = bf16[2,64,2048]{2,1,0:T(8,128)(2,1)S(1)} collective-permute-done((bf16[2,64,2048]{2,1,0:T(8,128)(2,1)S(1)}, bf16[2,64,2048]{2,1,0:T(8,128)(2,1)S(1)}, u32[]{:S(2)}, u32[]{:S(2)}) %collective-permute-start.40) | collective-permute-done | bytes 524320 | tf_op jit(solution)/shard_map/ppermute | solution.py:44
  187.1 9.9 %collective-permute-done.16 = bf16[2,64,2048]{2,1,0:T(8,128)(2,1)S(1)} collective-permute-done((bf16[2,64,2048]{2,1,0:T(8,128)(2,1)S(1)}, bf16[2,64,2048]{2,1,0:T(8,128)(2,1)S(1)}, u32[]{:S(2)}, u32[]{:S(2)}) %collective-permute-start.16) | collective-permute-done | bytes 524320 | tf_op jit(solution)/shard_map/ppermute | solution.py:44
  202.1 15.9 %shard_map.230 = (bf16[256,1536]{1,0:T(8,128)(2,1)S(1)}, bf16[256,1536]{1,0:T(8,128)(2,1)S(1)}, bf16[256,1536]{1,0:T(8,128)(2,1)S(1)}, f32[128,2048]{1,0:T(8,128...) custom-call(s32[9]{0:T(128)S(1)} %stack.425.info, ...), custom_call_target="tpu_custom_call" | custom-call | flops 9663676416 | bytes 18874368 | tf_op jit(solution)/shard_map/pallas_call | solution.py:690
  222.5 16.1 %shard_map.233 = (bf16[256,1536]{1,0:T(8,128)(2,1)S(1)}, bf16[256,1536]{1,0:T(8,128)(2,1)S(1)}, bf16[256,1536]{1,0:T(8,128)(2,1)S(1)}, f32[128,2048]{1,0:T(8,128...) custom-call(s32[9]{0:T(128)S(1)} %stack.425.info, ...), custom_call_target="tpu_custom_call" | custom-call | flops 9663676416 | bytes 18874368 | tf_op jit(solution)/shard_map/pallas_call | solution.py:690
  243.0 15.2 %collective-permute-done.41 = bf16[128,2048]{1,0:T(8,128)(2,1)S(1)} collective-permute-done((bf16[128,2048]{1,0:T(8,128)(2,1)S(1)}, bf16[128,2048]{1,0:T(8,128)(2,1)S(1)}, u32[]{:S(2)}, u32[]{:S(2)}) %collective-permute-start.41) | collective-permute-done | bytes 524320 | tf_op jit(solution)/shard_map/ppermute | solution.py:44
  260.1 12.5 %collective-permute-done.42 = bf16[1,64,2048]{2,1,0:T(8,128)(2,1)S(1)} collective-permute-done((bf16[1,64,2048]{2,1,0:T(8,128)(2,1)S(1)}, bf16[1,64,2048]{2,1,0:T(8,128)(2,1)S(1)}, u32[]{:S(2)}, u32[]{:S(2)}) %collective-permute-start.42) | collective-permute-done | bytes 262176 | tf_op jit(solution)/shard_map/ppermute | solution.py:44
  279.6 15.8 %collective-permute-done.43 = bf16[1,64,2048]{2,1,0:T(8,128)(2,1)S(1)} collective-permute-done((bf16[1,64,2048]{2,1,0:T(8,128)(2,1)S(1)}, bf16[1,64,2048]{2,1,0:T(8,128)(2,1)S(1)}, u32[]{:S(2)}, u32[]{:S(2)}) %collective-permute-start.43) | collective-permute-done | bytes 262176 | tf_op jit(solution)/shard_map/ppermute | solution.py:44
  300.8 10.9 %collective-permute-done.44 = bf16[2,64,2048]{2,1,0:T(8,128)(2,1)S(1)} collective-permute-done((bf16[2,64,2048]{2,1,0:T(8,128)(2,1)S(1)}, bf16[2,64,2048]{2,1,0:T(8,128)(2,1)S(1)}, u32[]{:S(2)}, u32[]{:S(2)}) %collective-permute-start.44) | collective-permute-done | bytes 524320 | tf_op jit(solution)/shard_map/ppermute | solution.py:44
  380.0 15.6 %shard_map.239 = bf16[2,4,3,512,768]{4,3,2,1,0:T(8,128)(2,1)} custom-call(s32[1]{0:T(128)} %bitcast.142.info, bf16[256,2048]{1,0:T(8,128)(2,1)S(1)} %bitcast.428, bf16[256,2048]{1,0:T(8,128)(2,1)} %bitcast.492, bf16[256,2048]{1,0:T(8,128)(2,1)} %get-tuple-element.188.grad_ref.refs_2_, bf16[256,2048]{1,0:T(8,128)(2,1)} %get-tuple-element.189.grad_ref.refs_3_, ...), custom_call_target="tpu_custom_call" | custom-call | flops 9663676416 | bytes 18874368 | tf_op jit(solution)/shard_map/pallas_call | solution.py:549
  395.6 22.9 %copy.98 = bf16[12288,768]{0,1:T(8,128)(2,1)} copy(bf16[12288,768]{1,0:T(8,128)(2,1)} %bitcast.434) | data formatting | bytes 37748736 | tf_op jit(solution)/shard_map/reshape | solution.py:765
  421.7 11.8 %collective-permute-done.45 = bf16[128,2048]{1,0:T(8,128)(2,1)} collective-permute-done((bf16[128,2048]{1,0:T(8,128)(2,1)S(1)}, bf16[128,2048]{1,0:T(8,128)(2,1)}, u32[]{:S(2)}, u32[]{:S(2)}) %collective-permute-start.45) | collective-permute-done | bytes 524320 | tf_op jit(solution)/shard_map/ppermute | solution.py:44
  436.2 14.0 %collective-permute-done.30 = bf16[128,2048]{1,0:T(8,128)(2,1)S(1)} collective-permute-done((bf16[128,2048]{1,0:T(8,128)(2,1)S(1)}, bf16[128,2048]{1,0:T(8,128)(2,1)S(1)}, u32[]{:S(2)}, u32[]{:S(2)}) %collective-permute-start.30) | collective-permute-done | bytes 524320 | tf_op jit(solution)/shard_map/ppermute | solution.py:44
  453.6 17.3 %collective-permute-done.31 = bf16[1,64,2048]{2,1,0:T(8,128)(2,1)S(1)} collective-permute-done((bf16[1,64,2048]{2,1,0:T(8,128)(2,1)S(1)}, bf16[1,64,2048]{2,1,0:T(8,128)(2,1)S(1)}, u32[]{:S(2)}, u32[]{:S(2)}) %collective-permute-start.31) | collective-permute-done | bytes 262176 | tf_op jit(solution)/shard_map/ppermute | solution.py:44
  488.1 19.4 %collective-permute-done.52 = bf16[128,2048]{1,0:T(8,128)(2,1)S(1)} collective-permute-done((bf16[128,2048]{1,0:T(8,128)(2,1)S(1)}, bf16[128,2048]{1,0:T(8,128)(2,1)S(1)}, u32[]{:S(2)}, u32[]{:S(2)}) %collective-permute-start.52) | collective-permute-done | bytes 524320 | tf_op jit(solution)/shard_map/ppermute | solution.py:44
  510.9 17.4 %collective-permute-done.53 = bf16[1,64,2048]{2,1,0:T(8,128)(2,1)S(1)} collective-permute-done((bf16[1,64,2048]{2,1,0:T(8,128)(2,1)S(1)}, bf16[1,64,2048]{2,1,0:T(8,128)(2,1)S(1)}, u32[]{:S(2)}, u32[]{:S(2)}) %collective-permute-start.53) | collective-permute-done | bytes 262176 | tf_op jit(solution)/shard_map/ppermute | solution.py:44
  554.9 33.2 %collective-permute-done.68 = f32[1,4352]{1,0:T(1,128)S(1)} collective-permute-done((f32[1,4352]{1,0:T(1,128)S(1)}, f32[1,4352]{1,0:T(1,128)S(1)}, u32[]{:S(2)}, u32[]{:S(2)}) %collective-permute-start.68) | collective-permute-done | bytes 17440 | tf_op jit(solution)/shard_map/ppermute | solution.py:44
  591.8 12.5 %collective-permute-done.62 = bf16[2,64,2048]{2,1,0:T(8,128)(2,1)S(1)} collective-permute-done((bf16[2,64,2048]{2,1,0:T(8,128)(2,1)S(1)}, bf16[2,64,2048]{2,1,0:T(8,128)(2,1)S(1)}, u32[]{:S(2)}, u32[]{:S(2)}) %collective-permute-start.62) | collective-permute-done | bytes 524320 | tf_op jit(solution)/shard_map/ppermute | solution.py:44
  604.9 9.5 %collective-permute-done.55 = bf16[2,64,2048]{2,1,0:T(8,128)(2,1)S(1)} collective-permute-done((bf16[2,64,2048]{2,1,0:T(8,128)(2,1)S(1)}, bf16[2,64,2048]{2,1,0:T(8,128)(2,1)S(1)}, u32[]{:S(2)}, u32[]{:S(2)}) %collective-permute-start.55) | collective-permute-done | bytes 524320 | tf_op jit(solution)/shard_map/ppermute | solution.py:44
  618.1 15.0 %collective-permute-done.63 = bf16[256,2048]{1,0:T(8,128)(2,1)S(1)} collective-permute-done((bf16[256,2048]{1,0:T(8,128)(2,1)S(1)}, bf16[256,2048]{1,0:T(8,128)(2,1)S(1)}, u32[]{:S(2)}, u32[]{:S(2)}) %collective-permute-start.63) | collective-permute-done | bytes 1048608 | tf_op jit(solution)/shard_map/ppermute | solution.py:44
  633.4 22.0 %collective-permute-done.56 = bf16[256,2048]{1,0:T(8,128)(2,1)S(1)} collective-permute-done((bf16[256,2048]{1,0:T(8,128)(2,1)S(1)}, bf16[256,2048]{1,0:T(8,128)(2,1)S(1)}, u32[]{:S(2)}, u32[]{:S(2)}) %collective-permute-start.56) | collective-permute-done | bytes 1048608 | tf_op jit(solution)/shard_map/ppermute | solution.py:44
  (430 shorter events, 296.9 us)
Async XLA Ops:
  7.2 650.9 %reduce-scatter.3.cloned.1.call-start = ((), (), s32[]{:S(2)}) async-start(), calls=%async_computation.2 | async-start | bytes 7077888 | tf_op jit(solution)/shard_map/reduce_scatter | solution.py:766
  36.3 28.6 %collective-permute-start.4 = (bf16[2,512,512]{2,1,0:T(8,128)(2,1)S(1)}, bf16[2,512,512]{2,1,0:T(8,128)(2,1)S(1)}, u32[]{:S(2)}, u32[]{:S(2)}) collective-permute-start(bf16[2,512,512]{2,1,0:T(8,128)(2,1)S(1)} %pad_maximum_fusion.7.query_mine), channel_id=1, source_target_pairs={{0,8},{8,0},{1,9},{9,1},{2,10},{10,2},{3,11},{11,3},{4,12},{12,4},... | collective-permute-start | bytes 3145736 | tf_op jit(solution)/shard_map/ppermute | solution.py:44
  51.0 43.7 %collective-permute-start.17 = (bf16[512,768]{1,0:T(8,128)(2,1)}, bf16[512,768]{1,0:T(8,128)(2,1)}, u32[]{:S(2)}, u32[]{:S(2)}) collective-permute-start(bf16[512,768]{1,0:T(8,128)(2,1)} %param.23), channel_id=1, source_target_pairs={{0,1},{1,0},{2,3},{3,2},{4,5},{5,4},{6,7},{7,6},{8,9},{9,8},{10,11... | collective-permute-start | bytes 2359304 | tf_op jit(solution)/shard_map/ppermute | solution.py:44
  63.4 54.7 %collective-permute-start.21 = (bf16[2,512,768]{2,1,0:T(8,128)(2,1)}, bf16[2,512,768]{2,1,0:T(8,128)(2,1)}, u32[]{:S(2)}, u32[]{:S(2)}) collective-permute-start(bf16[2,512,768]{2,1,0:T(8,128)(2,1)} %pad_maximum_fusion.5), channel_id=1, source_target_pairs={{0,1},{1,0},{2,3},{3,2},{4,5},{5,4},{6,7},{7,6},{8,9},{9,8},{10,11... | collective-permute-start | bytes 4718600 | tf_op jit(solution)/shard_map/ppermute | solution.py:44
  98.5 42.3 %collective-permute-start.18 = (bf16[512,1536]{1,0:T(8,128)(2,1)S(1)}, bf16[512,1536]{1,0:T(8,128)(2,1)}, u32[]{:S(2)}, u32[]{:S(2)}) collective-permute-start(bf16[512,1536]{1,0:T(8,128)(2,1)S(1)} %constant_dynamic-update-slice_fusion.6), channel_id=1, source_target_pairs={{0,16},{16,0},{1,17},{17,1},{2,18},{18,2},{3,19},{19,3},{4,20},{20... | collective-permute-start | bytes 4718600 | tf_op jit(solution)/shard_map/ppermute | solution.py:39
  109.0 36.1 %collective-permute-start.24 = (bf16[2,512,768]{2,1,0:T(8,128)(2,1)S(1)}, bf16[2,512,768]{2,1,0:T(8,128)(2,1)}, u32[]{:S(2)}, u32[]{:S(2)}) collective-permute-start(bf16[2,512,768]{2,1,0:T(8,128)(2,1)S(1)} %pad_maximum_fusion.6), channel_id=1, source_target_pairs={{0,1},{1,0},{2,3},{3,2},{4,5},{5,4},{6,7},{7,6},{8,9},{9,8},{10,11... | collective-permute-start | bytes 4718600 | tf_op jit(solution)/shard_map/ppermute | solution.py:44
  120.2 78.1 %collective-permute-start.22 = (bf16[2,512,1536]{2,1,0:T(8,128)(2,1)S(1)}, bf16[2,512,1536]{2,1,0:T(8,128)(2,1)S(1)}, u32[]{:S(2)}, u32[]{:S(2)}) collective-permute-start(bf16[2,512,1536]{2,1,0:T(8,128)(2,1)S(1)} %pad_maximum_fusion.3.up_mine), channel_id=1, source_target_pairs={{0,8},{8,0},{1,9},{9,1},{2,10},{10,2},{3,11},{11,3},{4,12},{12,4},... | collective-permute-start | bytes 9437192 | tf_op jit(solution)/shard_map/ppermute | solution.py:44
  120.4 26.9 %collective-permute-start.14 = (bf16[1,64,2048]{2,1,0:T(8,128)(2,1)S(1)}, bf16[1,64,2048]{2,1,0:T(8,128)(2,1)S(1)}, u32[]{:S(2)}, u32[]{:S(2)}) collective-permute-start(bf16[1,64,2048]{2,1,0:T(8,128)(2,1)S(1)} %fusion.41), channel_id=1, source_target_pairs={{0,4},{2,6},{4,0},{6,2},{1,5},{3,7},{5,1},{7,3},{8,12},{10,14},{12... | collective-permute-start | bytes 786440 | tf_op jit(solution)/shard_map/ppermute | solution.py:44
  142.5 55.7 %collective-permute-start.19 = (bf16[2,512,1536]{2,1,0:T(8,128)(2,1)S(1)}, bf16[2,512,1536]{2,1,0:T(8,128)(2,1)S(1)}, u32[]{:S(2)}, u32[]{:S(2)}) collective-permute-start(bf16[2,512,1536]{2,1,0:T(8,128)(2,1)S(1)} %pad_maximum_fusion.2.gate_mine), channel_id=1, source_target_pairs={{0,8},{8,0},{1,9},{9,1},{2,10},{10,2},{3,11},{11,3},{4,12},{12,4},... | collective-permute-start | bytes 9437192 | tf_op jit(solution)/shard_map/ppermute | solution.py:44
  147.2 51.0 %collective-permute-start.25 = (bf16[2,512,1536]{2,1,0:T(8,128)(2,1)S(1)}, bf16[2,512,1536]{2,1,0:T(8,128)(2,1)S(1)}, u32[]{:S(2)}, u32[]{:S(2)}) collective-permute-start(bf16[2,512,1536]{2,1,0:T(8,128)(2,1)S(1)} %pad_maximum_fusion.4.down_mine), channel_id=1, source_target_pairs={{0,8},{8,0},{1,9},{9,1},{2,10},{10,2},{3,11},{11,3},{4,12},{12,4},... | collective-permute-start | bytes 9437192 | tf_op jit(solution)/shard_map/ppermute | solution.py:44
  374.7 288.2 %reduce-scatter.5.cloned.1.call-start = ((), (), s32[]{:S(2)}) async-start(), calls=%async_computation.3 | async-start | bytes 21233664 | tf_op jit(solution)/shard_map/reduce_scatter | solution.py:766
  421.1 29.1 %collective-permute-start.30 = (bf16[128,2048]{1,0:T(8,128)(2,1)S(1)}, bf16[128,2048]{1,0:T(8,128)(2,1)S(1)}, u32[]{:S(2)}, u32[]{:S(2)}) collective-permute-start(bf16[128,2048]{1,0:T(8,128)(2,1)S(1)} %copy-done.27), channel_id=1, source_target_pairs={{0,2},{2,0},{4,6},{6,4},{1,3},{3,1},{5,7},{7,5},{8,10},{10,8},{12,... | collective-permute-start | bytes 1572872 | tf_op jit(solution)/shard_map/ppermute | solution.py:44
  450.7 31.5 %collective-permute-start.47 = (bf16[1,64,2048]{2,1,0:T(8,128)(2,1)S(1)}, bf16[1,64,2048]{2,1,0:T(8,128)(2,1)S(1)}, u32[]{:S(2)}, u32[]{:S(2)}) collective-permute-start(bf16[1,64,2048]{2,1,0:T(8,128)(2,1)S(1)} %add_convert_fusion), channel_id=1, source_target_pairs={{0,4},{2,6},{4,0},{6,2},{1,5},{3,7},{5,1},{7,3},{8,12},{10,14},{12... | collective-permute-start | bytes 786440 | tf_op jit(solution)/shard_map/ppermute | solution.py:44
  471.2 36.6 %collective-permute-start.59 = (bf16[128,2048]{1,0:T(8,128)(2,1)S(1)}, bf16[128,2048]{1,0:T(8,128)(2,1)S(1)}, u32[]{:S(2)}, u32[]{:S(2)}) collective-permute-start(bf16[128,2048]{1,0:T(8,128)(2,1)S(1)} %copy-done.31), channel_id=1, source_target_pairs={{0,2},{2,0},{4,6},{6,4},{1,3},{3,1},{5,7},{7,5},{8,10},{10,8},{12,... | collective-permute-start | bytes 1572872 | tf_op jit(solution)/shard_map/ppermute | solution.py:44
  473.8 33.7 %collective-permute-start.52 = (bf16[128,2048]{1,0:T(8,128)(2,1)S(1)}, bf16[128,2048]{1,0:T(8,128)(2,1)S(1)}, u32[]{:S(2)}, u32[]{:S(2)}) collective-permute-start(bf16[128,2048]{1,0:T(8,128)(2,1)S(1)} %copy-done.33), channel_id=1, source_target_pairs={{0,2},{2,0},{4,6},{6,4},{1,3},{3,1},{5,7},{7,5},{8,10},{10,8},{12,... | collective-permute-start | bytes 1572872 | tf_op jit(solution)/shard_map/ppermute | solution.py:44
  482.4 56.8 %collective-permute-start.48 = (bf16[2,64,2048]{2,1,0:T(8,128)(2,1)S(1)}, bf16[2,64,2048]{2,1,0:T(8,128)(2,1)S(1)}, u32[]{:S(2)}, u32[]{:S(2)}) collective-permute-start(bf16[2,64,2048]{2,1,0:T(8,128)(2,1)S(1)} %maximum_select_fusion.23), channel_id=1, source_target_pairs={{0,2},{2,0},{4,6},{6,4},{1,3},{3,1},{5,7},{7,5},{8,10},{10,8},{12,... | collective-permute-start | bytes 1572872 | tf_op jit(solution)/shard_map/ppermute | solution.py:44
  488.0 63.2 %collective-permute-start.33 = (bf16[2,64,2048]{2,1,0:T(8,128)(2,1)S(1)}, bf16[2,64,2048]{2,1,0:T(8,128)(2,1)S(1)}, u32[]{:S(2)}, u32[]{:S(2)}) collective-permute-start(bf16[2,64,2048]{2,1,0:T(8,128)(2,1)S(1)} %maximum_select_fusion.17), channel_id=1, source_target_pairs={{0,2},{2,0},{4,6},{6,4},{1,3},{3,1},{5,7},{7,5},{8,10},{10,8},{12,... | collective-permute-start | bytes 1572872 | tf_op jit(solution)/shard_map/ppermute | solution.py:44
  539.5 75.5 %collective-permute-start.49 = (bf16[256,2048]{1,0:T(8,128)(2,1)S(1)}, bf16[256,2048]{1,0:T(8,128)(2,1)S(1)}, u32[]{:S(2)}, u32[]{:S(2)}) collective-permute-start(bf16[256,2048]{1,0:T(8,128)(2,1)S(1)} %bitcast.447), channel_id=1, source_target_pairs={{0,1},{1,0},{2,3},{3,2},{4,5},{5,4},{6,7},{7,6},{8,9},{9,8},{10,11... | collective-permute-start | bytes 3145736 | tf_op jit(solution)/shard_map/ppermute | solution.py:44
  549.2 40.1 %collective-permute-start.61 = (bf16[1,64,2048]{2,1,0:T(8,128)(2,1)S(1)}, bf16[1,64,2048]{2,1,0:T(8,128)(2,1)S(1)}, u32[]{:S(2)}, u32[]{:S(2)}) collective-permute-start(bf16[1,64,2048]{2,1,0:T(8,128)(2,1)S(1)} %bitcast.475), channel_id=1, source_target_pairs={{0,4},{2,6},{4,0},{6,2},{1,5},{3,7},{5,1},{7,3},{8,12},{10,14},{12... | collective-permute-start | bytes 786440 | tf_op jit(solution)/shard_map/ppermute | solution.py:44
  550.4 37.8 %collective-permute-start.68 = (f32[1,4352]{1,0:T(1,128)S(1)}, f32[1,4352]{1,0:T(1,128)S(1)}, u32[]{:S(2)}, u32[]{:S(2)}) collective-permute-start(f32[1,4352]{1,0:T(1,128)S(1)} %add.371), channel_id=1, source_target_pairs={{0,1},{1,0},{2,3},{3,2},{4,5},{5,4},{6,7},{7,6},{8,9},{9,8},{10,11... | collective-permute-start | bytes 52232 | tf_op jit(solution)/shard_map/ppermute | solution.py:44
  551.5 63.8 %collective-permute-start.34 = (bf16[256,2048]{1,0:T(8,128)(2,1)S(1)}, bf16[256,2048]{1,0:T(8,128)(2,1)S(1)}, u32[]{:S(2)}, u32[]{:S(2)}) collective-permute-start(bf16[256,2048]{1,0:T(8,128)(2,1)S(1)} %bitcast.449), channel_id=1, source_target_pairs={{0,1},{1,0},{2,3},{3,2},{4,5},{5,4},{6,7},{7,6},{8,9},{9,8},{10,11... | collective-permute-start | bytes 3145736 | tf_op jit(solution)/shard_map/ppermute | solution.py:44
  552.8 38.1 %collective-permute-start.54 = (bf16[1,64,2048]{2,1,0:T(8,128)(2,1)S(1)}, bf16[1,64,2048]{2,1,0:T(8,128)(2,1)S(1)}, u32[]{:S(2)}, u32[]{:S(2)}) collective-permute-start(bf16[1,64,2048]{2,1,0:T(8,128)(2,1)S(1)} %bitcast.471), channel_id=1, source_target_pairs={{0,4},{2,6},{4,0},{6,2},{1,5},{3,7},{5,1},{7,3},{8,12},{10,14},{12... | collective-permute-start | bytes 786440 | tf_op jit(solution)/shard_map/ppermute | solution.py:44
  604.6 28.5 %collective-permute-start.63 = (bf16[256,2048]{1,0:T(8,128)(2,1)S(1)}, bf16[256,2048]{1,0:T(8,128)(2,1)S(1)}, u32[]{:S(2)}, u32[]{:S(2)}) collective-permute-start(bf16[256,2048]{1,0:T(8,128)(2,1)S(1)} %bitcast.451), channel_id=1, source_target_pairs={{0,1},{1,0},{2,3},{3,2},{4,5},{5,4},{6,7},{7,6},{8,9},{9,8},{10,11... | collective-permute-start | bytes 3145736 | tf_op jit(solution)/shard_map/ppermute | solution.py:44
  614.7 40.7 %collective-permute-start.56 = (bf16[256,2048]{1,0:T(8,128)(2,1)S(1)}, bf16[256,2048]{1,0:T(8,128)(2,1)S(1)}, u32[]{:S(2)}, u32[]{:S(2)}) collective-permute-start(bf16[256,2048]{1,0:T(8,128)(2,1)S(1)} %bitcast.453), channel_id=1, source_target_pairs={{0,1},{1,0},{2,3},{3,2},{4,5},{5,4},{6,7},{7,6},{8,9},{9,8},{10,11... | collective-permute-start | bytes 3145736 | tf_op jit(solution)/shard_map/ppermute | solution.py:44
  (122 other events, 1589.7 us)
Sparse Core Ops, SparseCore 0:
  374.9 61.7 reduce-scatter.2
  440.7 148.5 reduce-scatter.4

commit v3 on v2

v3 whole, which is shorter than its diff:
```python
import functools

import jax
import jax.numpy as jnp
from jax import lax
from jax.experimental import pallas as pl
from jax.experimental.layout import Layout, with_layout_constraint
from jax.experimental.pallas import tpu as pltpu
from jax.sharding import Mesh
from jax.sharding import PartitionSpec as P

EPSILON = 1e-06
ROTARY_BASE = 1000000.0
BF16 = jnp.bfloat16
F32 = jnp.float32
BLOCKS = ("bo", "bi")
TENSORS = ("to", "ti")
HIDDEN_CHUNK = 768
VMEM_LIMIT = 48 * 1024 * 1024


def normed(values, gain):
    return values * lax.rsqrt(jnp.mean(values * values, axis=-1, keepdims=True) + EPSILON) * gain


def rotation_tables(positions, head_dim):
    half = head_dim // 2
    inverse = jnp.power(F32(ROTARY_BASE), -(jnp.arange(half, dtype=F32) * 2.0 / head_dim))
    angles = positions.astype(F32)[:, None] * inverse[None, :]
    cosine, sine = jnp.cos(angles), jnp.sin(angles)
    return jnp.concatenate([cosine, cosine], -1), jnp.concatenate([-sine, sine], -1)


def after(array, *earlier):
    if not earlier:
        return array
    return lax.optimization_barrier((array,) + earlier)[0]


def together(arrays, earlier):
    arrays = tuple(arrays)
    if not earlier:
        return arrays
    return tuple(lax.optimization_barrier(arrays + tuple(earlier))[: len(arrays)])


def shifted(array, axis, step):
    count = lax.axis_size(axis)
    return lax.ppermute(array, axis, [(i, (i + step) % count) for i in range(count)])


def swapped(array, axis, distance=1):
    count = lax.axis_size(axis)
    return lax.ppermute(array, axis, [(i, i ^ distance) for i in range(count)])


def pick(array, index, dimension=0):
    return lax.dynamic_index_in_dim(array, index, dimension, keepdims=False)


def paired(own, other, first, dimension):
    return jnp.where(
        first, jnp.stack([own, other], dimension), jnp.stack([other, own], dimension)
    )


def gather_axis(array, axis, dimension=0):
    count = lax.axis_size(axis)
    index = lax.axis_index(axis)
    if count == 2:
        return paired(array, swapped(array, axis), index == 0, dimension)
    shape = array.shape[:dimension] + (count,) + array.shape[dimension:]
    whole = jnp.zeros(shape, array.dtype)
    for step in range(count):
        piece = array if step == 0 else shifted(array, axis, step)
        whole = lax.dynamic_update_index_in_dim(
            whole, piece, (index + count - step) % count, dimension
        )
    return whole


class Chain:
    def __init__(self):
        self.done = []

    def swap(self, arrays, distances, before=(), during=()):
        before = tuple(a for some in before for a in some) + (self.done[-2] if len(self.done) > 1 else ())
        arrays = together(arrays, before)
        arrived = tuple(swapped(a, "to", d) for a, d in zip(arrays, distances))
        arrived = together(arrived, during)
        self.done.append(arrived)
        return arrived


def sum_rows(chain, first_kept, first_sent, second_kept, second_sent, before=(), during=()):
    count = lax.axis_size("to")
    index = lax.axis_index("to")
    rows, width = first_kept.shape
    shard = 2 * rows // count
    near, far = 1, count // 2
    while True:
        arrived = chain.swap((first_sent, second_sent), (near, far), before[:1], during)
        before, during = before[1:], ()
        first = first_kept + arrived[0].astype(F32)
        second = second_kept + arrived[1].astype(F32)
        near, far = 2 * near, far // 2
        yield
        if far < 1:
            return jnp.concatenate([first, second], axis=-1)
        bit = lax.rem(index // near, 2)
        view = first.reshape(-1, 2, shard, width)
        first_sent = pick(view, 1 - bit, 1).astype(BF16).reshape(-1, width)
        first_kept = pick(view, bit, 1).reshape(-1, width)
        bit = lax.rem(index // far, 2)
        view = second.reshape(2, -1, width)
        second_sent = pick(view, 1 - bit).astype(BF16)
        second_kept = pick(view, bit)


def gather_rows(chain, shard, before=()):
    before = tuple(before)
    count = lax.axis_size("to")
    index = lax.axis_index("to")
    rows = shard.shape[0]
    width = shard.shape[1] // 2
    first, second = shard[None, :, :width], shard[None, :, width:]
    far, near = count // 2, 1
    while far >= 1:
        arrived = chain.swap((first, second), (far, near), before[:1])
        before = before[1:]
        first = paired(first, arrived[0], lax.rem(index // far, 2) == 0, 1)
        second = paired(second, arrived[1], lax.rem(index // near, 2) == 0, 0)
        first = first.reshape(-1, rows, width)
        second = second.reshape(-1, rows, width)
        far, near = far // 2, 2 * near
        yield
    return jnp.concatenate([first.reshape(-1, width), second.reshape(-1, width)], axis=-1)


def gather_parts(chain, shard, before=()):
    rows = shard.shape[0]
    width = shard.shape[1] // 2
    first, second = shard[None, :, :width], shard[None, :, width:]
    far, near = lax.axis_size("to") // 2, 1
    while True:
        arrived = chain.swap((first, second), (far, near), before[:1])
        before = before[1:]
        far, near = far // 2, 2 * near
        yield
        if far < 1:
            return first, arrived[0], second, arrived[1]
        first = jnp.concatenate([first, arrived[0]])
        second = jnp.concatenate([second, arrived[1]])


def gather_masks(count):
    orders = []
    for distances in (lambda i: count >> (i + 1), lambda i: 1 << i):
        masks = [0]
        for i in range(count.bit_length() - 1):
            masks += [mask | distances(i) for mask in masks]
        orders.append(masks)
    return orders


def run(*stages):
    results = [None] * len(stages)
    left = dict(enumerate(stages))
    while left:
        for index in list(left):
            try:
                next(left[index])
            except StopIteration as end:
                results[index] = end.value
                del left[index]
    return results


def sum_over(vector, axes):
    for axis in axes:
        distance = 1
        while distance < lax.axis_size(axis):
            vector = vector + swapped(vector, axis, distance)
            distance *= 2
    return vector


def over_pair(array, late=()):
    return jnp.concatenate([array, after(swapped(array, "ti"), *late)], axis=-1)


def over_blocks(array, late=()):
    count = lax.axis_size("bo")
    arrived = [after(shifted(array, "bo", step), *late) for step in range(1, count)]
    return jnp.stack([array] + arrived)


def over_cores(array):
    return array, swapped(array, "bi")


LOW, HIGH, INNER, FIRST, OUTER, PLACES = 0, 1, 2, 3, 4, 5


def mxu(left, right):
    return jnp.dot(left, right, preferred_element_type=F32)


def mxu_back(left, right):
    return lax.dot_general(left, right, (((1,), (1,)), ((), ())), preferred_element_type=F32)


def mxu_outer(left, right):
    return lax.dot_general(left, right, (((0,), (0,)), ((), ())), preferred_element_type=F32)


def columns(info, position, size):
    if info is None:
        return slice(position * size, (position + 1) * size)
    return pl.ds(pl.multiple_of(info[PLACES + position] * size, 128), size)


def project(info, rows_ref, *weights):
    blocks = [(ref, i) for ref in weights for i in range(ref.shape[0])]
    total = None
    for position, (ref, i) in enumerate(blocks):
        term = mxu(rows_ref[:, columns(info, position, ref.shape[1])], ref[i])
        total = term if total is None else total + term
    return total


def project_back(grads, position, *weights):
    blocks = [(ref, i) for ref in weights for i in range(ref.shape[0])]
    ref, i = blocks[position]
    return mxu_back(grads, ref[i])


def write_halves(info, counts, total_ref, outputs):
    first_kept, first_sent, second_kept, second_sent = outputs
    rows, width = total_ref.shape
    shard, middle = rows // counts, width // 2
    for j in range(counts // 2):
        for target, bit in ((first_kept, info[LOW]), (first_sent, 1 - info[LOW])):
            source = pl.ds(pl.multiple_of((2 * j + bit) * shard, shard), shard)
            target[j, 0] = total_ref[source, :middle].astype(target.dtype)
        for target, bit in ((second_kept, info[HIGH]), (second_sent, 1 - info[HIGH])):
            source = pl.ds(pl.multiple_of((bit * (counts // 2) + j) * shard, shard), shard)
            target[j, 0] = total_ref[source, middle:].astype(target.dtype)


def read_parts(info, counts, parts, target):
    rows, width = target.shape
    shard, middle = rows // counts, width // 2
    for side, masks in enumerate(gather_masks(counts)):
        for i, mask in enumerate(masks):
            ref = parts[2 * side + 2 * i // counts]
            place = pl.multiple_of(jnp.bitwise_xor(info[OUTER], mask) * shard, shard)
            columns_now = slice(side * middle, (side + 1) * middle)
            target[pl.ds(place, shard), columns_now] = ref[i % (counts // 2), 0]


def unit(values):
    return lax.rsqrt(jnp.mean(values * values, axis=-1, keepdims=True) + EPSILON)


def swap_halves(values):
    return pltpu.roll(values, values.shape[-1] // 2, 1)


def prepare_kernel(
    sizes,
    info,
    x_ref,
    gain_ref,
    query_gain_ref,
    key_gain_ref,
    cosine_ref,
    sine_ref,
    query_mine,
    query_theirs,
    kv_mine,
    kv_theirs,
    normal_ref,
    query_raw_ref,
    key_raw_ref,
    query_ref,
    kv_ref,
):
    head_dim, pair_heads, key_heads = sizes
    x = x_ref[0].astype(F32)
    normal_ref, query_raw_ref, key_raw_ref, query_ref, kv_ref = (
        ref.at[0] for ref in (normal_ref, query_raw_ref, key_raw_ref, query_ref, kv_ref)
    )
    normal_ref[...] = (x * unit(x) * gain_ref[...]).astype(BF16)
    cosine, sine = cosine_ref[...], sine_ref[...]

    def rotated(raw, gain):
        values = raw * unit(raw) * gain
        return (values * cosine + swap_halves(values) * sine).astype(BF16)

    query_raw = project(info, normal_ref, query_mine, query_theirs)
    query_raw_ref[...] = query_raw
    for head in range(query_raw.shape[1] // head_dim):
        part = slice(head * head_dim, (head + 1) * head_dim)
        query_ref[:, part] = rotated(query_raw[:, part], query_gain_ref[...])
    kv_raw = project(info, normal_ref, kv_mine, kv_theirs)
    for head in range(pair_heads):
        start = (2 * key_heads * (head // key_heads) + head % key_heads) * head_dim
        raw = kv_raw[:, start : start + head_dim]
        key_raw_ref[:, head * head_dim : (head + 1) * head_dim] = raw
        kv_ref[0, head] = rotated(raw, key_gain_ref[...])
        start += key_heads * head_dim
        kv_ref[1, head] = kv_raw[:, start : start + head_dim].astype(BF16)


def visible_scores(info, queries, keys, position, blocks, rows, scale):
    scores = mxu_back(queries, keys) * scale
    if position == 0:
        query_rows = lax.broadcasted_iota(jnp.int32, scores.shape, 0) % rows
        key_rows = lax.broadcasted_iota(jnp.int32, scores.shape, 1)
        return jnp.where(key_rows <= query_rows, scores, -jnp.inf)
    return jnp.where(info[PLACES + blocks + position] > 0, scores, -jnp.inf)


def attend_kernel(
    sizes,
    info,
    query_ref,
    kv_mine,
    kv_theirs,
    out_mine,
    out_theirs,
    attn_ref,
    log_ref,
    attended_ref,
    first_kept,
    first_sent,
    second_kept,
    second_sent,
    scores_ref,
    total_ref,
):
    head_dim, pair_heads, group, counts = sizes
    query_ref, attn_ref, log_ref, attended_ref = (
        ref.at[0] for ref in (query_ref, attn_ref, log_ref, attended_ref)
    )
    rows = query_ref.shape[0]
    half = kv_mine.shape[0]
    scale = head_dim ** (-0.5)
    lanes = lax.broadcasted_iota(jnp.int32, (rows, head_dim), 1)
    logs = jnp.zeros((rows, head_dim), F32)

    def key_value(which, position, head):
        ref = kv_mine if position < half else kv_theirs
        return ref[position % half, 0, which, head]

    for head in range(pair_heads):
        queries = jnp.concatenate(
            [
                query_ref[:, (head * group + i) * head_dim : (head * group + i + 1) * head_dim]
                for i in range(group)
            ]
        )
        top = None
        for position in range(2 * half):
            scores = visible_scores(
                info, queries, key_value(0, position, head), position, 2 * half, rows, scale
            )
            scores_ref[position] = scores
            block_top = jnp.max(scores, axis=-1, keepdims=True)
            top = block_top if top is None else jnp.maximum(top, block_top)
        total = jnp.zeros_like(top)
        weighted = jnp.zeros((group * rows, head_dim), F32)
        for position in range(2 * half):
            weights = jnp.exp(scores_ref[position] - top)
            total += jnp.sum(weights, axis=-1, keepdims=True)
            weighted += mxu(weights.astype(BF16), key_value(1, position, head))
        attn = weighted / total
        log_total = top + jnp.log(total)
        for i in range(group):
            index = head * group + i
            part = slice(index * head_dim, (index + 1) * head_dim)
            piece = attn[i * rows : (i + 1) * rows]
            attn_ref[:, part] = piece
            attended_ref[:, part] = piece.astype(BF16)
            logs = jnp.where(lanes == index, log_total[i * rows : (i + 1) * rows], logs)
    log_ref[...] = logs
    attended = attended_ref[...]
    for position in range(2 * half):
        total_ref[:, columns(info, position, out_mine.shape[1])] = project_back(
            attended, position, out_mine, out_theirs
        )
    write_halves(info, counts, total_ref, (first_kept, first_sent, second_kept, second_sent))


def feed_forward_kernel(
    counts,
    info,
    first_own,
    first_other,
    second_own,
    second_other,
    grad_ref,
    gate_ref,
    up_ref,
    down_ref,
    active_ref,
    grad_gate_ref,
    grad_up_ref,
    mid_ref,
    *outputs,
):
    grad_total, mlp_total = outputs[8:]
    step = pl.program_id(0)

    @pl.when(step == 0)
    def _():
        read_parts(info, counts, (first_own, first_other, second_own, second_other), mid_ref)

    blocks, size = gate_ref.shape[0], gate_ref.shape[1]
    gate = project(None, mid_ref, gate_ref)
    up = project(None, mid_ref, up_ref)
    grad = project(None, grad_ref.at[0], down_ref)
    slope = jax.nn.sigmoid(gate)
    silu = gate * slope
    active = (silu * up).astype(BF16)
    grad_gate = (grad * up * slope * (1.0 + gate * (1.0 - slope))).astype(BF16)
    grad_up = (grad * silu).astype(BF16)
    active_ref[...] = active
    grad_gate_ref[...] = grad_gate
    grad_up_ref[...] = grad_up

    def term(position):
        part = columns(None, position, size)
        grad_term = project_back(grad_gate, position, gate_ref) + project_back(
            grad_up, position, up_ref
        )
        return part, grad_term, project_back(active, position, down_ref)

    @pl.when(step == 0)
    def _():
        for position in range(blocks):
            part, grad_term, mlp_term = term(position)
            grad_total[:, part] = grad_term
            mlp_total[:, part] = mlp_term

    @pl.when(step > 0)
    def _():
        for position in range(blocks):
            part, grad_term, mlp_term = term(position)
            grad_total[:, part] += grad_term
            mlp_total[:, part] += mlp_term

    @pl.when(step == pl.num_programs(0) - 1)
    def _():
        write_halves(info, counts, grad_total, outputs[:4])
        write_halves(info, counts, mlp_total, outputs[4:8])


def attend_back_kernel(
    sizes,
    info,
    first_own,
    first_other,
    second_own,
    second_other,
    out_mine,
    out_theirs,
    query_ref,
    kv_mine,
    kv_theirs,
    attn_ref,
    log_ref,
    branch_ref,
    grad_query_ref,
    kept_ref,
    sent_ref,
):
    head_dim, pair_heads, group, counts = sizes
    query_ref, attn_ref, log_ref, branch_ref, grad_query_ref = (
        ref.at[0] for ref in (query_ref, attn_ref, log_ref, branch_ref, grad_query_ref)
    )
    read_parts(info, counts, (first_own, first_other, second_own, second_other), branch_ref)
    rows = query_ref.shape[0]
    half = kv_mine.shape[0]
    scale = head_dim ** (-0.5)
    grad_attended = project(info, branch_ref, out_mine, out_theirs).astype(BF16)

    def key_value(which, position, head):
        ref = kv_mine if position < half else kv_theirs
        return ref[position % half, 0, which, head]

    for head in range(pair_heads):
        parts = [
            slice((head * group + i) * head_dim, (head * group + i + 1) * head_dim)
            for i in range(group)
        ]
        queries = jnp.concatenate([query_ref[:, part] for part in parts])
        grads = jnp.concatenate([grad_attended[:, part] for part in parts])
        attn = jnp.concatenate([attn_ref[:, part] for part in parts])
        logs = jnp.concatenate(
            [log_ref[:, head * group + i : head * group + i + 1] for i in range(group)]
        )
        row_dots = jnp.sum(grads.astype(F32) * attn, axis=-1, keepdims=True)
        grad_query = jnp.zeros((group * rows, head_dim), F32)
        for position in range(2 * half):
            keys = key_value(0, position, head)
            scores = visible_scores(info, queries, keys, position, 2 * half, rows, scale)
            probs = jnp.exp(scores - logs)
            grad_probs = mxu_back(grads, key_value(1, position, head))
            grad_scores = (probs * (grad_probs - row_dots) * scale).astype(BF16)
            grad_query += mxu(grad_scores, keys)
            target = kept_ref if position < half else sent_ref
            target[position % half, 0, 0, head] = mxu_outer(grad_scores, queries).astype(target.dtype)
            target[position % half, 0, 1, head] = mxu_outer(probs.astype(BF16), grads).astype(
                target.dtype
            )
        for i, part in enumerate(parts):
            grad_query_ref[:, part] = grad_query[i * rows : (i + 1) * rows]


def finish_kernel(
    sizes,
    info,
    grad_query_ref,
    query_raw_ref,
    key_raw_ref,
    shares_ref,
    query_gain_ref,
    key_gain_ref,
    cosine_ref,
    sine_ref,
    query_mine,
    query_theirs,
    kv_mine,
    kv_theirs,
    query_low_ref,
    kv_low_ref,
    gains_ref,
    first_kept,
    first_sent,
    second_kept,
    second_sent,
    total_ref,
):
    head_dim, pair_heads, key_heads, counts = sizes
    grad_query_ref, query_raw_ref, key_raw_ref, shares_ref, query_low_ref, kv_low_ref, gains_ref = (
        ref.at[0]
        for ref in (
            grad_query_ref,
            query_raw_ref,
            key_raw_ref,
            shares_ref,
            query_low_ref,
            kv_low_ref,
            gains_ref,
        )
    )
    cosine, sine = cosine_ref[...], sine_ref[...]

    def back(grad, raw, gain):
        grad = grad * cosine - swap_halves(grad) * sine
        scale = unit(raw)
        gain_term = jnp.sum(grad * raw * scale, axis=0, keepdims=True)
        inner = grad * gain
        mean = jnp.mean(inner * raw, axis=-1, keepdims=True)
        return (scale * inner - raw * (scale * scale * scale * mean)).astype(BF16), gain_term

    total = jnp.zeros((1, head_dim), F32)
    for head in range(query_raw_ref.shape[1] // head_dim):
        part = slice(head * head_dim, (head + 1) * head_dim)
        query_low_ref[:, part], term = back(
            grad_query_ref[:, part], query_raw_ref[:, part], query_gain_ref[...]
        )
        total += term
    gains_ref[0:1, :] = total
    total = jnp.zeros((1, head_dim), F32)
    for head in range(pair_heads):
        start = (2 * key_heads * (head // key_heads) + head % key_heads) * head_dim
        kv_low_ref[:, start : start + head_dim], term = back(
            shares_ref[0, head],
            key_raw_ref[:, head * head_dim : (head + 1) * head_dim],
            key_gain_ref[...],
        )
        total += term
        start += key_heads * head_dim
        kv_low_ref[:, start : start + head_dim] = shares_ref[1, head].astype(BF16)
    gains_ref[1:2, :] = total
    query_low, kv_low = query_low_ref[...], kv_low_ref[...]
    for position in range(2 * query_mine.shape[0]):
        total_ref[:, columns(info, position, query_mine.shape[1])] = project_back(
            query_low, position, query_mine, query_theirs
        ) + project_back(kv_low, position, kv_mine, kv_theirs)
    write_halves(info, counts, total_ref, (first_kept, first_sent, second_kept, second_sent))


def weight_kernel(counts, products, info, *refs):
    arrays, start = [], 0
    for count in counts:
        arrays.append(refs[start : start + count])
        start += count
    out_ref = refs[-1]

    def rows_of(members):
        flat = [ref[...].reshape(-1, ref.shape[-1]) for ref in members]
        return flat[0] if len(flat) == 1 else jnp.concatenate(flat)

    place = 0
    for left, rights in products:
        left_rows = rows_of(arrays[left])
        for right in rights:
            total = mxu_outer(left_rows, rows_of(arrays[right])).astype(BF16)
            if len(out_ref.shape) == 5:
                out_ref[0, 0, place] = total
                place += 1
            else:
                out_ref[0, 0, :, place : place + total.shape[1]] = total
                place += total.shape[1]


def whole_spec(dims):
    return pl.BlockSpec(dims, lambda i, info: (0,) * len(dims))


def group_spec(array, dimension=0):
    dims = array.shape[:dimension] + (1,) + array.shape[dimension + 1 :]
    rest = len(dims) - dimension - 1
    return pl.BlockSpec(dims, lambda g, info: (0,) * dimension + (g,) + (0,) * rest)


def group_call(kernel, groups, info, operands, outputs, scratch=(), flops=0):
    moved = sum(a.size * a.dtype.itemsize for a, _ in tuple(operands) + tuple(outputs))
    return pl.pallas_call(
        kernel,
        out_shape=[a for a, _ in outputs],
        grid_spec=pltpu.PrefetchScalarGridSpec(
            num_scalar_prefetch=1,
            grid=(groups,),
            in_specs=[spec for _, spec in operands],
            out_specs=[spec for _, spec in outputs],
            scratch_shapes=list(scratch),
        ),
        compiler_params=pltpu.CompilerParams(vmem_limit_bytes=VMEM_LIMIT),
        cost_estimate=pl.CostEstimate(flops=flops, bytes_accessed=moved, transcendentals=0),
    )(info, *[a for a, _ in operands])


def shape(dims, dtype):
    return jax.ShapeDtypeStruct(dims, dtype)


def weight_blocks(info, lefts, rights, products, blocks, pair, stacked, in_order):
    width = lefts[0][0].shape[-1]
    size = width // blocks
    batch_rows = sum(a.shape[0] for a in lefts[0]) if lefts[0][0].ndim == 2 else None
    operands, specs = [], []
    for array in [a for members in lefts for a in members]:
        operands.append(array)
        if array.ndim == 2:
            spec = pl.BlockSpec((array.shape[0], size), lambda t, b, info: (0, b))
        elif array.shape[0] * array.shape[1] == batch_rows or batch_rows is None:
            spec = pl.BlockSpec(array.shape[:2] + (size,), lambda t, b, info: (0, 0, b))
        else:
            spec = pl.BlockSpec(
                (array.shape[0] // pair, array.shape[1], size),
                lambda t, b, info: (info[INNER], 0, b),
            )
        specs.append(spec)
    widths = []
    for members in rights:
        widths.append(members[0].shape[-1] // pair)
        for array in members:
            operands.append(array)
            dims = array.shape[:-1] + (array.shape[-1] // pair,)
            zeros = (0,) * (array.ndim - 1)
            specs.append(
                pl.BlockSpec(
                    dims,
                    lambda t, b, info, zeros=zeros: zeros
                    + (t if in_order else lax.rem(t + info[INNER], 2),),
                )
            )
    if stacked:
        dims = (pair, blocks, len(rights), size, widths[0])
        out_spec = pl.BlockSpec((1, 1) + dims[2:], lambda t, b, info: (t, b, 0, 0, 0))
    else:
        dims = (pair, blocks, size, sum(widths))
        out_spec = pl.BlockSpec((1, 1) + dims[2:], lambda t, b, info: (t, b, 0, 0))
    counts = [len(members) for members in tuple(lefts) + tuple(rights)]
    placed = [(left, [len(lefts) + right for right in columns_of]) for left, columns_of in products]
    rows = rights[0][0].size * len(rights[0]) // rights[0][0].shape[-1]
    flops = 2 * rows * width * pair * sum(widths)
    moved = 2 * pair * width * sum(widths)
    return pl.pallas_call(
        functools.partial(weight_kernel, counts, placed),
        out_shape=shape(dims, BF16),
        grid_spec=pltpu.PrefetchScalarGridSpec(
            num_scalar_prefetch=1,
            grid=(pair, blocks),
            in_specs=specs,
            out_specs=out_spec,
        ),
        compiler_params=pltpu.CompilerParams(vmem_limit_bytes=VMEM_LIMIT),
        cost_estimate=pl.CostEstimate(flops=flops, bytes_accessed=moved, transcendentals=0),
    )(info, *operands)


def local(
    hidden_in,
    out_grad,
    norm_in,
    w_query,
    key_weight,
    value_weight,
    w_out,
    query_gain,
    key_gain,
    norm_mid,
    w_gate,
    w_up,
    w_down,
):
    block_outers = lax.axis_size("bo")
    blocks = block_outers * lax.axis_size("bi")
    block_outer = lax.axis_index("bo")
    block_inner = lax.axis_index("bi")
    block = block_outer * lax.axis_size("bi") + block_inner
    outer = lax.axis_index("to")
    inner = lax.axis_index("ti")
    pair = lax.axis_size("ti")
    counts = lax.axis_size("to")
    batch, rows, width = hidden_in.shape
    head_dim = query_gain.shape[0] * blocks
    query_width = w_query.shape[1]
    key_width = key_weight.shape[1]
    hidden_units = w_gate.shape[1]
    key_heads = key_width // head_dim
    query_heads = query_width * pair // head_dim
    pair_heads = key_heads * pair
    group_size = query_heads // pair_heads
    shard_rows = rows // counts

    query_half = over_pair(w_query)
    kv_half = over_blocks(jnp.concatenate([key_weight, value_weight], axis=1))
    query_most = over_blocks(query_half)
    kv_most = over_pair(kv_half)
    query_full = over_cores(query_most)
    kv_full = over_cores(kv_most)
    out_half = over_blocks(after(w_out.T, query_half))
    mlp_own = jnp.concatenate([w_gate, w_up, w_down.T], axis=1)
    mlp_own = with_layout_constraint(after(mlp_own, query_most, kv_most), Layout((0, 1)))
    mlp_weights = lax.all_gather(mlp_own, ("ti", "bo", "bi"), axis=0)

    own_gains = jnp.concatenate([norm_in, norm_mid, query_gain, key_gain])[None]
    own_gains = after(own_gains, kv_half)
    all_gains = gather_axis(gather_axis(own_gains, "bo"), "bi", 1)
    all_gains = all_gains.reshape(blocks, -1).astype(F32)
    part = norm_in.shape[0]
    gain_in = all_gains[:, :part].reshape(-1)
    gain_mid = all_gains[:, part : 2 * part].reshape(-1)
    head_part = query_gain.shape[0]
    gain_query = all_gains[:, 2 * part : 2 * part + head_part].reshape(1, -1)
    gain_key = all_gains[:, 2 * part + head_part :].reshape(1, -1)

    positions = block * rows + jnp.arange(rows, dtype=jnp.int32)
    cosine, sine = rotation_tables(positions, head_dim)
    block_ids = []
    for side in range(2):
        side_inner = block_inner if side == 0 else 1 - block_inner
        for step in range(block_outers):
            owner = lax.rem(block_outer + block_outers - step, block_outers)
            block_ids.append(owner * 2 + side_inner)
    groups = batch // pair
    first_sequence = inner * groups
    info = jnp.stack(
        [lax.rem(outer, 2), outer // (counts // 2), inner, first_sequence, outer]
        + block_ids
        + [(b < block).astype(jnp.int32) for b in block_ids]
    ).astype(jnp.int32)

    chain = Chain()
    all_heads = query_heads * head_dim
    all_keys = pair_heads * head_dim
    kv_dims = (groups, 2, pair_heads, rows, head_dim)
    side_dims = (block_outers,) + kv_dims
    half_dims = (counts // 2, groups, shard_rows, width // 2)
    whole_rows = pltpu.VMEM((rows, width), F32)

    def by_group(dims, dtype, dimension=0):
        array = shape(dims, dtype)
        return array, group_spec(array, dimension)

    def per_group(*arrays):
        return tuple((a, group_spec(a)) for a in arrays)

    def per_second(*arrays):
        return tuple((a, group_spec(a, 1)) for a in arrays)

    def shared(*arrays):
        return tuple((a, whole_spec(a.shape)) for a in arrays)

    halves = (by_group(half_dims, F32, 1), by_group(half_dims, BF16, 1)) * 2

    def flat(parts):
        return [part.reshape(-1, part.shape[-1]) for part in parts]

    def own_sequences(array):
        return (array, pl.BlockSpec((1, rows, width), lambda g, info: (info[FIRST] + g, 0, 0)))

    normal_in, query_raw, key_raw, query_rows, kv_rows = group_call(
        functools.partial(prepare_kernel, (head_dim, pair_heads, key_heads)),
        groups,
        info,
        (own_sequences(hidden_in),)
        + shared(after(gain_in[None], out_half), gain_query, gain_key, cosine, sine)
        + shared(*query_full, *kv_full),
        (
            by_group((groups, rows, width), BF16),
            by_group((groups, rows, all_heads), F32),
            by_group((groups, rows, all_keys), F32),
            by_group((groups, rows, all_heads), BF16),
            by_group(kv_dims, BF16),
        ),
        flops=2 * groups * rows * width * (all_heads + 2 * all_keys),
    )
    kv_blocks = over_blocks(kv_rows)
    key_value = over_cores(kv_blocks)
    out_full = over_cores(over_pair(out_half, (kv_blocks,)))
    attn, log_total, attended, *out_parts = group_call(
        functools.partial(attend_kernel, (head_dim, pair_heads, group_size, counts)),
        groups,
        info,
        per_group(query_rows) + per_second(*key_value) + shared(*out_full),
        (
            by_group((groups, rows, all_heads), F32),
            by_group((groups, rows, head_dim), F32),
            by_group((groups, rows, all_heads), BF16),
        )
        + halves,
        scratch=[pltpu.VMEM((blocks, group_size * rows, rows), F32), whole_rows],
        flops=2 * groups * rows * all_heads * (width + 4 * blocks * rows),
    )

    def own_shard(array):
        starts = (first_sequence, outer * shard_rows, 0)
        part = lax.dynamic_slice(array, starts, (groups, shard_rows, width))
        return part.reshape(-1, width).astype(F32)

    x_shard = own_shard(hidden_in)
    grad_out_shard = own_shard(out_grad)
    residual = x_shard + run(sum_rows(chain, *flat(out_parts)))[0]
    normal_mid = normed(residual, gain_mid).astype(BF16).reshape(groups, shard_rows, width)
    mid_parts = []
    for group in range(groups):
        mid_parts += run(gather_parts(chain, normal_mid[group]))

    chunks = pair * hidden_units // HIDDEN_CHUNK
    steps = hidden_units // HIDDEN_CHUNK
    weight_dims = (blocks, width // blocks, HIDDEN_CHUNK)

    def weight_spec(place):
        return pl.BlockSpec(
            weight_dims, lambda i, info: (i // steps, 0, place * steps + lax.rem(i, steps))
        )

    piece = pl.BlockSpec((rows, HIDDEN_CHUNK), lambda i, info: (0, i))
    hidden_shape = shape((rows, pair * hidden_units), BF16)
    one_dims = (counts // 2, 1, shard_rows, width // 2)
    one_halves = (shape(one_dims, F32), shape(one_dims, BF16)) * 4
    mid, active, grad_gate, grad_up, grad_parts, mlp_parts = [], [], [], [], [], []
    for group in range(groups):
        parts = [part.reshape(one_dims) for part in mid_parts[group]]
        sequence = pl.BlockSpec(
            (1, rows, width), lambda i, info, group=group: (info[FIRST] + group, 0, 0)
        )
        results = pl.pallas_call(
            functools.partial(feed_forward_kernel, counts),
            out_shape=(hidden_shape,) * 3 + (shape((rows, width), BF16),) + one_halves,
            grid_spec=pltpu.PrefetchScalarGridSpec(
                num_scalar_prefetch=1,
                grid=(chunks,),
                in_specs=[whole_spec(one_dims)] * 4 + [sequence] + [weight_spec(i) for i in range(3)],
                out_specs=(piece,) * 3 + (whole_spec((rows, width)),) + (whole_spec(one_dims),) * 8,
                scratch_shapes=[whole_rows] * 2,
            ),
            compiler_params=pltpu.CompilerParams(vmem_limit_bytes=VMEM_LIMIT),
            cost_estimate=pl.CostEstimate(
                flops=12 * rows * width * pair * hidden_units,
                bytes_accessed=6 * width * pair * hidden_units,
                transcendentals=rows * pair * hidden_units,
            ),
        )(info, *parts, out_grad, mlp_weights, mlp_weights, mlp_weights)
        active.append(results[0])
        grad_gate.append(results[1])
        grad_up.append(results[2])
        mid.append(results[3])
        grad_parts.append(results[4:8])
        mlp_parts.append(results[8:])

    grad_normal_mid, mlp_sums = [], []
    first_arrived = ()
    for group in range(groups - 1):
        stages = [
            sum_rows(chain, *flat(parts[group]), during=(active[-1],))
            for parts in (grad_parts, mlp_parts)
        ]
        mark = len(chain.done)
        grad_sum, mlp_sum = run(*stages)
        first_arrived = chain.done[mark]
        grad_normal_mid.append(grad_sum)
        mlp_sums.append(mlp_sum)
    mlp_terms = weight_blocks(
        after(info, *first_arrived),
        (mid, [out_grad]),
        (grad_gate, grad_up, active),
        [(0, [0, 1]), (1, [2])],
        blocks,
        pair,
        True,
        True,
    )
    grad_normal_mid += run(sum_rows(chain, *flat(grad_parts[-1]), during=(mlp_terms,)))
    _, pull_mid = jax.vjp(normed, residual, gain_mid)
    grad_norm, gain_mid_term = pull_mid(jnp.concatenate(grad_normal_mid))
    grad_residual = grad_out_shard + grad_norm
    (branch_parts,) = run(gather_parts(chain, grad_residual.astype(BF16)))
    branch_first = chain.done[-2][0]
    branch_parts = [part.reshape(half_dims) for part in branch_parts]
    branch, grad_query, kv_kept, kv_sent = group_call(
        functools.partial(attend_back_kernel, (head_dim, pair_heads, group_size, counts)),
        groups,
        info,
        per_second(*branch_parts)
        + shared(*out_full)
        + per_group(query_rows)
        + per_second(*key_value)
        + per_group(attn, log_total),
        (
            by_group((groups, rows, width), BF16),
            by_group((groups, rows, all_heads), F32),
            by_group(side_dims, F32, 1),
            by_group(side_dims, BF16, 1),
        ),
        flops=2 * groups * rows * all_heads * (width + 10 * blocks * rows),
    )

    def layer_rows(group, mlp_sum):
        part = jnp.split(lax.optimization_barrier(residual), groups)[group]
        return (part + mlp_sum).astype(BF16)

    layer_first = [layer_rows(group, mlp_sums[group]) for group in range(groups - 1)]
    stages = [sum_rows(chain, *flat(mlp_parts[-1]), before=((grad_query,),))]
    stages += [gather_rows(chain, shard, ((grad_query,),)) for shard in layer_first]
    mlp_sum, *layer_whole = run(*stages)
    layer_last = layer_rows(groups - 1, mlp_sum)
    layer_both = [gather_axis(whole, "ti") for whole in layer_whole]
    done_before = tuple(a for done in chain.done[-len(stages) :] for a in done)

    mine = kv_kept + swapped(kv_sent, "bi").astype(F32)
    low = mine.astype(BF16)
    shares = mine[0]
    for step in range(1, block_outers):
        shares += shifted(low[step], "bo", block_outers - step).astype(F32)
    grad_query_low, grad_kv_low, gain_terms, *in_parts = group_call(
        functools.partial(finish_kernel, (head_dim, pair_heads, key_heads, counts)),
        groups,
        info,
        per_group(grad_query, query_raw, key_raw, shares)
        + shared(gain_query, gain_key, cosine, sine, *query_full, *kv_full),
        (
            by_group((groups, rows, all_heads), BF16),
            by_group((groups, rows, 2 * all_keys), BF16),
            by_group((groups, 2, head_dim), F32),
        )
        + halves,
        scratch=[whole_rows],
        flops=2 * groups * rows * width * (all_heads + 2 * all_keys),
    )
    attn_terms = weight_blocks(
        info,
        ([normal_in], [branch]),
        ([grad_query_low], [grad_kv_low], [attended]),
        [(0, [0, 1]), (1, [2])],
        blocks,
        pair,
        False,
        False,
    )

    in_parts = flat(in_parts)
    (grad_normal_in,) = run(
        sum_rows(
            chain, *in_parts, before=(done_before, tuple(layer_both)), during=(attn_terms,)
        )
    )
    _, pull_first = jax.vjp(normed, x_shard, gain_in)
    grad_norm, gain_in_term = pull_first(grad_normal_in)
    hidden_shard = (grad_residual + grad_norm).astype(BF16).reshape(groups, shard_rows, width)

    def weight_sum(terms):
        flat = terms.reshape((-1,) + terms.shape[-1:])
        raw = lax.psum_scatter(flat, ("ti", "bo", "bi"), scatter_dimension=0, tiled=True)
        share = with_layout_constraint(raw, Layout((0, 1)))
        return share.astype(F32).reshape(terms.shape[2:]), raw

    share_mlp, mlp_raw = weight_sum(after(mlp_terms, branch_first))
    share_attn, _ = weight_sum(after(attn_terms, mlp_raw))
    vectors = jnp.concatenate([gain_in_term, gain_mid_term, gain_terms.sum(0).reshape(-1)])
    vectors = sum_over(vectors[None], ("ti",))
    hidden_pairs = [
        gather_axis(hidden_shard[group], "ti").reshape(-1, width)
        for group in range(groups // 2, groups)
    ]
    first = (tuple(hidden_pairs) + (vectors,),)
    stages = [gather_rows(chain, layer_last)]
    stages += [gather_rows(chain, hidden_shard[group], first) for group in range(groups // 2)]
    layer_whole, *hidden_whole = run(*stages)
    layer_both.append(gather_axis(layer_whole, "ti"))
    hidden_both = [gather_axis(whole, "ti") for whole in hidden_whole]
    for both in hidden_pairs:
        (whole,) = run(gather_rows(chain, both))
        whole = whole.reshape(counts, pair, shard_rows, width)
        hidden_both.append(whole.transpose(1, 0, 2, 3).reshape(pair, rows, width))
    vectors = sum_over(vectors, BLOCKS + ("to",))[0]

    def vector_share(first, size):
        return lax.dynamic_slice_in_dim(vectors, first + block * (size // blocks), size // blocks)

    kv_start = query_width + 2 * key_width
    return (
        jnp.stack(layer_both, axis=1).reshape(batch, rows, width),
        jnp.stack(hidden_both, axis=1).reshape(batch, rows, width),
        vector_share(0, width),
        share_attn[:, :query_width],
        share_attn[:, query_width : query_width + key_width],
        share_attn[:, query_width + key_width : kv_start],
        share_attn[:, kv_start:].T,
        vector_share(2 * width, head_dim),
        vector_share(2 * width + head_dim, head_dim),
        vector_share(width, width),
        share_mlp[0],
        share_mlp[1],
        share_mlp[2].T,
    )


def solution(mesh):
    block_count, tensor_count = mesh.devices.shape
    split = Mesh(
        mesh.devices.reshape(block_count // 2, 2, tensor_count // 2, 2), BLOCKS + TENSORS
    )
    row_weight = P(BLOCKS, TENSORS)
    column_weight = P(TENSORS, BLOCKS)
    tokens = P(None, BLOCKS, None)
    vector = P(BLOCKS)
    weights = (
        vector,
        row_weight,
        row_weight,
        row_weight,
        column_weight,
        vector,
        vector,
        vector,
        row_weight,
        row_weight,
        column_weight,
    )
    return jax.shard_map(
        local,
        mesh=split,
        in_specs=(tokens, tokens) + weights,
        out_specs=(tokens, tokens) + weights,
        check_vma=False,
    )
```

time: 691 us -> 551 us (0.80)
  waiting for transfers between devices: 366 us -> 255 us
  local copies, waits for them, and re-layouts: 94.3 us -> 39 us
  other arithmetic: 38.2 us -> 52.1 us
  starting transfers between devices: 68.4 us -> 80.7 us
    ppermute x59 -> x71, waiting for transfers between devices: 326 us -> 204 us  [swapped(): return lax.ppermute(array, axis, [(i, i ^ distance) for i in range(count)])]
    reshape x2 -> x0, local copies, waits for them, and re-layouts: 31.6 us -> none  [weight_sum(): flat = terms.reshape((-1,) + terms.shape[-1:])]
    ppermute x59 -> x71, starting transfers between devices: 58.6 us -> 74.5 us  [swapped(): return lax.ppermute(array, axis, [(i, i ^ distance) for i in range(count)])]
    unnamed x165 -> x168, local copies, waits for them, and re-layouts: 37.7 us -> 24.2 us
    ppermute x10 -> x5, waiting for transfers between devices: 39.2 us -> 51.1 us  [shifted(): lax.ppermute(array, axis, [(i, (i + step) % count) for i in range(count)])]
    select_n x30, other arithmetic: 4.07 us -> 11.7 us  [paired(): jnp.where(first, jnp.stack([own, other], dimension), jnp.stack([other, ow...]
    another operation x10 -> x9, other arithmetic: 15.2 us -> 9.14 us  [the longest x4 2.38 us: over_blocks(): return jnp.stack([array] + arrived)]
    pallas_call x10 -> x6, Pallas kernels: 65.5 us -> 64 us  [the longest x4 39.8 us: group_call(): pl.pallas_call(kernel, out_shape=[a for a, _ in outputs], grid_spec=pltpu...]
  transfers between devices with their start and end apart: 71 -> 79, of which waited for: 40 -> 51; matrix products, arithmetic and copies ran while one was open for 13% -> 12% of each run, Pallas kernels for 9% -> 18%
where the time goes in v3:
time: 551 us; the launch traced here: 543 us
  waiting for transfers between devices  255 us (46%)
  Pallas kernels  100 us (18%)
  starting transfers between devices  80.7 us (15%)
  other arithmetic  52.1 us (9%)
  local copies, waits for them, and re-layouts  39 us (7%)
  between operations  16 us (3%)
    ppermute x71, waiting for transfers between devices, swapped(): return lax.ppermute(array, axis, [(i, i ^ distance) for i in range(count)])  204 us
    ppermute x71, starting transfers between devices, swapped(): return lax.ppermute(array, axis, [(i, i ^ distance) for i in range(count)])  74.5 us
    ppermute x5, waiting for transfers between devices, shifted(): lax.ppermute(array, axis, [(i, (i + step) % count) for i in range(count)])  51.1 us
    pallas_call x4, Pallas kernels, group_call(): pl.pallas_call(kernel, out_shape=[a for a, _ in outputs], grid_spec=pltpu...  39.8 us
    pallas_call x2, Pallas kernels, local(): pl.pallas_call(functools.partial(feed_forward_kernel, counts), out_shape=...  36.1 us
    unnamed x168, local copies, waits for them, and re-layouts  24.2 us
    pallas_call x2, Pallas kernels, weight_blocks(): pl.pallas_call(functools.partial(weight_kernel, counts, placed), out_shap...  24.2 us
    select_n x30, other arithmetic, paired(): jnp.where(first, jnp.stack([own, other], dimension), jnp.stack([other, ow...  11.7 us
  transfers between devices with their start and end apart: 79, of which 51 were waited for; matrix products, arithmetic and copies ran while one was open for 12% of the time, Pallas kernels for 18%

profile of v3, /device:TPU:0, one launch (start us, length us, event | category | flops | bytes accessed | tf_op | source)
XLA Modules:
  0.0 542.5 jit_solution(3944924916942270035)
XLA Ops:
  22.9 8.5 %collective-permute-done.5 = bf16[512,512]{1,0:T(8,128)(2,1)} collective-permute-done((bf16[512,512]{1,0:T(8,128)(2,1)S(1)}, bf16[512,512]{1,0:T(8,128)(2,1)}, u32[]{:S(2)}, u32[]{:S(2)}) %collective-permute-start.5) | collective-permute-done | bytes 524320 | tf_op jit(solution)/shard_map/ppermute | solution.py:49
  45.8 6.9 %shard_map.228 = (bf16[2,256,2048]{2,1,0:T(8,128)(2,1)}, f32[2,256,512]{2,1,0:T(8,128)S(1)}, f32[2,256,256]{2,1,0:T(8,128)S(1)}, bf16[2,256,512]{2,1,0:T(8,128)(2,1)S(1)}, bf16[2,2,2,256,128]{4,3,2,1,0:T(8,128)(2,1)S(1)}) custom-call(s32[13]{0:T(128)S(1)} %stack.410.info, bf16[4,256,2048]{2,1,0:T(8,128)(2,1)} %x_ref.1, f32[1,2048]{1,0:T(1,128)S(1)} %bitcast.306, ...), custom_call_target="tpu_custom_call" | custom-call | flops 2147483648 | bytes 13378560 | tf_op jit(solution)/shard_map/pallas_call | solution.py:633
  53.9 24.0 %collective-permute-done.9 = bf16[2,2,2,256,128]{4,3,2,1,0:T(8,128)(2,1)S(1)} collective-permute-done((bf16[2,2,2,256,128]{4,3,2,1,0:T(8,128)(2,1)S(1)}, bf16[2,2,2,256,128]{4,3,2,1,0:T(8,128)(2,1)S(1)}, u32[]{:S(2)}, u32[]{:S(2)}) %collective-permute-start.9) | collective-permute-done | bytes 524320 | tf_op jit(solution)/shard_map/ppermute | solution.py:49
  85.3 8.7 %shard_map.229 = (f32[2,256,512]{2,1,0:T(8,128)S(1)}, f32[2,256,128]{2,1,0:T(8,128)S(1)}, bf16[2,256,512]{2,1,0:T(8,128)(2,1)S(1)}, f32[2,2,64,1024]{3,2,1,0:T(8...) custom-call(s32[13]{0:T(128)S(1)} %stack.410.info, ...), custom_call_target="tpu_custom_call" | custom-call | flops 3221225472 | bytes 9699328 | tf_op jit(solution)/shard_map/pallas_call | solution.py:633
  100.6 21.2 %collective-permute-done.13 = bf16[256,1024]{1,0:T(8,128)(2,1)S(1)} collective-permute-done((bf16[256,1024]{1,0:T(8,128)(2,1)}, bf16[256,1024]{1,0:T(8,128)(2,1)S(1)}, u32[]{:S(2)}, u32[]{:S(2)}) %collective-permute-start.13) | collective-permute-done | bytes 524320 | tf_op jit(solution)/shard_map/ppermute | solution.py:54
  128.9 10.0 %collective-permute-done.14 = bf16[128,1024]{1,0:T(8,128)(2,1)} collective-permute-done((bf16[128,1024]{1,0:T(8,128)(2,1)}, bf16[128,1024]{1,0:T(8,128)(2,1)}, u32[]{:S(2)}, u32[]{:S(2)}) %collective-permute-start.14) | collective-permute-done | bytes 262176 | tf_op jit(solution)/shard_map/ppermute | solution.py:54
  147.3 6.0 %collective-permute-done.17 = bf16[1,64,1024]{2,1,0:T(8,128)(2,1)S(1)} collective-permute-done((bf16[1,64,1024]{2,1,0:T(8,128)(2,1)S(1)}, bf16[1,64,1024]{2,1,0:T(8,128)(2,1)S(1)}, u32[]{:S(2)}, u32[]{:S(2)}) %collective-permute-start.17) | collective-permute-done | bytes 131104 | tf_op jit(solution)/shard_map/ppermute | solution.py:54
  160.4 8.5 %collective-permute-done.22 = bf16[1,64,1024]{2,1,0:T(8,128)(2,1)S(1)} collective-permute-done((bf16[1,64,1024]{2,1,0:T(8,128)(2,1)S(1)}, bf16[1,64,1024]{2,1,0:T(8,128)(2,1)S(1)}, u32[]{:S(2)}, u32[]{:S(2)}) %collective-permute-start.22) | collective-permute-done | bytes 131104 | tf_op jit(solution)/shard_map/ppermute | solution.py:54
  175.6 18.2 %shard_map.230 = (bf16[256,1536]{1,0:T(8,128)(2,1)S(1)}, bf16[256,1536]{1,0:T(8,128)(2,1)S(1)}, bf16[256,1536]{1,0:T(8,128)(2,1)}, bf16[256,2048]{1,0:T(8,128)(2...) custom-call(s32[13]{0:T(128)S(1)} %stack.410.info, ...), custom_call_target="tpu_custom_call" | custom-call | flops 9663676416 | bytes 18874368 | tf_op jit(solution)/shard_map/pallas_call | solution.py:876
  198.7 17.9 %shard_map.231 = (bf16[256,1536]{1,0:T(8,128)(2,1)S(1)}, bf16[256,1536]{1,0:T(8,128)(2,1)S(1)}, bf16[256,1536]{1,0:T(8,128)(2,1)}, bf16[256,2048]{1,0:T(8,128)(2...) custom-call(s32[13]{0:T(128)S(1)} %stack.410.info, ...), custom_call_target="tpu_custom_call" | custom-call | flops 9663676416 | bytes 18874368 | tf_op jit(solution)/shard_map/pallas_call | solution.py:876
  230.1 15.9 %shard_map.232 = bf16[2,4,3,512,768]{4,3,2,1,0:T(8,128)(2,1)} custom-call(s32[13]{0:T(128)S(1)} %stack.410.info, bf16[256,2048]{1,0:T(8,128)(2,1)S(1)} %copy-done.20, bf16[256,2048]{1,0:T(8,128)(2,1)} %get-tuple-element.171.refs_1_, bf16[4,256,2048]{2,1,0:T(8,128)(2,1)} %refs_2_.1, bf16[256,1536]{1,0:T(8,128)(2,1)S(1)} %get-tuple-element.172.refs_3_, ...), custom_call_target="tpu_custom_call" | custom-call | flops 9663676416 | bytes 18874368 | tf_op jit(solution)/shard_map/pallas_call | solution.py:694
  258.9 9.3 %collective-permute-done.37 = bf16[1,128,1024]{2,1,0:T(8,128)(2,1)S(1)} collective-permute-done((bf16[1,128,1024]{2,1,0:T(8,128)(2,1)S(1)}, bf16[1,128,1024]{2,1,0:T(8,128)(2,1)S(1)}, u32[]{:S(2)}, u32[]{:S(2)}) %collective-permute-start.37) | collective-permute-done | bytes 262176 | tf_op jit(solution)/shard_map/ppermute | solution.py:54
  270.2 13.1 %collective-permute-done.38 = bf16[1,128,1024]{2,1,0:T(8,128)(2,1)S(1)} collective-permute-done((bf16[1,128,1024]{2,1,0:T(8,128)(2,1)S(1)}, bf16[1,128,1024]{2,1,0:T(8,128)(2,1)S(1)}, u32[]{:S(2)}, u32[]{:S(2)}) %collective-permute-start.38) | collective-permute-done | bytes 262176 | tf_op jit(solution)/shard_map/ppermute | solution.py:54
  285.8 11.2 %collective-permute-done.39 = bf16[2,128,1024]{2,1,0:T(8,128)(2,1)S(1)} collective-permute-done((bf16[2,128,1024]{2,1,0:T(8,128)(2,1)S(1)}, bf16[2,128,1024]{2,1,0:T(8,128)(2,1)S(1)}, u32[]{:S(2)}, u32[]{:S(2)}) %collective-permute-start.39) | collective-permute-done | bytes 524320 | tf_op jit(solution)/shard_map/ppermute | solution.py:54
  299.3 13.0 %shard_map.233 = (bf16[2,256,2048]{2,1,0:T(8,128)(2,1)}, f32[2,256,512]{2,1,0:T(8,128)S(1)}, f32[2,2,2,2,256,128]{5,4,3,2,1,0:T(8,128)}, bf16[2,2,2,2,256,128]{5,4,3,2,1,0:T(8,128)(2,1)}) custom-call(s32[13]{0:T(128)S(1)} %stack.410.info, bf16[2,2,64,1024]{3,2,1,0:T(8,128)(2,1)S(1)} %pad_maximum_fusion.13.first_own, bf16[2,2,64,1024]{3,2,1,0:T(8,128)(2,1)S(1)} %bitcast.307, ...), custom_call_target="tpu_custom_call" | custom-call | flops 6442450944 | bytes 14417920 | tf_op jit(solution)/shard_map/pallas_call | solution.py:633
  314.8 6.6 %collective-permute-done.47 = bf16[128,1024]{1,0:T(8,128)(2,1)S(1)} collective-permute-done((bf16[128,1024]{1,0:T(8,128)(2,1)S(1)}, bf16[128,1024]{1,0:T(8,128)(2,1)S(1)}, u32[]{:S(2)}, u32[]{:S(2)}) %collective-permute-start.47) | collective-permute-done | bytes 262176 | tf_op jit(solution)/shard_map/ppermute | solution.py:54
  343.7 8.9 %collective-permute-done.43 = bf16[2,64,1024]{2,1,0:T(8,128)(2,1)} collective-permute-done((bf16[2,64,1024]{2,1,0:T(8,128)(2,1)}, bf16[2,64,1024]{2,1,0:T(8,128)(2,1)}, u32[]{:S(2)}, u32[]{:S(2)}) %collective-permute-start.43) | collective-permute-done | bytes 262176 | tf_op jit(solution)/shard_map/ppermute | solution.py:54
  363.4 14.1 %collective-permute-done.51 = bf16[2,2,2,256,128]{4,3,2,1,0:T(8,128)(2,1)} collective-permute-done((bf16[2,2,2,256,128]{4,3,2,1,0:T(8,128)(2,1)}, bf16[2,2,2,256,128]{4,3,2,1,0:T(8,128)(2,1)}, u32[]{:S(2)}, u32[]{:S(2)}) %collective-permute-start.51) | collective-permute-done | bytes 524320 | tf_op jit(solution)/shard_map/ppermute | solution.py:49
  380.7 11.3 %shard_map.234 = (bf16[2,256,512]{2,1,0:T(8,128)(2,1)S(1)}, bf16[2,256,512]{2,1,0:T(8,128)(2,1)S(1)}, f32[2,2,128]{2,1,0:T(2,128)S(1)}, f32[2,2,64,1024]{3,2,1,0...) custom-call(s32[13]{0:T(128)S(1)} %stack.410.info, ...), custom_call_target="tpu_custom_call" | custom-call | flops 2147483648 | bytes 12323840 | tf_op jit(solution)/shard_map/pallas_call | solution.py:633
  400.9 8.2 %shard_map.235 = bf16[2,4,512,768]{3,2,1,0:T(8,128)(2,1)} custom-call(s32[13]{0:T(128)S(1)} %stack.410.info, bf16[2,256,2048]{2,1,0:T(8,128)(2,1)S(1)} %copy-done.3, bf16[2,256,2048]{2,1,0:T(8,128)(2,1)S(1)} %copy-done.4, bf16[2,256,512]{2,1,0:T(8,128)(2,1)S(1)} %copy-done.17, bf16[2,256,512]{2,1,0:T(8,128)(2,1)S(1)} %copy-done.19, ...), custom_call_target="tpu_custom_call" | custom-call | flops 3221225472 | bytes 6291456 | tf_op jit(solution)/shard_map/pallas_call | solution.py:694
  423.2 7.9 %collective-permute-done.54 = bf16[1,64,1024]{2,1,0:T(8,128)(2,1)S(1)} collective-permute-done((bf16[1,64,1024]{2,1,0:T(8,128)(2,1)S(1)}, bf16[1,64,1024]{2,1,0:T(8,128)(2,1)S(1)}, u32[]{:S(2)}, u32[]{:S(2)}) %collective-permute-start.54) | collective-permute-done | bytes 131104 | tf_op jit(solution)/shard_map/ppermute | solution.py:54
  478.2 5.8 %collective-permute-done.68 = bf16[1,128,1024]{2,1,0:T(8,128)(2,1)S(1)} collective-permute-done((bf16[1,128,1024]{2,1,0:T(8,128)(2,1)S(1)}, bf16[1,128,1024]{2,1,0:T(8,128)(2,1)S(1)}, u32[]{:S(2)}, u32[]{:S(2)}) %collective-permute-start.68) | collective-permute-done | bytes 262176 | tf_op jit(solution)/shard_map/ppermute | solution.py:54
  484.2 5.4 collective-permute-done.69
  498.6 18.3 %collective-permute-done.70 = bf16[2,128,1024]{2,1,0:T(8,128)(2,1)S(1)} collective-permute-done((bf16[2,128,1024]{2,1,0:T(8,128)(2,1)S(1)}, bf16[2,128,1024]{2,1,0:T(8,128)(2,1)S(1)}, u32[]{:S(2)}, u32[]{:S(2)}) %collective-permute-start.70) | collective-permute-done | bytes 524320 | tf_op jit(solution)/shard_map/ppermute | solution.py:54
  (464 shorter events, 247.8 us)
Async XLA Ops:
  7.2 168.4 %all-gather.3.cloned.1.call-start = ((), (), s32[]{:S(2)}) async-start(), calls=%async_computation.4 | async-start | bytes 21233664 | tf_op jit(solution)/shard_map/all_gather | solution.py:752
  34.1 377.8 %reduce-scatter.3.cloned.1.call-start = ((), (), s32[]{:S(2)}) async-start(), calls=%async_computation.2 | async-start | bytes 21233664 | tf_op jit(solution)/shard_map/reduce_scatter | solution.py:1002
  52.7 25.1 %collective-permute-start.9 = (bf16[2,2,2,256,128]{4,3,2,1,0:T(8,128)(2,1)S(1)}, bf16[2,2,2,256,128]{4,3,2,1,0:T(8,128)(2,1)S(1)}, u32[]{:S(2)}, u32[]{:S(2)}) collective-permute-start(bf16[2,2,2,256,128]{4,3,2,1,0:T(8,128)(2,1)S(1)} %get-tuple-element.128), channel_id=1, source_target_pairs={{0,16},{16,0},{1,17},{17,1},{2,18},{18,2},{3,19},{19,3},{4,20},{20... | collective-permute-start | bytes 1572872 | tf_op jit(solution)/shard_map/ppermute | solution.py:49
  53.9 25.1 %collective-permute-start.11 = (bf16[2,512,256]{2,1,0:T(8,128)(2,1)S(1)}, bf16[2,512,256]{2,1,0:T(8,128)(2,1)S(1)}, u32[]{:S(2)}, u32[]{:S(2)}) collective-permute-start(bf16[2,512,256]{2,1,0:T(8,128)(2,1)S(1)} %pad_maximum_fusion.12), channel_id=1, source_target_pairs={{0,1},{1,0},{2,3},{3,2},{4,5},{5,4},{6,7},{7,6},{8,9},{9,8},{10,11... | collective-permute-start | bytes 1572872 | tf_op jit(solution)/shard_map/ppermute | solution.py:54
  96.6 25.3 %collective-permute-start.13 = (bf16[256,1024]{1,0:T(8,128)(2,1)}, bf16[256,1024]{1,0:T(8,128)(2,1)S(1)}, u32[]{:S(2)}, u32[]{:S(2)}) collective-permute-start(bf16[256,1024]{1,0:T(8,128)(2,1)} %bitcast.29), channel_id=1, source_target_pairs={{0,2},{2,0},{4,6},{6,4},{1,3},{3,1},{5,7},{7,5},{8,10},{10,8},{12,... | collective-permute-start | bytes 1572872 | tf_op jit(solution)/shard_map/ppermute | solution.py:54
  98.1 27.2 %collective-permute-start.15 = (bf16[256,1024]{1,0:T(8,128)(2,1)}, bf16[256,1024]{1,0:T(8,128)(2,1)}, u32[]{:S(2)}, u32[]{:S(2)}) collective-permute-start(bf16[256,1024]{1,0:T(8,128)(2,1)} %bitcast.34), channel_id=1, source_target_pairs={{0,4},{2,6},{4,0},{6,2},{1,5},{3,7},{5,1},{7,3},{8,12},{10,14},{12... | collective-permute-start | bytes 1572872 | tf_op jit(solution)/shard_map/ppermute | solution.py:54
  173.4 23.1 %collective-permute-start.23 = (bf16[2,64,1024]{2,1,0:T(8,128)(2,1)S(1)}, bf16[2,64,1024]{2,1,0:T(8,128)(2,1)S(1)}, u32[]{:S(2)}, u32[]{:S(2)}) collective-permute-start(bf16[2,64,1024]{2,1,0:T(8,128)(2,1)S(1)} %get-tuple-element.144), channel_id=1, source_target_pairs={{0,2},{2,0},{4,6},{6,4},{1,3},{3,1},{5,7},{7,5},{8,10},{10,8},{12,... | collective-permute-start | bytes 786440 | tf_op jit(solution)/shard_map/ppermute | solution.py:54
  173.7 22.8 %collective-permute-start.24 = (bf16[2,64,1024]{2,1,0:T(8,128)(2,1)S(1)}, bf16[2,64,1024]{2,1,0:T(8,128)(2,1)S(1)}, u32[]{:S(2)}, u32[]{:S(2)}) collective-permute-start(bf16[2,64,1024]{2,1,0:T(8,128)(2,1)S(1)} %get-tuple-element.145), channel_id=1, source_target_pairs={{0,4},{2,6},{4,0},{6,2},{1,5},{3,7},{5,1},{7,3},{8,12},{10,14},{12... | collective-permute-start | bytes 786440 | tf_op jit(solution)/shard_map/ppermute | solution.py:54
  193.7 22.9 %collective-permute-start.29 = (bf16[128,1024]{1,0:T(8,128)(2,1)S(1)}, bf16[128,1024]{1,0:T(8,128)(2,1)S(1)}, u32[]{:S(2)}, u32[]{:S(2)}) collective-permute-start(bf16[128,1024]{1,0:T(8,128)(2,1)S(1)} %bitcast.316), channel_id=1, source_target_pairs={{0,2},{2,0},{4,6},{6,4},{1,3},{3,1},{5,7},{7,5},{8,10},{10,8},{12,... | collective-permute-start | bytes 786440 | tf_op jit(solution)/shard_map/ppermute | solution.py:54
  194.1 22.6 %collective-permute-start.30 = (bf16[128,1024]{1,0:T(8,128)(2,1)S(1)}, bf16[128,1024]{1,0:T(8,128)(2,1)S(1)}, u32[]{:S(2)}, u32[]{:S(2)}) collective-permute-start(bf16[128,1024]{1,0:T(8,128)(2,1)S(1)} %bitcast.315), channel_id=1, source_target_pairs={{0,4},{2,6},{4,0},{6,2},{1,5},{3,7},{5,1},{7,3},{8,12},{10,14},{12... | collective-permute-start | bytes 786440 | tf_op jit(solution)/shard_map/ppermute | solution.py:54
  196.5 23.2 %collective-permute-start.25 = (bf16[128,1024]{1,0:T(8,128)(2,1)S(1)}, bf16[128,1024]{1,0:T(8,128)(2,1)S(1)}, u32[]{:S(2)}, u32[]{:S(2)}) collective-permute-start(bf16[128,1024]{1,0:T(8,128)(2,1)S(1)} %bitcast.314), channel_id=1, source_target_pairs={{0,2},{2,0},{4,6},{6,4},{1,3},{3,1},{5,7},{7,5},{8,10},{10,8},{12,... | collective-permute-start | bytes 786440 | tf_op jit(solution)/shard_map/ppermute | solution.py:54
  196.8 23.6 %collective-permute-start.26 = (bf16[128,1024]{1,0:T(8,128)(2,1)S(1)}, bf16[128,1024]{1,0:T(8,128)(2,1)S(1)}, u32[]{:S(2)}, u32[]{:S(2)}) collective-permute-start(bf16[128,1024]{1,0:T(8,128)(2,1)S(1)} %bitcast.313), channel_id=1, source_target_pairs={{0,4},{2,6},{4,0},{6,2},{1,5},{3,7},{5,1},{7,3},{8,12},{10,14},{12... | collective-permute-start | bytes 786440 | tf_op jit(solution)/shard_map/ppermute | solution.py:54
  220.7 25.6 %collective-permute-start.27 = (bf16[64,1024]{1,0:T(8,128)(2,1)S(1)}, bf16[64,1024]{1,0:T(8,128)(2,1)S(1)}, u32[]{:S(2)}, u32[]{:S(2)}) collective-permute-start(bf16[64,1024]{1,0:T(8,128)(2,1)S(1)} %fusion.17), channel_id=1, source_target_pairs={{0,4},{2,6},{4,0},{6,2},{1,5},{3,7},{5,1},{7,3},{8,12},{10,14},{12... | collective-permute-start | bytes 393224 | tf_op jit(solution)/shard_map/ppermute | solution.py:54
  220.8 25.6 %collective-permute-start.28 = (bf16[64,1024]{1,0:T(8,128)(2,1)S(1)}, bf16[64,1024]{1,0:T(8,128)(2,1)S(1)}, u32[]{:S(2)}, u32[]{:S(2)}) collective-permute-start(bf16[64,1024]{1,0:T(8,128)(2,1)S(1)} %fusion.18), channel_id=1, source_target_pairs={{0,2},{2,0},{4,6},{6,4},{1,3},{3,1},{5,7},{7,5},{8,10},{10,8},{12,... | collective-permute-start | bytes 393224 | tf_op jit(solution)/shard_map/ppermute | solution.py:54
  268.2 263.3 %reduce-scatter.5.cloned.1.call-start = ((), (), s32[]{:S(2)}) async-start(), calls=%async_computation.3 | async-start | bytes 7077888 | tf_op jit(solution)/shard_map/reduce_scatter | solution.py:1002
  322.3 32.8 %collective-permute-start.50 = (bf16[2,2,2,2,256,128]{5,4,3,2,1,0:T(8,128)(2,1)}, bf16[2,2,2,2,256,128]{5,4,3,2,1,0:T(8,128)(2,1)S(1)}, u32[]{:S(2)}, u32[]{:S(2)}) collective-permute-start(bf16[2,2,2,2,256,128]{5,4,3,2,1,0:T(8,128)(2,1)} %get-tuple-element.204), channel_id=1, source_target_pairs={{0,8},{8,0},{1,9},{9,1},{2,10},{10,2},{3,11},{11,3},{4,12},{12,4},... | collective-permute-start | bytes 3145736 | tf_op jit(solution)/shard_map/ppermute | solution.py:54
  361.1 48.1 %collective-permute-start.45 = (bf16[256,2048]{1,0:T(8,128)(2,1)}, bf16[256,2048]{1,0:T(8,128)(2,1)}, u32[]{:S(2)}, u32[]{:S(2)}) collective-permute-start(bf16[256,2048]{1,0:T(8,128)(2,1)} %get-tuple-element.286), channel_id=1, source_target_pairs={{0,1},{1,0},{2,3},{3,2},{4,5},{5,4},{6,7},{7,6},{8,9},{9,8},{10,11... | collective-permute-start | bytes 3145736 | tf_op jit(solution)/shard_map/ppermute | solution.py:54
  431.9 29.0 %collective-permute-start.56 = (bf16[2,64,1024]{2,1,0:T(8,128)(2,1)}, bf16[2,64,1024]{2,1,0:T(8,128)(2,1)}, u32[]{:S(2)}, u32[]{:S(2)}) collective-permute-start(bf16[2,64,1024]{2,1,0:T(8,128)(2,1)} %maximum_select_fusion.21), channel_id=1, source_target_pairs={{0,2},{2,0},{4,6},{6,4},{1,3},{3,1},{5,7},{7,5},{8,10},{10,8},{12,... | collective-permute-start | bytes 786440 | tf_op jit(solution)/shard_map/ppermute | solution.py:54
  431.9 30.2 %collective-permute-start.57 = (bf16[2,64,1024]{2,1,0:T(8,128)(2,1)}, bf16[2,64,1024]{2,1,0:T(8,128)(2,1)}, u32[]{:S(2)}, u32[]{:S(2)}) collective-permute-start(bf16[2,64,1024]{2,1,0:T(8,128)(2,1)} %maximum_select_fusion.22), channel_id=1, source_target_pairs={{0,4},{2,6},{4,0},{6,2},{1,5},{3,7},{5,1},{7,3},{8,12},{10,14},{12... | collective-permute-start | bytes 786440 | tf_op jit(solution)/shard_map/ppermute | solution.py:54
  463.5 56.0 %collective-permute-start.58 = (bf16[256,2048]{1,0:T(8,128)(2,1)S(1)}, bf16[256,2048]{1,0:T(8,128)(2,1)S(1)}, u32[]{:S(2)}, u32[]{:S(2)}) collective-permute-start(bf16[256,2048]{1,0:T(8,128)(2,1)S(1)} %get-tuple-element.288), channel_id=1, source_target_pairs={{0,1},{1,0},{2,3},{3,2},{4,5},{5,4},{6,7},{7,6},{8,9},{9,8},{10,11... | collective-permute-start | bytes 3145736 | tf_op jit(solution)/shard_map/ppermute | solution.py:54
  468.9 20.7 %collective-permute-start.69 = (bf16[1,128,1024]{2,1,0:T(8,128)(2,1)S(1)}, bf16[1,128,1024]{2,1,0:T(8,128)(2,1)S(1)}, u32[]{:S(2)}, u32[]{:S(2)}) collective-permute-start(bf16[1,128,1024]{2,1,0:T(8,128)(2,1)S(1)} %get-tuple-element.230), channel_id=1, source_target_pairs={{0,2},{2,0},{4,6},{6,4},{1,3},{3,1},{5,7},{7,5},{8,10},{10,8},{12,... | collective-permute-start | bytes 786440 | tf_op jit(solution)/shard_map/ppermute | solution.py:54
  494.2 22.8 %collective-permute-start.70 = (bf16[2,128,1024]{2,1,0:T(8,128)(2,1)S(1)}, bf16[2,128,1024]{2,1,0:T(8,128)(2,1)S(1)}, u32[]{:S(2)}, u32[]{:S(2)}) collective-permute-start(bf16[2,128,1024]{2,1,0:T(8,128)(2,1)S(1)} %maximum_select_fusion.13), channel_id=1, source_target_pairs={{0,2},{2,0},{4,6},{6,4},{1,3},{3,1},{5,7},{7,5},{8,10},{10,8},{12,... | collective-permute-start | bytes 1572872 | tf_op jit(solution)/shard_map/ppermute | solution.py:54
  495.8 23.2 %collective-permute-start.71 = (bf16[2,128,1024]{2,1,0:T(8,128)(2,1)S(1)}, bf16[2,128,1024]{2,1,0:T(8,128)(2,1)S(1)}, u32[]{:S(2)}, u32[]{:S(2)}) collective-permute-start(bf16[2,128,1024]{2,1,0:T(8,128)(2,1)S(1)} %maximum_select_fusion.14), channel_id=1, source_target_pairs={{0,4},{2,6},{4,0},{6,2},{1,5},{3,7},{5,1},{7,3},{8,12},{10,14},{12... | collective-permute-start | bytes 1572872 | tf_op jit(solution)/shard_map/ppermute | solution.py:54
  497.2 25.0 %collective-permute-start.67 = (bf16[256,2048]{1,0:T(8,128)(2,1)S(1)}, bf16[256,2048]{1,0:T(8,128)(2,1)S(1)}, u32[]{:S(2)}, u32[]{:S(2)}) collective-permute-start(bf16[256,2048]{1,0:T(8,128)(2,1)S(1)} %get-tuple-element.284), channel_id=1, source_target_pairs={{0,1},{1,0},{2,3},{3,2},{4,5},{5,4},{6,7},{7,6},{8,9},{9,8},{10,11... | collective-permute-start | bytes 3145736 | tf_op jit(solution)/shard_map/ppermute | solution.py:54
  (134 other events, 1238.3 us)
Sparse Core Ops, SparseCore 0:
  34.2 110.2 all-gather.2
  268.3 141.7 reduce-scatter.2
  413.6 68.2 reduce-scatter.4

commit v4 on v3

--- a/solution.py
+++ b/solution.py
@@ -87,7 +87,7 @@
         before = tuple(a for some in before for a in some) + (self.done[-2] if len(self.done) > 1 else ())
         arrays = together(arrays, before)
         arrived = tuple(swapped(a, "to", d) for a, d in zip(arrays, distances))
-        arrived = together(arrived, during)
+        arrived = together(arrived, tuple(a for some in during for a in some))
         self.done.append(arrived)
         return arrived
 
@@ -99,14 +99,14 @@
     shard = 2 * rows // count
     near, far = 1, count // 2
     while True:
-        arrived = chain.swap((first_sent, second_sent), (near, far), before[:1], during)
-        before, during = before[1:], ()
-        first = first_kept + arrived[0].astype(F32)
-        second = second_kept + arrived[1].astype(F32)
+        arrived = chain.swap((first_sent, second_sent), (near, far), before[:1], during[:1])
+        before, during = before[1:], during[1:]
         near, far = 2 * near, far // 2
         yield
         if far < 1:
-            return jnp.concatenate([first, second], axis=-1)
+            return first_kept, arrived[0], second_kept, arrived[1]
+        first = first_kept + arrived[0].astype(F32)
+        second = second_kept + arrived[1].astype(F32)
         bit = lax.rem(index // near, 2)
         view = first.reshape(-1, 2, shard, width)
         first_sent = pick(view, 1 - bit, 1).astype(BF16).reshape(-1, width)
@@ -117,7 +117,7 @@
         second_kept = pick(view, bit)
 
 
-def gather_rows(chain, shard, before=()):
+def gather_rows(chain, shard, before=(), during=(), vector=None):
     before = tuple(before)
     count = lax.axis_size("to")
     index = lax.axis_index("to")
@@ -126,21 +126,25 @@
     first, second = shard[None, :, :width], shard[None, :, width:]
     far, near = count // 2, 1
     while far >= 1:
-        arrived = chain.swap((first, second), (far, near), before[:1])
-        before = before[1:]
+        arrays, distances = (first, second), (far, near)
+        if vector is not None:
+            arrays, distances = arrays + (vector,), distances + (near,)
+        arrived = chain.swap(arrays, distances, before[:1], during[:1])
+        before, during = before[1:], during[1:]
+        if vector is not None:
+            vector = vector + arrived[2]
         first = paired(first, arrived[0], lax.rem(index // far, 2) == 0, 1)
         second = paired(second, arrived[1], lax.rem(index // near, 2) == 0, 0)
         first = first.reshape(-1, rows, width)
         second = second.reshape(-1, rows, width)
         far, near = far // 2, 2 * near
         yield
-    return jnp.concatenate([first.reshape(-1, width), second.reshape(-1, width)], axis=-1)
-
-
-def gather_parts(chain, shard, before=()):
-    rows = shard.shape[0]
-    width = shard.shape[1] // 2
-    first, second = shard[None, :, :width], shard[None, :, width:]
+    whole = jnp.concatenate([first.reshape(-1, width), second.reshape(-1, width)], axis=-1)
+    return whole if vector is None else (whole, vector)
+
+
+def gather_parts(chain, first, second, before=()):
+    first, second = first[None], second[None]
     far, near = lax.axis_size("to") // 2, 1
     while True:
         arrived = chain.swap((first, second), (far, near), before[:1])
@@ -235,17 +239,17 @@
     return mxu_back(grads, ref[i])
 
 
-def write_halves(info, counts, total_ref, outputs):
+def write_halves(info, counts, total_ref, outputs, place=0):
     first_kept, first_sent, second_kept, second_sent = outputs
     rows, width = total_ref.shape
     shard, middle = rows // counts, width // 2
     for j in range(counts // 2):
         for target, bit in ((first_kept, info[LOW]), (first_sent, 1 - info[LOW])):
             source = pl.ds(pl.multiple_of((2 * j + bit) * shard, shard), shard)
-            target[j, 0] = total_ref[source, :middle].astype(target.dtype)
+            target[j, place] = total_ref[source, :middle].astype(target.dtype)
         for target, bit in ((second_kept, info[HIGH]), (second_sent, 1 - info[HIGH])):
             source = pl.ds(pl.multiple_of((bit * (counts // 2) + j) * shard, shard), shard)
-            target[j, 0] = total_ref[source, middle:].astype(target.dtype)
+            target[j, place] = total_ref[source, middle:].astype(target.dtype)
 
 
 def read_parts(info, counts, parts, target):
@@ -311,6 +315,57 @@
         kv_ref[0, head] = rotated(raw, key_gain_ref[...])
         start += key_heads * head_dim
         kv_ref[1, head] = kv_raw[:, start : start + head_dim].astype(BF16)
+
+
+def row_sums(parts):
+    first_kept, first_arrived, second_kept, second_arrived = (ref[...] for ref in parts)
+    return jnp.concatenate(
+        [first_kept + first_arrived.astype(F32), second_kept + second_arrived.astype(F32)], axis=-1
+    )
+
+
+def norm_back(grad, values, gain):
+    scale = unit(values)
+    inner = grad * gain
+    mean = jnp.mean(inner * values, axis=-1, keepdims=True)
+    term = jnp.sum(grad * values * scale, axis=0, keepdims=True)
+    return scale * inner - values * (scale * scale * scale * mean), term
+
+
+def residual_kernel(x_ref, gain_ref, *refs):
+    residual_ref, first_ref, second_ref = refs[4:]
+    residual = x_ref[...].astype(F32) + row_sums(refs[:4])
+    residual_ref[...] = residual
+    normal = (residual * unit(residual) * gain_ref[...]).astype(BF16)
+    middle = normal.shape[1] // 2
+    first_ref[...] = normal[:, :middle]
+    second_ref[...] = normal[:, middle:]
+
+
+def residual_back_kernel(groups, residual_ref, grad_out_ref, gain_ref, *refs):
+    layer_ref, grad_ref, first_ref, second_ref, term_ref = refs[4 * groups :]
+    shard = residual_ref.shape[0] // groups
+    middle = residual_ref.shape[1] // 2
+    total = jnp.zeros(term_ref.shape, F32)
+    for group in range(groups):
+        place = slice(group * shard, (group + 1) * shard)
+        sums = row_sums(refs[4 * group : 4 * group + 4])
+        residual = residual_ref[place, :]
+        layer_ref[place, :] = (residual + sums[shard:]).astype(BF16)
+        grad, term = norm_back(sums[:shard], residual, gain_ref[...])
+        grad += grad_out_ref[place, :].astype(F32)
+        total += term
+        grad_ref[place, :] = grad
+        first_ref[place, :] = grad[:, :middle].astype(BF16)
+        second_ref[place, :] = grad[:, middle:].astype(BF16)
+    term_ref[...] = total
+
+
+def hidden_kernel(x_ref, gain_ref, grad_residual_ref, *refs):
+    hidden_ref, term_ref = refs[4:]
+    grad, term = norm_back(row_sums(refs[:4]), x_ref[...].astype(F32), gain_ref[...])
+    hidden_ref[...] = (grad_residual_ref[...] + grad).astype(BF16)
+    term_ref[...] = term
 
 
 def visible_scores(info, queries, keys, position, blocks, rows, scale):
@@ -410,7 +465,7 @@
     mid_ref,
     *outputs,
 ):
-    grad_total, mlp_total = outputs[8:]
+    grad_total, mlp_total = outputs[4:]
     step = pl.program_id(0)
 
     @pl.when(step == 0)
@@ -453,8 +508,8 @@
 
     @pl.when(step == pl.num_programs(0) - 1)
     def _():
-        write_halves(info, counts, grad_total, outputs[:4])
-        write_halves(info, counts, mlp_total, outputs[4:8])
+        write_halves(info, counts, grad_total, outputs[:4], 0)
+        write_halves(info, counts, mlp_total, outputs[:4], 1)
 
 
 def attend_back_kernel(
@@ -626,6 +681,16 @@
     dims = array.shape[:dimension] + (1,) + array.shape[dimension + 1 :]
     rest = len(dims) - dimension - 1
     return pl.BlockSpec(dims, lambda g, info: (0,) * dimension + (g,) + (0,) * rest)
+
+
+def plain_call(kernel, operands, outputs):
+    moved = sum(a.size * a.dtype.itemsize for a in tuple(operands) + tuple(outputs))
+    return pl.pallas_call(
+        kernel,
+        out_shape=tuple(outputs),
+        compiler_params=pltpu.CompilerParams(vmem_limit_bytes=VMEM_LIMIT),
+        cost_estimate=pl.CostEstimate(flops=0, bytes_accessed=moved, transcendentals=0),
+    )(*operands)
 
 
 def group_call(kernel, groups, info, operands, outputs, scratch=(), flops=0):
@@ -748,8 +813,6 @@
     kv_full = over_cores(kv_most)
     out_half = over_blocks(after(w_out.T, query_half))
     mlp_own = jnp.concatenate([w_gate, w_up, w_down.T], axis=1)
-    mlp_own = with_layout_constraint(after(mlp_own, query_most, kv_most), Layout((0, 1)))
-    mlp_weights = lax.all_gather(mlp_own, ("ti", "bo", "bi"), axis=0)
 
     own_gains = jnp.concatenate([norm_in, norm_mid, query_gain, key_gain])[None]
     own_gains = after(own_gains, kv_half)
@@ -823,6 +886,8 @@
         ),
         flops=2 * groups * rows * width * (all_heads + 2 * all_keys),
     )
+    mlp_own = with_layout_constraint(after(mlp_own, query_rows), Layout((0, 1)))
+    mlp_weights = lax.all_gather(mlp_own, ("ti", "bo", "bi"), axis=0)
     kv_blocks = over_blocks(kv_rows)
     key_value = over_cores(kv_blocks)
     out_full = over_cores(over_pair(out_half, (kv_blocks,)))
@@ -844,15 +909,22 @@
     def own_shard(array):
         starts = (first_sequence, outer * shard_rows, 0)
         part = lax.dynamic_slice(array, starts, (groups, shard_rows, width))
-        return part.reshape(-1, width).astype(F32)
+        return part.reshape(-1, width)
 
     x_shard = own_shard(hidden_in)
     grad_out_shard = own_shard(out_grad)
-    residual = x_shard + run(sum_rows(chain, *flat(out_parts)))[0]
-    normal_mid = normed(residual, gain_mid).astype(BF16).reshape(groups, shard_rows, width)
+    shard_dims = (groups * shard_rows, width)
+    half_shard = shape((groups * shard_rows, width // 2), BF16)
+    (sums,) = run(sum_rows(chain, *flat(out_parts)))
+    residual, *normal_mid = plain_call(
+        residual_kernel,
+        (x_shard, gain_mid[None]) + sums,
+        (shape(shard_dims, F32), half_shard, half_shard),
+    )
+    normal_mid = [half.reshape(groups, shard_rows, -1) for half in normal_mid]
     mid_parts = []
     for group in range(groups):
-        mid_parts += run(gather_parts(chain, normal_mid[group]))
+        mid_parts += run(gather_parts(chain, *(half[group] for half in normal_mid)))
 
     chunks = pair * hidden_units // HIDDEN_CHUNK
     steps = hidden_units // HIDDEN_CHUNK
@@ -866,8 +938,9 @@
     piece = pl.BlockSpec((rows, HIDDEN_CHUNK), lambda i, info: (0, i))
     hidden_shape = shape((rows, pair * hidden_units), BF16)
     one_dims = (counts // 2, 1, shard_rows, width // 2)
-    one_halves = (shape(one_dims, F32), shape(one_dims, BF16)) * 4
-    mid, active, grad_gate, grad_up, grad_parts, mlp_parts = [], [], [], [], [], []
+    two_dims = (counts // 2, 2, shard_rows, width // 2)
+    two_halves = (shape(two_dims, F32), shape(two_dims, BF16)) * 2
+    mid, active, grad_gate, grad_up, mlp_parts = [], [], [], [], []
     for group in range(groups):
         parts = [part.reshape(one_dims) for part in mid_parts[group]]
         sequence = pl.BlockSpec(
@@ -875,12 +948,12 @@
         )
         results = pl.pallas_call(
             functools.partial(feed_forward_kernel, counts),
-            out_shape=(hidden_shape,) * 3 + (shape((rows, width), BF16),) + one_halves,
+            out_shape=(hidden_shape,) * 3 + (shape((rows, width), BF16),) + two_halves,
             grid_spec=pltpu.PrefetchScalarGridSpec(
                 num_scalar_prefetch=1,
                 grid=(chunks,),
                 in_specs=[whole_spec(one_dims)] * 4 + [sequence] + [weight_spec(i) for i in range(3)],
-                out_specs=(piece,) * 3 + (whole_spec((rows, width)),) + (whole_spec(one_dims),) * 8,
+                out_specs=(piece,) * 3 + (whole_spec((rows, width)),) + (whole_spec(two_dims),) * 4,
                 scratch_shapes=[whole_rows] * 2,
             ),
             compiler_params=pltpu.CompilerParams(vmem_limit_bytes=VMEM_LIMIT),
@@ -894,21 +967,14 @@
         grad_gate.append(results[1])
         grad_up.append(results[2])
         mid.append(results[3])
-        grad_parts.append(results[4:8])
-        mlp_parts.append(results[8:])
-
-    grad_normal_mid, mlp_sums = [], []
+        mlp_parts.append(results[4:])
+
+    both_sums = []
     first_arrived = ()
     for group in range(groups - 1):
-        stages = [
-            sum_rows(chain, *flat(parts[group]), during=(active[-1],))
-            for parts in (grad_parts, mlp_parts)
-        ]
         mark = len(chain.done)
-        grad_sum, mlp_sum = run(*stages)
+        both_sums += run(sum_rows(chain, *flat(mlp_parts[group]), during=((active[-1],),)))
         first_arrived = chain.done[mark]
-        grad_normal_mid.append(grad_sum)
-        mlp_sums.append(mlp_sum)
     mlp_terms = weight_blocks(
         after(info, *first_arrived),
         (mid, [out_grad]),
@@ -919,12 +985,34 @@
         True,
         True,
     )
-    grad_normal_mid += run(sum_rows(chain, *flat(grad_parts[-1]), during=(mlp_terms,)))
-    _, pull_mid = jax.vjp(normed, residual, gain_mid)
-    grad_norm, gain_mid_term = pull_mid(jnp.concatenate(grad_normal_mid))
-    grad_residual = grad_out_shard + grad_norm
-    (branch_parts,) = run(gather_parts(chain, grad_residual.astype(BF16)))
-    branch_first = chain.done[-2][0]
+    both_sums += run(sum_rows(chain, *flat(mlp_parts[-1]), during=((mlp_terms,),)))
+    last_arrived = chain.done[-1]
+    layer_shard, grad_residual, *branch_halves, gain_mid_term = plain_call(
+        functools.partial(residual_back_kernel, groups),
+        (residual, grad_out_shard, gain_mid[None]) + tuple(a for sums in both_sums for a in sums),
+        (
+            shape(shard_dims, BF16),
+            shape(shard_dims, F32),
+            half_shard,
+            half_shard,
+            shape((1, width), F32),
+        ),
+    )
+
+    half_groups = groups // 2
+
+    def in_order(own, arrived):
+        return paired(own, arrived, inner == 0, 0)
+
+    layer_shard = layer_shard.reshape(groups, shard_rows, width)
+    late = layer_shard[half_groups:].reshape(-1, width)
+    late_arrived = swapped(late, "ti")
+    late = in_order(late, late_arrived).reshape(-1, width)
+    early_rows = half_groups * shard_rows
+    layer_rows = jnp.concatenate([layer_shard[:half_groups].reshape(-1, width), late])
+    (branch_parts,) = run(
+        gather_parts(chain, *branch_halves, ((), (late_arrived,)))
+    )
     branch_parts = [part.reshape(half_dims) for part in branch_parts]
     branch, grad_query, kv_kept, kv_sent = group_call(
         functools.partial(attend_back_kernel, (head_dim, pair_heads, group_size, counts)),
@@ -944,23 +1032,24 @@
         flops=2 * groups * rows * all_heads * (width + 10 * blocks * rows),
     )
 
-    def layer_rows(group, mlp_sum):
-        part = jnp.split(lax.optimization_barrier(residual), groups)[group]
-        return (part + mlp_sum).astype(BF16)
-
-    layer_first = [layer_rows(group, mlp_sums[group]) for group in range(groups - 1)]
-    stages = [sum_rows(chain, *flat(mlp_parts[-1]), before=((grad_query,),))]
-    stages += [gather_rows(chain, shard, ((grad_query,),)) for shard in layer_first]
-    mlp_sum, *layer_whole = run(*stages)
-    layer_last = layer_rows(groups - 1, mlp_sum)
-    layer_both = [gather_axis(whole, "ti") for whole in layer_whole]
-    done_before = tuple(a for done in chain.done[-len(stages) :] for a in done)
-
-    mine = kv_kept + swapped(kv_sent, "bi").astype(F32)
+    kv_arrived = swapped(kv_sent, "bi")
+    mine = kv_kept + kv_arrived.astype(F32)
     low = mine.astype(BF16)
+
+    layer_chain = Chain()
+    layer_stage = gather_rows(layer_chain, layer_rows, ((kv_arrived,),))
+    next(layer_stage)
+    layer_first = layer_chain.done[0]
     shares = mine[0]
     for step in range(1, block_outers):
-        shares += shifted(low[step], "bo", block_outers - step).astype(F32)
+        arrived = shifted(low[step], "bo", block_outers - step)
+        shares += after(arrived, *layer_first).astype(F32)
+    (layer_whole,) = run(layer_stage)
+    layer_second = layer_chain.done[1:]
+    layer_whole = layer_whole.reshape(counts, -1, width)
+    layer_early = layer_whole[:, :early_rows]
+    layer_arrived = swapped(layer_early, "ti")
+
     grad_query_low, grad_kv_low, gain_terms, *in_parts = group_call(
         functools.partial(finish_kernel, (head_dim, pair_heads, key_heads, counts)),
         groups,
@@ -988,14 +1077,15 @@
     )
 
     in_parts = flat(in_parts)
-    (grad_normal_in,) = run(
-        sum_rows(
-            chain, *in_parts, before=(done_before, tuple(layer_both)), during=(attn_terms,)
-        )
-    )
-    _, pull_first = jax.vjp(normed, x_shard, gain_in)
-    grad_norm, gain_in_term = pull_first(grad_normal_in)
-    hidden_shard = (grad_residual + grad_norm).astype(BF16).reshape(groups, shard_rows, width)
+    during = ((attn_terms,), (layer_arrived,))
+    (sums,) = run(sum_rows(chain, *in_parts, before=layer_second, during=during))
+    sum_arrived = chain.done[-1]
+    hidden_shard, gain_in_term = plain_call(
+        hidden_kernel,
+        (x_shard, gain_in[None], grad_residual) + sums,
+        (shape(shard_dims, BF16), shape((1, width), F32)),
+    )
+    hidden_shard = hidden_shard.reshape(groups, shard_rows, width)
 
     def weight_sum(terms):
         flat = terms.reshape((-1,) + terms.shape[-1:])
@@ -1003,44 +1093,58 @@
         share = with_layout_constraint(raw, Layout((0, 1)))
         return share.astype(F32).reshape(terms.shape[2:]), raw
 
-    share_mlp, mlp_raw = weight_sum(after(mlp_terms, branch_first))
-    share_attn, _ = weight_sum(after(attn_terms, mlp_raw))
-    vectors = jnp.concatenate([gain_in_term, gain_mid_term, gain_terms.sum(0).reshape(-1)])
-    vectors = sum_over(vectors[None], ("ti",))
-    hidden_pairs = [
-        gather_axis(hidden_shard[group], "ti").reshape(-1, width)
-        for group in range(groups // 2, groups)
-    ]
-    first = (tuple(hidden_pairs) + (vectors,),)
-    stages = [gather_rows(chain, layer_last)]
-    stages += [gather_rows(chain, hidden_shard[group], first) for group in range(groups // 2)]
-    layer_whole, *hidden_whole = run(*stages)
-    layer_both.append(gather_axis(layer_whole, "ti"))
-    hidden_both = [gather_axis(whole, "ti") for whole in hidden_whole]
-    for both in hidden_pairs:
-        (whole,) = run(gather_rows(chain, both))
-        whole = whole.reshape(counts, pair, shard_rows, width)
-        hidden_both.append(whole.transpose(1, 0, 2, 3).reshape(pair, rows, width))
-    vectors = sum_over(vectors, BLOCKS + ("to",))[0]
-
-    def vector_share(first, size):
-        return lax.dynamic_slice_in_dim(vectors, first + block * (size // blocks), size // blocks)
-
+    share_mlp, mlp_raw = weight_sum(after(mlp_terms, *last_arrived))
+    share_attn, _ = weight_sum(after(attn_terms, mlp_raw, *sum_arrived))
+    vectors = jnp.concatenate(
+        [gain_in_term[0], gain_mid_term[0], gain_terms.sum(0).reshape(-1)]
+    )
+    hidden_late = hidden_shard[half_groups:].reshape(-1, width)
+    hidden_arrived = swapped(hidden_late, "ti")
+    vectors = vectors[None]
+    vector_arrived = swapped(vectors, "ti")
+    hidden_early = hidden_shard[:half_groups].reshape(-1, width)
+    (hidden_early,) = run(gather_rows(chain, hidden_early, ((), (hidden_arrived,))))
+    hidden_early_arrived = swapped(hidden_early, "ti")
+    vectors = vectors + after(vector_arrived, *chain.done[-1])
+    hidden_late = in_order(hidden_late, hidden_arrived).reshape(-1, width)
+    during = ((), (hidden_early_arrived,))
+    ((hidden_late, vectors),) = run(
+        gather_rows(chain, hidden_late, during=during, vector=vectors)
+    )
+    vectors = sum_over(vectors, BLOCKS)[0]
     kv_start = query_width + 2 * key_width
-    return (
-        jnp.stack(layer_both, axis=1).reshape(batch, rows, width),
-        jnp.stack(hidden_both, axis=1).reshape(batch, rows, width),
-        vector_share(0, width),
+    weight_grads = (
         share_attn[:, :query_width],
         share_attn[:, query_width : query_width + key_width],
         share_attn[:, query_width + key_width : kv_start],
         share_attn[:, kv_start:].T,
+        share_mlp[0],
+        share_mlp[1],
+        share_mlp[2].T,
+    )
+    def assembled(early, arrived, late):
+        late = late.reshape(counts, pair, groups - half_groups, shard_rows, width)
+        late = late.transpose(1, 2, 0, 3, 4).reshape(pair, -1, rows, width)
+        early = in_order(early, arrived).reshape(pair, counts, half_groups, shard_rows, width)
+        early = early.transpose(0, 2, 1, 3, 4).reshape(pair, -1, rows, width)
+        return jnp.concatenate([early, late], axis=1).reshape(batch, rows, width)
+
+    layer_out = assembled(layer_early, layer_arrived, layer_whole[:, early_rows:])
+    hidden_early_arrived = after(hidden_early_arrived, layer_out, *weight_grads)
+    grad_hidden = assembled(hidden_early, hidden_early_arrived, hidden_late)
+
+    def vector_share(first, size):
+        return lax.dynamic_slice_in_dim(vectors, first + block * (size // blocks), size // blocks)
+
+    return (
+        layer_out,
+        grad_hidden,
+        vector_share(0, width),
+        *weight_grads[:4],
         vector_share(2 * width, head_dim),
         vector_share(2 * width + head_dim, head_dim),
         vector_share(width, width),
-        share_mlp[0],
-        share_mlp[1],
-        share_mlp[2].T,
+        *weight_grads[4:],
     )
 
 

time: 551 us -> 512 us (0.929)
  waiting for transfers between devices: 255 us -> 237 us
  other arithmetic: 52.1 us -> 36.5 us
  starting transfers between devices: 80.7 us -> 71.4 us
    ppermute x5, waiting for transfers between devices: 51.1 us -> 31.9 us  [shifted(): lax.ppermute(array, axis, [(i, (i + step) % count) for i in range(count)])]
    ppermute x71 -> x59, starting transfers between devices: 74.5 us -> 65.9 us  [swapped(): return lax.ppermute(array, axis, [(i, i ^ distance) for i in range(count)])]
    convert_element_type x4 -> x0, other arithmetic: 7.16 us -> none  [the longest x1 2.43 us: local(): (grad_residual + grad_norm).astype(BF16).reshape(groups, shard_rows, width)]
    concatenate x2 -> x4, other arithmetic: 0.1 us -> 6.51 us  [the longest x2 4.75 us: assembled(): return jnp.concatenate([early, late], axis=1).reshape(batch, rows, width)]
    select_n x30 -> x24, other arithmetic: 11.7 us -> 8.9 us  [paired(): jnp.where(first, jnp.stack([own, other], dimension), jnp.stack([other, ow...]
    unnamed x168 -> x123, local copies, waits for them, and re-layouts: 24.2 us -> 22.3 us
    ppermute x71 -> x59, waiting for transfers between devices: 204 us -> 205 us  [swapped(): return lax.ppermute(array, axis, [(i, i ^ distance) for i in range(count)])]
  transfers between devices with their start and end apart: 79 -> 67, of which waited for: 51 -> 41; matrix products, arithmetic and copies ran while one was open for 12% -> 11% of each run, Pallas kernels for 18% -> 19%
where the time goes in v4:
time: 512 us; the launch traced here: 505 us
  waiting for transfers between devices  237 us (46%)
  Pallas kernels  103 us (20%)
  starting transfers between devices  71.4 us (14%)
  local copies, waits for them, and re-layouts  41.2 us (8%)
  other arithmetic  36.5 us (7%)
  between operations  15.2 us (3%)
    ppermute x59, waiting for transfers between devices, swapped(): return lax.ppermute(array, axis, [(i, i ^ distance) for i in range(count)])  205 us
    ppermute x59, starting transfers between devices, swapped(): return lax.ppermute(array, axis, [(i, i ^ distance) for i in range(count)])  65.9 us
    pallas_call x4, Pallas kernels, group_call(): pl.pallas_call(kernel, out_shape=[a for a, _ in outputs], grid_spec=pltpu...  39.1 us
    pallas_call x2, Pallas kernels, local(): pl.pallas_call(functools.partial(feed_forward_kernel, counts), out_shape=...  36.2 us
    ppermute x5, waiting for transfers between devices, shifted(): lax.ppermute(array, axis, [(i, (i + step) % count) for i in range(count)])  31.9 us
    pallas_call x2, Pallas kernels, weight_blocks(): pl.pallas_call(functools.partial(weight_kernel, counts, placed), out_shap...  24 us
    unnamed x123, local copies, waits for them, and re-layouts  22.3 us
  transfers between devices with their start and end apart: 67, of which 41 were waited for; matrix products, arithmetic and copies ran while one was open for 11% of the time, Pallas kernels for 19%

profile of v4, /device:TPU:0, one launch (start us, length us, event | category | flops | bytes accessed | tf_op | source)
XLA Modules:
  0.0 504.6 jit_solution(5864932993613157717)
XLA Ops:
  29.5 8.7 %collective-permute-done.5 = bf16[512,512]{1,0:T(8,128)(2,1)S(1)} collective-permute-done((bf16[512,512]{1,0:T(8,128)(2,1)S(1)}, bf16[512,512]{1,0:T(8,128)(2,1)S(1)}, u32[]{:S(2)}, u32[]{:S(2)}) %collective-permute-start.5) | collective-permute-done | bytes 524320 | tf_op jit(solution)/shard_map/ppermute | solution.py:49
  44.8 6.8 %shard_map.228 = (bf16[2,256,2048]{2,1,0:T(8,128)(2,1)}, f32[2,256,512]{2,1,0:T(8,128)S(1)}, f32[2,256,256]{2,1,0:T(8,128)S(1)}, bf16[2,256,512]{2,1,0:T(8,128)(2,1)S(1)}, bf16[2,2,2,256,128]{4,3,2,1,0:T(8,128)(2,1)S(1)}) custom-call(s32[13]{0:T(128)S(1)} %stack.359.info, bf16[4,256,2048]{2,1,0:T(8,128)(2,1)} %x_ref.1, f32[1,2048]{1,0:T(1,128)S(1)} %bitcast.242, ...), custom_call_target="tpu_custom_call" | custom-call | flops 2147483648 | bytes 13378560 | tf_op jit(solution)/shard_map/pallas_call | solution.py:698
  57.0 17.1 %collective-permute-done.9 = bf16[2,2,2,256,128]{4,3,2,1,0:T(8,128)(2,1)S(1)} collective-permute-done((bf16[2,2,2,256,128]{4,3,2,1,0:T(8,128)(2,1)S(1)}, bf16[2,2,2,256,128]{4,3,2,1,0:T(8,128)(2,1)S(1)}, u32[]{:S(2)}, u32[]{:S(2)}) %collective-permute-start.9) | collective-permute-done | bytes 524320 | tf_op jit(solution)/shard_map/ppermute | solution.py:49
  79.5 8.2 %shard_map.229 = (f32[2,256,512]{2,1,0:T(8,128)S(1)}, f32[2,256,128]{2,1,0:T(8,128)S(1)}, bf16[2,256,512]{2,1,0:T(8,128)(2,1)S(1)}, f32[2,2,64,1024]{3,2,1,0:T(8...) custom-call(s32[13]{0:T(128)S(1)} %stack.359.info, ...), custom_call_target="tpu_custom_call" | custom-call | flops 3221225472 | bytes 9699328 | tf_op jit(solution)/shard_map/pallas_call | solution.py:698
  94.7 20.7 %collective-permute-done.13 = bf16[256,1024]{1,0:T(8,128)(2,1)} collective-permute-done((bf16[256,1024]{1,0:T(8,128)(2,1)S(1)}, bf16[256,1024]{1,0:T(8,128)(2,1)}, u32[]{:S(2)}, u32[]{:S(2)}) %collective-permute-start.13) | collective-permute-done | bytes 524320 | tf_op jit(solution)/shard_map/ppermute | solution.py:54
  123.7 7.3 %collective-permute-done.14.refs_1_ = bf16[128,1024]{1,0:T(8,128)(2,1)S(1)} collective-permute-done((bf16[128,1024]{1,0:T(8,128)(2,1)S(1)}, bf16[128,1024]{1,0:T(8,128)(2,1)S(1)}, u32[]{:S(2)}, u32[]{:S(2)}) %collective-permute-start.14) | collective-permute-done | bytes 262176 | tf_op jit(solution)/shard_map/ppermute | solution.py:54
  150.3 7.2 %collective-permute-done.22 = bf16[1,64,1024]{2,1,0:T(8,128)(2,1)S(1)} collective-permute-done((bf16[1,64,1024]{2,1,0:T(8,128)(2,1)S(1)}, bf16[1,64,1024]{2,1,0:T(8,128)(2,1)S(1)}, u32[]{:S(2)}, u32[]{:S(2)}) %collective-permute-start.22) | collective-permute-done | bytes 131104 | tf_op jit(solution)/shard_map/ppermute | solution.py:54
  161.4 18.0 %shard_map.231 = (bf16[256,1536]{1,0:T(8,128)(2,1)S(1)}, bf16[256,1536]{1,0:T(8,128)(2,1)S(1)}, bf16[256,1536]{1,0:T(8,128)(2,1)S(1)}, bf16[256,2048]{1,0:T(8,12...) custom-call(s32[13]{0:T(128)S(1)} %stack.359.info, ...), custom_call_target="tpu_custom_call" | custom-call | flops 9663676416 | bytes 18874368 | tf_op jit(solution)/shard_map/pallas_call | solution.py:949
  181.3 18.2 %shard_map.232 = (bf16[256,1536]{1,0:T(8,128)(2,1)S(1)}, bf16[256,1536]{1,0:T(8,128)(2,1)S(1)}, bf16[256,1536]{1,0:T(8,128)(2,1)S(1)}, bf16[256,2048]{1,0:T(8,12...) custom-call(s32[13]{0:T(128)S(1)} %stack.359.info, ...), custom_call_target="tpu_custom_call" | custom-call | flops 9663676416 | bytes 18874368 | tf_op jit(solution)/shard_map/pallas_call | solution.py:949
  209.3 15.9 %shard_map.233 = bf16[2,4,3,512,768]{4,3,2,1,0:T(8,128)(2,1)} custom-call(s32[13]{0:T(128)S(1)} %stack.359.info, bf16[256,2048]{1,0:T(8,128)(2,1)S(1)} %get-tuple-element.159.refs_0_, bf16[256,2048]{1,0:T(8,128)(2,1)} %copy-done.15, bf16[4,256,2048]{2,1,0:T(8,128)(2,1)} %refs_2_.1, bf16[256,1536]{1,0:T(8,128)(2,1)S(1)} %get-tuple-element.161.refs_3_, ...), custom_call_target="tpu_custom_call" | custom-call | flops 9663676416 | bytes 18874368 | tf_op jit(solution)/shard_map/pallas_call | solution.py:759
  225.2 12.8 %collective-permute-done.29 = bf16[256,1024]{1,0:T(8,128)(2,1)S(1)} collective-permute-done((bf16[256,1024]{1,0:T(8,128)(2,1)S(1)}, bf16[256,1024]{1,0:T(8,128)(2,1)S(1)}, u32[]{:S(2)}, u32[]{:S(2)}) %collective-permute-start.29) | collective-permute-done | bytes 524320 | tf_op jit(solution)/shard_map/ppermute | solution.py:54
  241.0 9.1 %collective-permute-done.31.refs_5_ = bf16[128,1024]{1,0:T(8,128)(2,1)S(1)} collective-permute-done((bf16[128,1024]{1,0:T(8,128)(2,1)S(1)}, bf16[128,1024]{1,0:T(8,128)(2,1)S(1)}, u32[]{:S(2)}, u32[]{:S(2)}) %collective-permute-start.31) | collective-permute-done | bytes 262176 | tf_op jit(solution)/shard_map/ppermute | solution.py:54
  258.0 9.2 %collective-permute-done.34 = bf16[1,128,1024]{2,1,0:T(8,128)(2,1)S(1)} collective-permute-done((bf16[1,128,1024]{2,1,0:T(8,128)(2,1)S(1)}, bf16[1,128,1024]{2,1,0:T(8,128)(2,1)S(1)}, u32[]{:S(2)}, u32[]{:S(2)}) %collective-permute-start.34) | collective-permute-done | bytes 262176 | tf_op jit(solution)/shard_map/ppermute | solution.py:54
  270.3 21.6 %collective-permute-done.36 = bf16[2,128,1024]{2,1,0:T(8,128)(2,1)S(1)} collective-permute-done((bf16[2,128,1024]{2,1,0:T(8,128)(2,1)S(1)}, bf16[2,128,1024]{2,1,0:T(8,128)(2,1)S(1)}, u32[]{:S(2)}, u32[]{:S(2)}) %collective-permute-start.36) | collective-permute-done | bytes 524320 | tf_op jit(solution)/shard_map/ppermute | solution.py:54
  293.4 13.2 %shard_map.235 = (bf16[2,256,2048]{2,1,0:T(8,128)(2,1)}, f32[2,256,512]{2,1,0:T(8,128)S(1)}, f32[2,2,2,2,256,128]{5,4,3,2,1,0:T(8,128)}, bf16[2,2,2,2,256,128]{5,4,3,2,1,0:T(8,128)(2,1)}) custom-call(s32[13]{0:T(128)S(1)} %stack.359.info, bf16[2,2,64,1024]{3,2,1,0:T(8,128)(2,1)S(1)} %pad_maximum_fusion.12.first_own, bf16[2,2,64,1024]{3,2,1,0:T(8,128)(2,1)S(1)} %bitcast.254, ...), custom_call_target="tpu_custom_call" | custom-call | flops 6442450944 | bytes 14417920 | tf_op jit(solution)/shard_map/pallas_call | solution.py:698
  314.9 13.8 %collective-permute-done.41 = bf16[1,192,1024]{2,1,0:T(8,128)(2,1)S(1)} collective-permute-done((bf16[1,192,1024]{2,1,0:T(8,128)(2,1)S(1)}, bf16[1,192,1024]{2,1,0:T(8,128)(2,1)S(1)}, u32[]{:S(2)}, u32[]{:S(2)}) %collective-permute-start.41) | collective-permute-done | bytes 393248 | tf_op jit(solution)/shard_map/ppermute | solution.py:54
  340.6 10.9 %shard_map.236 = (bf16[2,256,512]{2,1,0:T(8,128)(2,1)S(1)}, bf16[2,256,512]{2,1,0:T(8,128)(2,1)S(1)}, f32[2,2,128]{2,1,0:T(2,128)S(1)}, f32[2,2,64,1024]{3,2,1,0...) custom-call(s32[13]{0:T(128)S(1)} %stack.359.info, ...), custom_call_target="tpu_custom_call" | custom-call | flops 2147483648 | bytes 12323840 | tf_op jit(solution)/shard_map/pallas_call | solution.py:698
  351.6 8.1 %shard_map.237 = bf16[2,4,512,768]{3,2,1,0:T(8,128)(2,1)} custom-call(s32[13]{0:T(128)S(1)} %stack.359.info, bf16[2,256,2048]{2,1,0:T(8,128)(2,1)S(1)} %copy-done.3, bf16[2,256,2048]{2,1,0:T(8,128)(2,1)S(1)} %copy-done.4, bf16[2,256,512]{2,1,0:T(8,128)(2,1)S(1)} %get-tuple-element.196.refs_2_, bf16[2,256,512]{2,1,0:T(8,128)(2,1)S(1)} %get-tuple-element.197.refs_3_, ...), custom_call_target="tpu_custom_call" | custom-call | flops 3221225472 | bytes 6291456 | tf_op jit(solution)/shard_map/pallas_call | solution.py:759
  359.7 6.2 %collective-permute-done.42 = bf16[2,192,1024]{2,1,0:T(8,128)(2,1)} collective-permute-done((bf16[2,192,1024]{2,1,0:T(8,128)(2,1)}, bf16[2,192,1024]{2,1,0:T(8,128)(2,1)}, u32[]{:S(2)}, u32[]{:S(2)}) %collective-permute-start.42) | collective-permute-done | bytes 786464 | tf_op jit(solution)/shard_map/ppermute | solution.py:54
  372.1 18.5 %collective-permute-done.45 = bf16[256,1024]{1,0:T(8,128)(2,1)S(1)} collective-permute-done((bf16[256,1024]{1,0:T(8,128)(2,1)S(1)}, bf16[256,1024]{1,0:T(8,128)(2,1)S(1)}, u32[]{:S(2)}, u32[]{:S(2)}) %collective-permute-start.45) | collective-permute-done | bytes 524320 | tf_op jit(solution)/shard_map/ppermute | solution.py:54
  395.2 9.7 %collective-permute-done.47.refs_1_ = bf16[128,1024]{1,0:T(8,128)(2,1)S(1)} collective-permute-done((bf16[128,1024]{1,0:T(8,128)(2,1)S(1)}, bf16[128,1024]{1,0:T(8,128)(2,1)S(1)}, u32[]{:S(2)}, u32[]{:S(2)}) %collective-permute-start.47) | collective-permute-done | bytes 262176 | tf_op jit(solution)/shard_map/ppermute | solution.py:54
  424.6 7.5 %collective-permute-done.52 = bf16[2,64,1024]{2,1,0:T(8,128)(2,1)S(1)} collective-permute-done((bf16[2,64,1024]{2,1,0:T(8,128)(2,1)S(1)}, bf16[2,64,1024]{2,1,0:T(8,128)(2,1)S(1)}, u32[]{:S(2)}, u32[]{:S(2)}) %collective-permute-start.52) | collective-permute-done | bytes 262176 | tf_op jit(solution)/shard_map/ppermute | solution.py:54
  444.4 12.3 %collective-permute-done.58 = f32[1,4352]{1,0:T(1,128)S(1)} collective-permute-done((f32[1,4352]{1,0:T(1,128)S(1)}, f32[1,4352]{1,0:T(1,128)S(1)}, u32[]{:S(2)}, u32[]{:S(2)}) %collective-permute-start.58) | collective-permute-done | bytes 17440 | tf_op jit(solution)/shard_map/ppermute | solution.py:54
  462.5 10.7 %collective-permute-done.61 = f32[1,4352]{1,0:T(1,128)S(1)} collective-permute-done((f32[1,4352]{1,0:T(1,128)S(1)}, f32[1,4352]{1,0:T(1,128)S(1)}, u32[]{:S(2)}, u32[]{:S(2)}) %collective-permute-start.61) | collective-permute-done | bytes 17440 | tf_op jit(solution)/shard_map/ppermute | solution.py:54
  (363 shorter events, 197.8 us)
Async XLA Ops:
  7.2 154.3 %all-gather.3.cloned.1.call-start = ((), (), s32[]{:S(2)}) async-start(), calls=%async_computation.4 | async-start | bytes 21233664 | tf_op jit(solution)/shard_map/all_gather | solution.py:890
  55.0 351.7 %reduce-scatter.3.cloned.1.call-start = ((), (), s32[]{:S(2)}) async-start(), calls=%async_computation.2 | async-start | bytes 21233664 | tf_op jit(solution)/shard_map/reduce_scatter | solution.py:1092
  90.2 25.2 %collective-permute-start.13 = (bf16[256,1024]{1,0:T(8,128)(2,1)S(1)}, bf16[256,1024]{1,0:T(8,128)(2,1)}, u32[]{:S(2)}, u32[]{:S(2)}) collective-permute-start(bf16[256,1024]{1,0:T(8,128)(2,1)S(1)} %bitcast.247), channel_id=1, source_target_pairs={{0,2},{2,0},{4,6},{6,4},{1,3},{3,1},{5,7},{7,5},{8,10},{10,8},{12,... | collective-permute-start | bytes 1572872 | tf_op jit(solution)/shard_map/ppermute | solution.py:54
  91.9 26.1 %collective-permute-start.15 = (bf16[256,1024]{1,0:T(8,128)(2,1)S(1)}, bf16[256,1024]{1,0:T(8,128)(2,1)}, u32[]{:S(2)}, u32[]{:S(2)}) collective-permute-start(bf16[256,1024]{1,0:T(8,128)(2,1)S(1)} %bitcast.246), channel_id=1, source_target_pairs={{0,4},{2,6},{4,0},{6,2},{1,5},{3,7},{5,1},{7,3},{8,12},{10,14},{12... | collective-permute-start | bytes 1572872 | tf_op jit(solution)/shard_map/ppermute | solution.py:54
  158.3 23.0 %collective-permute-start.25 = (bf16[2,64,1024]{2,1,0:T(8,128)(2,1)S(1)}, bf16[2,64,1024]{2,1,0:T(8,128)(2,1)S(1)}, u32[]{:S(2)}, u32[]{:S(2)}) collective-permute-start(bf16[2,64,1024]{2,1,0:T(8,128)(2,1)S(1)} %get-tuple-element.145), channel_id=1, source_target_pairs={{0,2},{2,0},{4,6},{6,4},{1,3},{3,1},{5,7},{7,5},{8,10},{10,8},{12,... | collective-permute-start | bytes 786440 | tf_op jit(solution)/shard_map/ppermute | solution.py:54
  159.4 21.9 %collective-permute-start.26 = (bf16[2,64,1024]{2,1,0:T(8,128)(2,1)}, bf16[2,64,1024]{2,1,0:T(8,128)(2,1)S(1)}, u32[]{:S(2)}, u32[]{:S(2)}) collective-permute-start(bf16[2,64,1024]{2,1,0:T(8,128)(2,1)} %get-tuple-element.146), channel_id=1, source_target_pairs={{0,4},{2,6},{4,0},{6,2},{1,5},{3,7},{5,1},{7,3},{8,12},{10,14},{12... | collective-permute-start | bytes 786440 | tf_op jit(solution)/shard_map/ppermute | solution.py:54
  179.4 21.5 %collective-permute-start.23 = (bf16[256,1024]{1,0:T(8,128)(2,1)S(1)}, bf16[256,1024]{1,0:T(8,128)(2,1)S(1)}, u32[]{:S(2)}, u32[]{:S(2)}) collective-permute-start(bf16[256,1024]{1,0:T(8,128)(2,1)S(1)} %bitcast.253), channel_id=1, source_target_pairs={{0,2},{2,0},{4,6},{6,4},{1,3},{3,1},{5,7},{7,5},{8,10},{10,8},{12,... | collective-permute-start | bytes 1572872 | tf_op jit(solution)/shard_map/ppermute | solution.py:54
  180.3 22.6 %collective-permute-start.24 = (bf16[256,1024]{1,0:T(8,128)(2,1)S(1)}, bf16[256,1024]{1,0:T(8,128)(2,1)S(1)}, u32[]{:S(2)}, u32[]{:S(2)}) collective-permute-start(bf16[256,1024]{1,0:T(8,128)(2,1)S(1)} %bitcast.252), channel_id=1, source_target_pairs={{0,4},{2,6},{4,0},{6,2},{1,5},{3,7},{5,1},{7,3},{8,12},{10,14},{12... | collective-permute-start | bytes 1572872 | tf_op jit(solution)/shard_map/ppermute | solution.py:54
  204.3 34.1 %collective-permute-start.27 = (bf16[128,1024]{1,0:T(8,128)(2,1)S(1)}, bf16[128,1024]{1,0:T(8,128)(2,1)S(1)}, u32[]{:S(2)}, u32[]{:S(2)}) collective-permute-start(bf16[128,1024]{1,0:T(8,128)(2,1)S(1)} %fusion.5), channel_id=1, source_target_pairs={{0,4},{2,6},{4,0},{6,2},{1,5},{3,7},{5,1},{7,3},{8,12},{10,14},{12... | collective-permute-start | bytes 786440 | tf_op jit(solution)/shard_map/ppermute | solution.py:54
  204.7 33.7 %collective-permute-start.28 = (bf16[128,1024]{1,0:T(8,128)(2,1)S(1)}, bf16[128,1024]{1,0:T(8,128)(2,1)S(1)}, u32[]{:S(2)}, u32[]{:S(2)}) collective-permute-start(bf16[128,1024]{1,0:T(8,128)(2,1)S(1)} %fusion.6), channel_id=1, source_target_pairs={{0,2},{2,0},{4,6},{6,4},{1,3},{3,1},{5,7},{7,5},{8,10},{10,8},{12,... | collective-permute-start | bytes 786440 | tf_op jit(solution)/shard_map/ppermute | solution.py:54
  206.7 31.3 %collective-permute-start.29 = (bf16[256,1024]{1,0:T(8,128)(2,1)S(1)}, bf16[256,1024]{1,0:T(8,128)(2,1)S(1)}, u32[]{:S(2)}, u32[]{:S(2)}) collective-permute-start(bf16[256,1024]{1,0:T(8,128)(2,1)S(1)} %bitcast.251), channel_id=1, source_target_pairs={{0,2},{2,0},{4,6},{6,4},{1,3},{3,1},{5,7},{7,5},{8,10},{10,8},{12,... | collective-permute-start | bytes 1572872 | tf_op jit(solution)/shard_map/ppermute | solution.py:54
  206.7 31.3 %collective-permute-start.30 = (bf16[256,1024]{1,0:T(8,128)(2,1)S(1)}, bf16[256,1024]{1,0:T(8,128)(2,1)S(1)}, u32[]{:S(2)}, u32[]{:S(2)}) collective-permute-start(bf16[256,1024]{1,0:T(8,128)(2,1)S(1)} %bitcast.249), channel_id=1, source_target_pairs={{0,4},{2,6},{4,0},{6,2},{1,5},{3,7},{5,1},{7,3},{8,12},{10,14},{12... | collective-permute-start | bytes 1572872 | tf_op jit(solution)/shard_map/ppermute | solution.py:54
  250.3 237.8 %reduce-scatter.5.cloned.1.call-start = ((), (), s32[]{:S(2)}) async-start(), calls=%async_computation.3 | async-start | bytes 7077888 | tf_op jit(solution)/shard_map/reduce_scatter | solution.py:1092
  267.5 24.4 %collective-permute-start.36 = (bf16[2,128,1024]{2,1,0:T(8,128)(2,1)S(1)}, bf16[2,128,1024]{2,1,0:T(8,128)(2,1)S(1)}, u32[]{:S(2)}, u32[]{:S(2)}) collective-permute-start(bf16[2,128,1024]{2,1,0:T(8,128)(2,1)S(1)} %pad_maximum_fusion.13), channel_id=1, source_target_pairs={{0,2},{2,0},{4,6},{6,4},{1,3},{3,1},{5,7},{7,5},{8,10},{10,8},{12,... | collective-permute-start | bytes 1572872 | tf_op jit(solution)/shard_map/ppermute | solution.py:54
  267.6 25.8 %collective-permute-start.37 = (bf16[2,128,1024]{2,1,0:T(8,128)(2,1)S(1)}, bf16[2,128,1024]{2,1,0:T(8,128)(2,1)S(1)}, u32[]{:S(2)}, u32[]{:S(2)}) collective-permute-start(bf16[2,128,1024]{2,1,0:T(8,128)(2,1)S(1)} %pad_maximum_fusion.14), channel_id=1, source_target_pairs={{0,4},{2,6},{4,0},{6,2},{1,5},{3,7},{5,1},{7,3},{8,12},{10,14},{12... | collective-permute-start | bytes 1572872 | tf_op jit(solution)/shard_map/ppermute | solution.py:54
  309.7 20.7 %collective-permute-start.39 = (bf16[1,192,1024]{2,1,0:T(8,128)(2,1)S(1)}, bf16[1,192,1024]{2,1,0:T(8,128)(2,1)S(1)}, u32[]{:S(2)}, u32[]{:S(2)}) collective-permute-start(bf16[1,192,1024]{2,1,0:T(8,128)(2,1)S(1)} %get-tuple-element.181), channel_id=1, source_target_pairs={{0,4},{2,6},{4,0},{6,2},{1,5},{3,7},{5,1},{7,3},{8,12},{10,14},{12... | collective-permute-start | bytes 1179656 | tf_op jit(solution)/shard_map/ppermute | solution.py:54
  313.9 25.6 %collective-permute-start.44 = (bf16[2,2,2,256,128]{4,3,2,1,0:T(8,128)(2,1)S(1)}, bf16[2,2,2,256,128]{4,3,2,1,0:T(8,128)(2,1)S(1)}, u32[]{:S(2)}, u32[]{:S(2)}) collective-permute-start(bf16[2,2,2,256,128]{4,3,2,1,0:T(8,128)(2,1)S(1)} %fusion.1), channel_id=1, source_target_pairs={{0,16},{16,0},{1,17},{17,1},{2,18},{18,2},{3,19},{19,3},{4,20},{20... | collective-permute-start | bytes 1572872 | tf_op jit(solution)/shard_map/ppermute | solution.py:49
  329.7 36.2 %collective-permute-start.42 = (bf16[2,192,1024]{2,1,0:T(8,128)(2,1)}, bf16[2,192,1024]{2,1,0:T(8,128)(2,1)}, u32[]{:S(2)}, u32[]{:S(2)}) collective-permute-start(bf16[2,192,1024]{2,1,0:T(8,128)(2,1)} %maximum_select_fusion.9), channel_id=1, source_target_pairs={{0,4},{2,6},{4,0},{6,2},{1,5},{3,7},{5,1},{7,3},{8,12},{10,14},{12... | collective-permute-start | bytes 2359304 | tf_op jit(solution)/shard_map/ppermute | solution.py:54
  331.3 35.7 %collective-permute-start.40 = (bf16[2,192,1024]{2,1,0:T(8,128)(2,1)}, bf16[2,192,1024]{2,1,0:T(8,128)(2,1)S(1)}, u32[]{:S(2)}, u32[]{:S(2)}) collective-permute-start(bf16[2,192,1024]{2,1,0:T(8,128)(2,1)} %maximum_select_fusion.7), channel_id=1, source_target_pairs={{0,2},{2,0},{4,6},{6,4},{1,3},{3,1},{5,7},{7,5},{8,10},{10,8},{12,... | collective-permute-start | bytes 2359304 | tf_op jit(solution)/shard_map/ppermute | solution.py:54
  367.0 23.5 %collective-permute-start.45 = (bf16[256,1024]{1,0:T(8,128)(2,1)S(1)}, bf16[256,1024]{1,0:T(8,128)(2,1)S(1)}, u32[]{:S(2)}, u32[]{:S(2)}) collective-permute-start(bf16[256,1024]{1,0:T(8,128)(2,1)S(1)} %bitcast.250), channel_id=1, source_target_pairs={{0,2},{2,0},{4,6},{6,4},{1,3},{3,1},{5,7},{7,5},{8,10},{10,8},{12,... | collective-permute-start | bytes 1572872 | tf_op jit(solution)/shard_map/ppermute | solution.py:54
  367.0 24.9 %collective-permute-start.46 = (bf16[256,1024]{1,0:T(8,128)(2,1)S(1)}, bf16[256,1024]{1,0:T(8,128)(2,1)S(1)}, u32[]{:S(2)}, u32[]{:S(2)}) collective-permute-start(bf16[256,1024]{1,0:T(8,128)(2,1)S(1)} %bitcast.248), channel_id=1, source_target_pairs={{0,4},{2,6},{4,0},{6,2},{1,5},{3,7},{5,1},{7,3},{8,12},{10,14},{12... | collective-permute-start | bytes 1572872 | tf_op jit(solution)/shard_map/ppermute | solution.py:54
  372.0 34.7 %collective-permute-start.43 = (bf16[4,64,2048]{2,1,0:T(8,128)(2,1)S(1)}, bf16[4,64,2048]{2,1,0:T(8,128)(2,1)}, u32[]{:S(2)}, u32[]{:S(2)}) collective-permute-start(bf16[4,64,2048]{2,1,0:T(8,128)(2,1)S(1)} %pad_maximum_fusion.4), channel_id=1, source_target_pairs={{0,1},{1,0},{2,3},{3,2},{4,5},{5,4},{6,7},{7,6},{8,9},{9,8},{10,11... | collective-permute-start | bytes 3145736 | tf_op jit(solution)/shard_map/ppermute | solution.py:54
  437.1 19.6 %collective-permute-start.57 = (bf16[1,128,1024]{2,1,0:T(8,128)(2,1)S(1)}, bf16[1,128,1024]{2,1,0:T(8,128)(2,1)S(1)}, u32[]{:S(2)}, u32[]{:S(2)}) collective-permute-start(bf16[1,128,1024]{2,1,0:T(8,128)(2,1)S(1)} %get-tuple-element.219), channel_id=1, source_target_pairs={{0,2},{2,0},{4,6},{6,4},{1,3},{3,1},{5,7},{7,5},{8,10},{10,8},{12,... | collective-permute-start | bytes 786440 | tf_op jit(solution)/shard_map/ppermute | solution.py:54
  441.5 32.7 %collective-permute-start.54 = (bf16[256,2048]{1,0:T(8,128)(2,1)S(1)}, bf16[256,2048]{1,0:T(8,128)(2,1)S(1)}, u32[]{:S(2)}, u32[]{:S(2)}) collective-permute-start(bf16[256,2048]{1,0:T(8,128)(2,1)S(1)} %get-tuple-element.269), channel_id=1, source_target_pairs={{0,1},{1,0},{2,3},{3,2},{4,5},{5,4},{6,7},{7,6},{8,9},{9,8},{10,11... | collective-permute-start | bytes 3145736 | tf_op jit(solution)/shard_map/ppermute | solution.py:54
  (100 other events, 1008.8 us)
Sparse Core Ops, SparseCore 0:
  55.2 101.6 all-gather.2
  250.4 145.9 reduce-scatter.2
  406.9 74.9 reduce-scatter.4

commit v5 on v4

--- a/solution.py
+++ b/solution.py
@@ -1105,23 +1105,23 @@
     hidden_early = hidden_shard[:half_groups].reshape(-1, width)
     (hidden_early,) = run(gather_rows(chain, hidden_early, ((), (hidden_arrived,))))
     hidden_early_arrived = swapped(hidden_early, "ti")
-    vectors = vectors + after(vector_arrived, *chain.done[-1])
+    vectors = sum_over(vectors + after(vector_arrived, *chain.done[-2]), BLOCKS)
+    mlp_grads = (share_mlp[0], share_mlp[1], share_mlp[2].T)
     hidden_late = in_order(hidden_late, hidden_arrived).reshape(-1, width)
+    hidden_early_arrived = after(hidden_early_arrived, *mlp_grads)
     during = ((), (hidden_early_arrived,))
     ((hidden_late, vectors),) = run(
         gather_rows(chain, hidden_late, during=during, vector=vectors)
     )
-    vectors = sum_over(vectors, BLOCKS)[0]
+    vectors = vectors[0]
     kv_start = query_width + 2 * key_width
-    weight_grads = (
+    attn_grads = (
         share_attn[:, :query_width],
         share_attn[:, query_width : query_width + key_width],
         share_attn[:, query_width + key_width : kv_start],
         share_attn[:, kv_start:].T,
-        share_mlp[0],
-        share_mlp[1],
-        share_mlp[2].T,
-    )
+    )
+
     def assembled(early, arrived, late):
         late = late.reshape(counts, pair, groups - half_groups, shard_rows, width)
         late = late.transpose(1, 2, 0, 3, 4).reshape(pair, -1, rows, width)
@@ -1130,7 +1130,7 @@
         return jnp.concatenate([early, late], axis=1).reshape(batch, rows, width)
 
     layer_out = assembled(layer_early, layer_arrived, layer_whole[:, early_rows:])
-    hidden_early_arrived = after(hidden_early_arrived, layer_out, *weight_grads)
+    hidden_early_arrived = after(hidden_early_arrived, layer_out)
     grad_hidden = assembled(hidden_early, hidden_early_arrived, hidden_late)
 
     def vector_share(first, size):
@@ -1140,11 +1140,11 @@
         layer_out,
         grad_hidden,
         vector_share(0, width),
-        *weight_grads[:4],
+        *attn_grads,
         vector_share(2 * width, head_dim),
         vector_share(2 * width + head_dim, head_dim),
         vector_share(width, width),
-        *weight_grads[4:],
+        *mlp_grads,
     )
 
 

time: 512 us -> 507 us (level)
  local copies, waits for them, and re-layouts: 41.2 us -> 33.2 us
  other arithmetic: 36.5 us -> 44.3 us
    select_n x24, other arithmetic: 8.9 us -> 15.5 us  [paired(): jnp.where(first, jnp.stack([own, other], dimension), jnp.stack([other, ow...]
    unnamed x123 -> x119, local copies, waits for them, and re-layouts: 22.3 us -> 17.6 us
  transfers between devices with their start and end apart: 67 -> 67, of which waited for: 41 -> 41; matrix products, arithmetic and copies ran while one was open for 11% -> 12% of each run, Pallas kernels for 19% -> 19%
where the time goes in v5:
time: 507 us; the launch traced here: 501 us
  waiting for transfers between devices  234 us (46%)
  Pallas kernels  103 us (20%)
  starting transfers between devices  71.3 us (14%)
  other arithmetic  44.3 us (9%)
  local copies, waits for them, and re-layouts  33.2 us (7%)
  between operations  15.2 us (3%)
    ppermute x59, waiting for transfers between devices, swapped(): return lax.ppermute(array, axis, [(i, i ^ distance) for i in range(count)])  202 us
    ppermute x59, starting transfers between devices, swapped(): return lax.ppermute(array, axis, [(i, i ^ distance) for i in range(count)])  66 us
    pallas_call x4, Pallas kernels, group_call(): pl.pallas_call(kernel, out_shape=[a for a, _ in outputs], grid_spec=pltpu...  39.1 us
    pallas_call x2, Pallas kernels, local(): pl.pallas_call(functools.partial(feed_forward_kernel, counts), out_shape=...  36.3 us
    ppermute x5, waiting for transfers between devices, shifted(): lax.ppermute(array, axis, [(i, (i + step) % count) for i in range(count)])  32.2 us
    pallas_call x2, Pallas kernels, weight_blocks(): pl.pallas_call(functools.partial(weight_kernel, counts, placed), out_shap...  24 us
    unnamed x119, local copies, waits for them, and re-layouts  17.6 us
    select_n x24, other arithmetic, paired(): jnp.where(first, jnp.stack([own, other], dimension), jnp.stack([other, ow...  15.5 us
  transfers between devices with their start and end apart: 67, of which 41 were waited for; matrix products, arithmetic and copies ran while one was open for 12% of the time, Pallas kernels for 19%

profile of v5, /device:TPU:0, one launch (start us, length us, event | category | flops | bytes accessed | tf_op | source)
XLA Modules:
  0.0 500.9 jit_solution(3926901682825279439)
XLA Ops:
  29.5 8.7 %collective-permute-done.5 = bf16[512,512]{1,0:T(8,128)(2,1)S(1)} collective-permute-done((bf16[512,512]{1,0:T(8,128)(2,1)S(1)}, bf16[512,512]{1,0:T(8,128)(2,1)S(1)}, u32[]{:S(2)}, u32[]{:S(2)}) %collective-permute-start.5) | collective-permute-done | bytes 524320 | tf_op jit(solution)/shard_map/ppermute | solution.py:49
  44.8 6.8 %shard_map.228 = (bf16[2,256,2048]{2,1,0:T(8,128)(2,1)}, f32[2,256,512]{2,1,0:T(8,128)S(1)}, f32[2,256,256]{2,1,0:T(8,128)S(1)}, bf16[2,256,512]{2,1,0:T(8,128)(2,1)S(1)}, bf16[2,2,2,256,128]{4,3,2,1,0:T(8,128)(2,1)S(1)}) custom-call(s32[13]{0:T(128)S(1)} %stack.359.info, bf16[4,256,2048]{2,1,0:T(8,128)(2,1)} %x_ref.1, f32[1,2048]{1,0:T(1,128)S(1)} %bitcast.242, ...), custom_call_target="tpu_custom_call" | custom-call | flops 2147483648 | bytes 13378560 | tf_op jit(solution)/shard_map/pallas_call | solution.py:698
  57.0 17.1 %collective-permute-done.9 = bf16[2,2,2,256,128]{4,3,2,1,0:T(8,128)(2,1)S(1)} collective-permute-done((bf16[2,2,2,256,128]{4,3,2,1,0:T(8,128)(2,1)S(1)}, bf16[2,2,2,256,128]{4,3,2,1,0:T(8,128)(2,1)S(1)}, u32[]{:S(2)}, u32[]{:S(2)}) %collective-permute-start.9) | collective-permute-done | bytes 524320 | tf_op jit(solution)/shard_map/ppermute | solution.py:49
  79.5 8.2 %shard_map.229 = (f32[2,256,512]{2,1,0:T(8,128)S(1)}, f32[2,256,128]{2,1,0:T(8,128)S(1)}, bf16[2,256,512]{2,1,0:T(8,128)(2,1)S(1)}, f32[2,2,64,1024]{3,2,1,0:T(8...) custom-call(s32[13]{0:T(128)S(1)} %stack.359.info, ...), custom_call_target="tpu_custom_call" | custom-call | flops 3221225472 | bytes 9699328 | tf_op jit(solution)/shard_map/pallas_call | solution.py:698
  94.7 20.8 %collective-permute-done.13 = bf16[256,1024]{1,0:T(8,128)(2,1)} collective-permute-done((bf16[256,1024]{1,0:T(8,128)(2,1)S(1)}, bf16[256,1024]{1,0:T(8,128)(2,1)}, u32[]{:S(2)}, u32[]{:S(2)}) %collective-permute-start.13) | collective-permute-done | bytes 524320 | tf_op jit(solution)/shard_map/ppermute | solution.py:54
  123.6 7.3 %collective-permute-done.14.refs_1_ = bf16[128,1024]{1,0:T(8,128)(2,1)S(1)} collective-permute-done((bf16[128,1024]{1,0:T(8,128)(2,1)S(1)}, bf16[128,1024]{1,0:T(8,128)(2,1)S(1)}, u32[]{:S(2)}, u32[]{:S(2)}) %collective-permute-start.14) | collective-permute-done | bytes 262176 | tf_op jit(solution)/shard_map/ppermute | solution.py:54
  150.2 7.2 %collective-permute-done.22 = bf16[1,64,1024]{2,1,0:T(8,128)(2,1)S(1)} collective-permute-done((bf16[1,64,1024]{2,1,0:T(8,128)(2,1)S(1)}, bf16[1,64,1024]{2,1,0:T(8,128)(2,1)S(1)}, u32[]{:S(2)}, u32[]{:S(2)}) %collective-permute-start.22) | collective-permute-done | bytes 131104 | tf_op jit(solution)/shard_map/ppermute | solution.py:54
  161.7 18.0 %shard_map.231 = (bf16[256,1536]{1,0:T(8,128)(2,1)S(1)}, bf16[256,1536]{1,0:T(8,128)(2,1)S(1)}, bf16[256,1536]{1,0:T(8,128)(2,1)S(1)}, bf16[256,2048]{1,0:T(8,12...) custom-call(s32[13]{0:T(128)S(1)} %stack.359.info, ...), custom_call_target="tpu_custom_call" | custom-call | flops 9663676416 | bytes 18874368 | tf_op jit(solution)/shard_map/pallas_call | solution.py:949
  181.5 18.3 %shard_map.232 = (bf16[256,1536]{1,0:T(8,128)(2,1)S(1)}, bf16[256,1536]{1,0:T(8,128)(2,1)S(1)}, bf16[256,1536]{1,0:T(8,128)(2,1)S(1)}, bf16[256,2048]{1,0:T(8,12...) custom-call(s32[13]{0:T(128)S(1)} %stack.359.info, ...), custom_call_target="tpu_custom_call" | custom-call | flops 9663676416 | bytes 18874368 | tf_op jit(solution)/shard_map/pallas_call | solution.py:949
  209.5 15.9 %shard_map.233 = bf16[2,4,3,512,768]{4,3,2,1,0:T(8,128)(2,1)} custom-call(s32[13]{0:T(128)S(1)} %stack.359.info, bf16[256,2048]{1,0:T(8,128)(2,1)S(1)} %get-tuple-element.160.refs_0_, bf16[256,2048]{1,0:T(8,128)(2,1)} %copy-done.15, bf16[4,256,2048]{2,1,0:T(8,128)(2,1)} %refs_2_.1, bf16[256,1536]{1,0:T(8,128)(2,1)S(1)} %get-tuple-element.162.refs_3_, ...), custom_call_target="tpu_custom_call" | custom-call | flops 9663676416 | bytes 18874368 | tf_op jit(solution)/shard_map/pallas_call | solution.py:759
  225.4 12.8 %collective-permute-done.29 = bf16[256,1024]{1,0:T(8,128)(2,1)S(1)} collective-permute-done((bf16[256,1024]{1,0:T(8,128)(2,1)S(1)}, bf16[256,1024]{1,0:T(8,128)(2,1)S(1)}, u32[]{:S(2)}, u32[]{:S(2)}) %collective-permute-start.29) | collective-permute-done | bytes 524320 | tf_op jit(solution)/shard_map/ppermute | solution.py:54
  241.2 9.1 %collective-permute-done.31.refs_5_ = bf16[128,1024]{1,0:T(8,128)(2,1)S(1)} collective-permute-done((bf16[128,1024]{1,0:T(8,128)(2,1)S(1)}, bf16[128,1024]{1,0:T(8,128)(2,1)S(1)}, u32[]{:S(2)}, u32[]{:S(2)}) %collective-permute-start.31) | collective-permute-done | bytes 262176 | tf_op jit(solution)/shard_map/ppermute | solution.py:54
  258.1 9.1 %collective-permute-done.34 = bf16[1,128,1024]{2,1,0:T(8,128)(2,1)S(1)} collective-permute-done((bf16[1,128,1024]{2,1,0:T(8,128)(2,1)S(1)}, bf16[1,128,1024]{2,1,0:T(8,128)(2,1)S(1)}, u32[]{:S(2)}, u32[]{:S(2)}) %collective-permute-start.34) | collective-permute-done | bytes 262176 | tf_op jit(solution)/shard_map/ppermute | solution.py:54
  270.5 21.5 %collective-permute-done.36 = bf16[2,128,1024]{2,1,0:T(8,128)(2,1)S(1)} collective-permute-done((bf16[2,128,1024]{2,1,0:T(8,128)(2,1)S(1)}, bf16[2,128,1024]{2,1,0:T(8,128)(2,1)S(1)}, u32[]{:S(2)}, u32[]{:S(2)}) %collective-permute-start.36) | collective-permute-done | bytes 524320 | tf_op jit(solution)/shard_map/ppermute | solution.py:54
  293.3 13.2 %shard_map.235 = (bf16[2,256,2048]{2,1,0:T(8,128)(2,1)}, f32[2,256,512]{2,1,0:T(8,128)S(1)}, f32[2,2,2,2,256,128]{5,4,3,2,1,0:T(8,128)}, bf16[2,2,2,2,256,128]{5,4,3,2,1,0:T(8,128)(2,1)}) custom-call(s32[13]{0:T(128)S(1)} %stack.359.info, bf16[2,2,64,1024]{3,2,1,0:T(8,128)(2,1)S(1)} %pad_maximum_fusion.12.first_own, bf16[2,2,64,1024]{3,2,1,0:T(8,128)(2,1)S(1)} %bitcast.254, ...), custom_call_target="tpu_custom_call" | custom-call | flops 6442450944 | bytes 14417920 | tf_op jit(solution)/shard_map/pallas_call | solution.py:698
  315.0 14.0 %collective-permute-done.41 = bf16[1,192,1024]{2,1,0:T(8,128)(2,1)S(1)} collective-permute-done((bf16[1,192,1024]{2,1,0:T(8,128)(2,1)S(1)}, bf16[1,192,1024]{2,1,0:T(8,128)(2,1)S(1)}, u32[]{:S(2)}, u32[]{:S(2)}) %collective-permute-start.41) | collective-permute-done | bytes 393248 | tf_op jit(solution)/shard_map/ppermute | solution.py:54
  333.2 6.5 %collective-permute-done.44 = bf16[2,2,2,256,128]{4,3,2,1,0:T(8,128)(2,1)S(1)} collective-permute-done((bf16[2,2,2,256,128]{4,3,2,1,0:T(8,128)(2,1)S(1)}, bf16[2,2,2,256,128]{4,3,2,1,0:T(8,128)(2,1)S(1)}, u32[]{:S(2)}, u32[]{:S(2)}) %collective-permute-start.44) | collective-permute-done | bytes 524320 | tf_op jit(solution)/shard_map/ppermute | solution.py:49
  340.8 10.9 %shard_map.236 = (bf16[2,256,512]{2,1,0:T(8,128)(2,1)S(1)}, bf16[2,256,512]{2,1,0:T(8,128)(2,1)S(1)}, f32[2,2,128]{2,1,0:T(2,128)S(1)}, f32[2,2,64,1024]{3,2,1,0...) custom-call(s32[13]{0:T(128)S(1)} %stack.359.info, ...), custom_call_target="tpu_custom_call" | custom-call | flops 2147483648 | bytes 12323840 | tf_op jit(solution)/shard_map/pallas_call | solution.py:698
  351.8 8.1 %shard_map.237 = bf16[2,4,512,768]{3,2,1,0:T(8,128)(2,1)} custom-call(s32[13]{0:T(128)S(1)} %stack.359.info, bf16[2,256,2048]{2,1,0:T(8,128)(2,1)S(1)} %copy-done.3, bf16[2,256,2048]{2,1,0:T(8,128)(2,1)S(1)} %copy-done.4, bf16[2,256,512]{2,1,0:T(8,128)(2,1)S(1)} %get-tuple-element.197.refs_2_, bf16[2,256,512]{2,1,0:T(8,128)(2,1)S(1)} %get-tuple-element.198.refs_3_, ...), custom_call_target="tpu_custom_call" | custom-call | flops 3221225472 | bytes 6291456 | tf_op jit(solution)/shard_map/pallas_call | solution.py:759
  372.3 18.5 %collective-permute-done.45 = bf16[256,1024]{1,0:T(8,128)(2,1)S(1)} collective-permute-done((bf16[256,1024]{1,0:T(8,128)(2,1)S(1)}, bf16[256,1024]{1,0:T(8,128)(2,1)S(1)}, u32[]{:S(2)}, u32[]{:S(2)}) %collective-permute-start.45) | collective-permute-done | bytes 524320 | tf_op jit(solution)/shard_map/ppermute | solution.py:54
  395.5 9.7 %collective-permute-done.47.refs_1_ = bf16[128,1024]{1,0:T(8,128)(2,1)S(1)} collective-permute-done((bf16[128,1024]{1,0:T(8,128)(2,1)S(1)}, bf16[128,1024]{1,0:T(8,128)(2,1)S(1)}, u32[]{:S(2)}, u32[]{:S(2)}) %collective-permute-start.47) | collective-permute-done | bytes 262176 | tf_op jit(solution)/shard_map/ppermute | solution.py:54
  433.3 8.4 %collective-permute-done.60 = f32[1,4352]{1,0:T(1,128)S(1)} collective-permute-done((f32[1,4352]{1,0:T(1,128)S(1)}, f32[1,4352]{1,0:T(1,128)S(1)}, u32[]{:S(2)}, u32[]{:S(2)}) %collective-permute-start.60) | collective-permute-done | bytes 17440 | tf_op jit(solution)/shard_map/ppermute | solution.py:54
  441.6 7.6 %collective-permute-done.53 = bf16[2,64,1024]{2,1,0:T(8,128)(2,1)S(1)} collective-permute-done((bf16[2,64,1024]{2,1,0:T(8,128)(2,1)S(1)}, bf16[2,64,1024]{2,1,0:T(8,128)(2,1)S(1)}, u32[]{:S(2)}, u32[]{:S(2)}) %collective-permute-start.53) | collective-permute-done | bytes 262176 | tf_op jit(solution)/shard_map/ppermute | solution.py:54
  463.5 17.1 %collective-permute-done.54 = bf16[256,2048]{1,0:T(8,128)(2,1)} collective-permute-done((bf16[256,2048]{1,0:T(8,128)(2,1)}, bf16[256,2048]{1,0:T(8,128)(2,1)}, u32[]{:S(2)}, u32[]{:S(2)}) %collective-permute-start.54) | collective-permute-done | bytes 1048608 | tf_op jit(solution)/shard_map/ppermute | solution.py:54
  (359 shorter events, 191.1 us)
Async XLA Ops:
  7.2 154.5 %all-gather.3.cloned.1.call-start = ((), (), s32[]{:S(2)}) async-start(), calls=%async_computation.4 | async-start | bytes 21233664 | tf_op jit(solution)/shard_map/all_gather | solution.py:890
  55.1 351.6 %reduce-scatter.3.cloned.1.call-start = ((), (), s32[]{:S(2)}) async-start(), calls=%async_computation.2 | async-start | bytes 21233664 | tf_op jit(solution)/shard_map/reduce_scatter | solution.py:1092
  90.2 25.2 %collective-permute-start.13 = (bf16[256,1024]{1,0:T(8,128)(2,1)S(1)}, bf16[256,1024]{1,0:T(8,128)(2,1)}, u32[]{:S(2)}, u32[]{:S(2)}) collective-permute-start(bf16[256,1024]{1,0:T(8,128)(2,1)S(1)} %bitcast.247), channel_id=1, source_target_pairs={{0,2},{2,0},{4,6},{6,4},{1,3},{3,1},{5,7},{7,5},{8,10},{10,8},{12,... | collective-permute-start | bytes 1572872 | tf_op jit(solution)/shard_map/ppermute | solution.py:54
  91.9 26.1 %collective-permute-start.15 = (bf16[256,1024]{1,0:T(8,128)(2,1)S(1)}, bf16[256,1024]{1,0:T(8,128)(2,1)}, u32[]{:S(2)}, u32[]{:S(2)}) collective-permute-start(bf16[256,1024]{1,0:T(8,128)(2,1)S(1)} %bitcast.246), channel_id=1, source_target_pairs={{0,4},{2,6},{4,0},{6,2},{1,5},{3,7},{5,1},{7,3},{8,12},{10,14},{12... | collective-permute-start | bytes 1572872 | tf_op jit(solution)/shard_map/ppermute | solution.py:54
  158.5 23.0 %collective-permute-start.25 = (bf16[2,64,1024]{2,1,0:T(8,128)(2,1)S(1)}, bf16[2,64,1024]{2,1,0:T(8,128)(2,1)S(1)}, u32[]{:S(2)}, u32[]{:S(2)}) collective-permute-start(bf16[2,64,1024]{2,1,0:T(8,128)(2,1)S(1)} %get-tuple-element.146), channel_id=1, source_target_pairs={{0,2},{2,0},{4,6},{6,4},{1,3},{3,1},{5,7},{7,5},{8,10},{10,8},{12,... | collective-permute-start | bytes 786440 | tf_op jit(solution)/shard_map/ppermute | solution.py:54
  180.4 22.7 %collective-permute-start.24 = (bf16[256,1024]{1,0:T(8,128)(2,1)S(1)}, bf16[256,1024]{1,0:T(8,128)(2,1)S(1)}, u32[]{:S(2)}, u32[]{:S(2)}) collective-permute-start(bf16[256,1024]{1,0:T(8,128)(2,1)S(1)} %bitcast.252), channel_id=1, source_target_pairs={{0,4},{2,6},{4,0},{6,2},{1,5},{3,7},{5,1},{7,3},{8,12},{10,14},{12... | collective-permute-start | bytes 1572872 | tf_op jit(solution)/shard_map/ppermute | solution.py:54
  204.4 34.1 %collective-permute-start.27 = (bf16[128,1024]{1,0:T(8,128)(2,1)S(1)}, bf16[128,1024]{1,0:T(8,128)(2,1)S(1)}, u32[]{:S(2)}, u32[]{:S(2)}) collective-permute-start(bf16[128,1024]{1,0:T(8,128)(2,1)S(1)} %fusion.5), channel_id=1, source_target_pairs={{0,4},{2,6},{4,0},{6,2},{1,5},{3,7},{5,1},{7,3},{8,12},{10,14},{12... | collective-permute-start | bytes 786440 | tf_op jit(solution)/shard_map/ppermute | solution.py:54
  204.8 33.7 %collective-permute-start.28 = (bf16[128,1024]{1,0:T(8,128)(2,1)S(1)}, bf16[128,1024]{1,0:T(8,128)(2,1)S(1)}, u32[]{:S(2)}, u32[]{:S(2)}) collective-permute-start(bf16[128,1024]{1,0:T(8,128)(2,1)S(1)} %fusion.6), channel_id=1, source_target_pairs={{0,2},{2,0},{4,6},{6,4},{1,3},{3,1},{5,7},{7,5},{8,10},{10,8},{12,... | collective-permute-start | bytes 786440 | tf_op jit(solution)/shard_map/ppermute | solution.py:54
  206.7 31.4 %collective-permute-start.29 = (bf16[256,1024]{1,0:T(8,128)(2,1)S(1)}, bf16[256,1024]{1,0:T(8,128)(2,1)S(1)}, u32[]{:S(2)}, u32[]{:S(2)}) collective-permute-start(bf16[256,1024]{1,0:T(8,128)(2,1)S(1)} %bitcast.251), channel_id=1, source_target_pairs={{0,2},{2,0},{4,6},{6,4},{1,3},{3,1},{5,7},{7,5},{8,10},{10,8},{12,... | collective-permute-start | bytes 1572872 | tf_op jit(solution)/shard_map/ppermute | solution.py:54
  206.9 31.3 %collective-permute-start.30 = (bf16[256,1024]{1,0:T(8,128)(2,1)S(1)}, bf16[256,1024]{1,0:T(8,128)(2,1)S(1)}, u32[]{:S(2)}, u32[]{:S(2)}) collective-permute-start(bf16[256,1024]{1,0:T(8,128)(2,1)S(1)} %bitcast.249), channel_id=1, source_target_pairs={{0,4},{2,6},{4,0},{6,2},{1,5},{3,7},{5,1},{7,3},{8,12},{10,14},{12... | collective-permute-start | bytes 1572872 | tf_op jit(solution)/shard_map/ppermute | solution.py:54
  250.4 239.7 %reduce-scatter.5.cloned.1.call-start = ((), (), s32[]{:S(2)}) async-start(), calls=%async_computation.3 | async-start | bytes 7077888 | tf_op jit(solution)/shard_map/reduce_scatter | solution.py:1092
  267.5 24.5 %collective-permute-start.36 = (bf16[2,128,1024]{2,1,0:T(8,128)(2,1)S(1)}, bf16[2,128,1024]{2,1,0:T(8,128)(2,1)S(1)}, u32[]{:S(2)}, u32[]{:S(2)}) collective-permute-start(bf16[2,128,1024]{2,1,0:T(8,128)(2,1)S(1)} %pad_maximum_fusion.13), channel_id=1, source_target_pairs={{0,2},{2,0},{4,6},{6,4},{1,3},{3,1},{5,7},{7,5},{8,10},{10,8},{12,... | collective-permute-start | bytes 1572872 | tf_op jit(solution)/shard_map/ppermute | solution.py:54
  267.7 25.5 %collective-permute-start.37 = (bf16[2,128,1024]{2,1,0:T(8,128)(2,1)S(1)}, bf16[2,128,1024]{2,1,0:T(8,128)(2,1)S(1)}, u32[]{:S(2)}, u32[]{:S(2)}) collective-permute-start(bf16[2,128,1024]{2,1,0:T(8,128)(2,1)S(1)} %pad_maximum_fusion.14), channel_id=1, source_target_pairs={{0,4},{2,6},{4,0},{6,2},{1,5},{3,7},{5,1},{7,3},{8,12},{10,14},{12... | collective-permute-start | bytes 1572872 | tf_op jit(solution)/shard_map/ppermute | solution.py:54
  314.1 25.6 %collective-permute-start.44 = (bf16[2,2,2,256,128]{4,3,2,1,0:T(8,128)(2,1)S(1)}, bf16[2,2,2,256,128]{4,3,2,1,0:T(8,128)(2,1)S(1)}, u32[]{:S(2)}, u32[]{:S(2)}) collective-permute-start(bf16[2,2,2,256,128]{4,3,2,1,0:T(8,128)(2,1)S(1)} %fusion.1), channel_id=1, source_target_pairs={{0,16},{16,0},{1,17},{17,1},{2,18},{18,2},{3,19},{19,3},{4,20},{20... | collective-permute-start | bytes 1572872 | tf_op jit(solution)/shard_map/ppermute | solution.py:49
  330.0 36.1 %collective-permute-start.42 = (bf16[2,192,1024]{2,1,0:T(8,128)(2,1)}, bf16[2,192,1024]{2,1,0:T(8,128)(2,1)}, u32[]{:S(2)}, u32[]{:S(2)}) collective-permute-start(bf16[2,192,1024]{2,1,0:T(8,128)(2,1)} %maximum_select_fusion.9), channel_id=1, source_target_pairs={{0,4},{2,6},{4,0},{6,2},{1,5},{3,7},{5,1},{7,3},{8,12},{10,14},{12... | collective-permute-start | bytes 2359304 | tf_op jit(solution)/shard_map/ppermute | solution.py:54
  331.2 35.8 %collective-permute-start.40 = (bf16[2,192,1024]{2,1,0:T(8,128)(2,1)}, bf16[2,192,1024]{2,1,0:T(8,128)(2,1)S(1)}, u32[]{:S(2)}, u32[]{:S(2)}) collective-permute-start(bf16[2,192,1024]{2,1,0:T(8,128)(2,1)} %maximum_select_fusion.7), channel_id=1, source_target_pairs={{0,2},{2,0},{4,6},{6,4},{1,3},{3,1},{5,7},{7,5},{8,10},{10,8},{12,... | collective-permute-start | bytes 2359304 | tf_op jit(solution)/shard_map/ppermute | solution.py:54
  367.1 23.7 %collective-permute-start.45 = (bf16[256,1024]{1,0:T(8,128)(2,1)S(1)}, bf16[256,1024]{1,0:T(8,128)(2,1)S(1)}, u32[]{:S(2)}, u32[]{:S(2)}) collective-permute-start(bf16[256,1024]{1,0:T(8,128)(2,1)S(1)} %bitcast.250), channel_id=1, source_target_pairs={{0,2},{2,0},{4,6},{6,4},{1,3},{3,1},{5,7},{7,5},{8,10},{10,8},{12,... | collective-permute-start | bytes 1572872 | tf_op jit(solution)/shard_map/ppermute | solution.py:54
  367.1 25.0 %collective-permute-start.46 = (bf16[256,1024]{1,0:T(8,128)(2,1)S(1)}, bf16[256,1024]{1,0:T(8,128)(2,1)S(1)}, u32[]{:S(2)}, u32[]{:S(2)}) collective-permute-start(bf16[256,1024]{1,0:T(8,128)(2,1)S(1)} %bitcast.248), channel_id=1, source_target_pairs={{0,4},{2,6},{4,0},{6,2},{1,5},{3,7},{5,1},{7,3},{8,12},{10,14},{12... | collective-permute-start | bytes 1572872 | tf_op jit(solution)/shard_map/ppermute | solution.py:54
  372.2 34.4 %collective-permute-start.43 = (bf16[4,64,2048]{2,1,0:T(8,128)(2,1)S(1)}, bf16[4,64,2048]{2,1,0:T(8,128)(2,1)}, u32[]{:S(2)}, u32[]{:S(2)}) collective-permute-start(bf16[4,64,2048]{2,1,0:T(8,128)(2,1)S(1)} %pad_maximum_fusion.4), channel_id=1, source_target_pairs={{0,1},{1,0},{2,3},{3,2},{4,5},{5,4},{6,7},{7,6},{8,9},{9,8},{10,11... | collective-permute-start | bytes 3145736 | tf_op jit(solution)/shard_map/ppermute | solution.py:54
  430.6 23.2 %collective-permute-start.58 = (bf16[1,128,1024]{2,1,0:T(8,128)(2,1)S(1)}, bf16[1,128,1024]{2,1,0:T(8,128)(2,1)S(1)}, u32[]{:S(2)}, u32[]{:S(2)}) collective-permute-start(bf16[1,128,1024]{2,1,0:T(8,128)(2,1)S(1)} %get-tuple-element.219), channel_id=1, source_target_pairs={{0,4},{2,6},{4,0},{6,2},{1,5},{3,7},{5,1},{7,3},{8,12},{10,14},{12... | collective-permute-start | bytes 786440 | tf_op jit(solution)/shard_map/ppermute | solution.py:54
  450.7 29.8 %collective-permute-start.54 = (bf16[256,2048]{1,0:T(8,128)(2,1)}, bf16[256,2048]{1,0:T(8,128)(2,1)}, u32[]{:S(2)}, u32[]{:S(2)}) collective-permute-start(bf16[256,2048]{1,0:T(8,128)(2,1)} %get-tuple-element.271), channel_id=1, source_target_pairs={{0,1},{1,0},{2,3},{3,2},{4,5},{5,4},{6,7},{7,6},{8,9},{9,8},{10,11... | collective-permute-start | bytes 3145736 | tf_op jit(solution)/shard_map/ppermute | solution.py:54
  455.6 26.0 %collective-permute-start.61 = (bf16[2,128,1024]{2,1,0:T(8,128)(2,1)}, bf16[2,128,1024]{2,1,0:T(8,128)(2,1)}, u32[]{:S(2)}, u32[]{:S(2)}) collective-permute-start(bf16[2,128,1024]{2,1,0:T(8,128)(2,1)} %maximum_select_fusion.15), channel_id=1, source_target_pairs={{0,2},{2,0},{4,6},{6,4},{1,3},{3,1},{5,7},{7,5},{8,10},{10,8},{12,... | collective-permute-start | bytes 1572872 | tf_op jit(solution)/shard_map/ppermute | solution.py:54
  455.6 26.0 %collective-permute-start.62 = (bf16[2,128,1024]{2,1,0:T(8,128)(2,1)}, bf16[2,128,1024]{2,1,0:T(8,128)(2,1)}, u32[]{:S(2)}, u32[]{:S(2)}) collective-permute-start(bf16[2,128,1024]{2,1,0:T(8,128)(2,1)} %maximum_select_fusion.16), channel_id=1, source_target_pairs={{0,4},{2,6},{4,0},{6,2},{1,5},{3,7},{5,1},{7,3},{8,12},{10,14},{12... | collective-permute-start | bytes 1572872 | tf_op jit(solution)/shard_map/ppermute | solution.py:54
  458.2 23.4 %collective-permute-start.63 = (f32[1,4352]{1,0:T(1,128)S(1)}, f32[1,4352]{1,0:T(1,128)S(1)}, u32[]{:S(2)}, u32[]{:S(2)}) collective-permute-start(f32[1,4352]{1,0:T(1,128)S(1)} %add.166), channel_id=1, source_target_pairs={{0,4},{2,6},{4,0},{6,2},{1,5},{3,7},{5,1},{7,3},{8,12},{10,14},{12... | collective-permute-start | bytes 52232 | tf_op jit(solution)/shard_map/ppermute | solution.py:54
  (98 other events, 1074.5 us)
Sparse Core Ops, SparseCore 0:
  55.2 101.6 all-gather.2
  250.5 145.3 reduce-scatter.2
  406.8 71.4 reduce-scatter.4
